TPU v7x, 32 devices: a whole 2x2x4 slice. The times are simulated.
32 devices in a mesh: replica: 8 (over y, x, core), group: 4 (over z).
Axes of the slice: x: 2, y: 2, z: 4, core: 2. Of those that a mesh axis runs over, the one named last changes fastest.
Arguments:
- tokens: bfloat16 [8192, 768], P(('replica', 'group')), may hold values from -6 to 6
- segment: int32 [8192], P(('replica', 'group')), may hold values from 0 to 255, as said below
- g_attn: bfloat16 [768], P('group'), may hold values from 0.5 to 1.5
- w_qkv: bfloat16 [768, 2304], P('group'), may hold values from -0.21875 to 0.21875
- w_out: bfloat16 [768, 768], P('group'), may hold values from -0.625 to 0.625
- g_mlp: bfloat16 [768], P('group'), may hold values from 0.5 to 1.5
- w_in: bfloat16 [768, 2304], P('group'), may hold values from -0.21875 to 0.21875
- w_down: bfloat16 [1152, 768], P('group'), may hold values from -0.1875 to 0.1875
- grad_out: bfloat16 [8192, 768], P(('replica', 'group')), may hold values from -6 to 6
Outputs:
- output: bfloat16 [8192, 768], P(('replica', 'group'))
- tokens_grad: bfloat16 [8192, 768], P(('replica', 'group'))
- g_attn_grad: float32 [768], P('group')
- w_qkv_grad: float32 [768, 2304], P('group')
- w_out_grad: float32 [768, 768], P('group')
- g_mlp_grad: float32 [768], P('group')
- w_in_grad: float32 [768, 2304], P('group')
- w_down_grad: float32 [1152, 768], P('group')
Inputs may be any that keep to these rules, and one draw needn't show every extreme that they name: Within each block of 256 rows segment starts at 0 and rises by 0 or 1 from row to row; in every draw some block is one sequence of 256 tokens and some other block is 256 sequences of one token.
All inputs are finite; a program needn't handle non-finite values.
Results may differ from a plain program's by a relative error of at most 0.015.
Values may be sent and summed in bfloat16 or wider, within the bound.
No kernel may reach another device: no remote copies, remote signals or barrier semaphores. Data moves between devices by JAX's collectives and lax.ppermute only.
A program may use at most 128 MiB of HBM per device.

v0:
```python
import jax
import jax.numpy as jnp
from jax import lax
from jax.sharding import PartitionSpec as P

HEADS = 12
HEAD_DIM = 64
FF = 1152


norm_eps = 1e-05
rope_base = 160000.0


def token_positions(segment):
    length = segment.shape[0]
    index = jnp.arange(length, dtype=jnp.int32)
    before = jnp.concatenate([jnp.full((1,), -1, jnp.int32), segment[:-1]])
    first = lax.cummax(jnp.where(segment != before, index, 0), axis=0)
    return index - first


def rotary_tables(position):
    half_dim = HEAD_DIM // 2
    inverse = rope_base ** (-(jnp.arange(half_dim, dtype=jnp.float32) * 2.0 / HEAD_DIM))
    angles = position.astype(jnp.float32)[:, None] * inverse[None, :]
    angles = jnp.concatenate([angles, angles], axis=1)
    return (jnp.cos(angles)[:, None, :], jnp.sin(angles)[:, None, :])


def rotate_half(values):
    half_dim = values.shape[-1] // 2
    return jnp.concatenate([-values[..., half_dim:], values[..., :half_dim]], axis=-1)


def normalize(values):
    centred = values - jnp.mean(values, axis=1, keepdims=True)
    inverse = lax.rsqrt(jnp.mean(centred * centred, axis=1, keepdims=True) + norm_eps)
    return (centred * inverse, inverse)


def norm_back(upstream, normed, inverse, gain):
    gain_grad = jnp.sum(upstream * normed, axis=0)
    scaled = upstream * gain
    inner = (
        scaled
        - jnp.mean(scaled, axis=1, keepdims=True)
        - normed * jnp.mean(scaled * normed, axis=1, keepdims=True)
    )
    return (inverse * inner, gain_grad)


def geglu(first_half, second_half):
    return jax.nn.gelu(first_half, approximate=False) * second_half


def on_device(tokens, segment, g_attn, w_qkv, w_out, g_mlp, w_in, w_down, grad_out):
    length = tokens.shape[0]
    width = tokens.shape[1]
    head_scale = HEAD_DIM ** (-0.5)
    resid = tokens.astype(jnp.float32)
    position = token_positions(segment)
    cosine, sine = rotary_tables(position)
    same_seq = (segment[:, None] == segment[None, :])[None]
    attn_full = (
        lax.all_gather(g_attn, "group", axis=0, tiled=True),
        lax.all_gather(w_qkv, "group", axis=0, tiled=True),
        lax.all_gather(w_out, "group", axis=0, tiled=True),
    )
    gain_one = attn_full[0].astype(jnp.float32)
    normed_one, inverse_one = normalize(resid)
    attn_in = (normed_one * gain_one).astype(jnp.bfloat16)
    qkv = jnp.dot(attn_in, attn_full[1], preferred_element_type=jnp.float32)
    query_raw = qkv[:, :width].reshape(length, HEADS, HEAD_DIM)
    key_raw = qkv[:, width : 2 * width].reshape(length, HEADS, HEAD_DIM)
    values = qkv[:, 2 * width :].reshape(length, HEADS, HEAD_DIM).astype(jnp.bfloat16)
    queries = (query_raw * cosine + rotate_half(query_raw) * sine).astype(jnp.bfloat16)
    keys = (key_raw * cosine + rotate_half(key_raw) * sine).astype(jnp.bfloat16)
    scores = (
        jnp.einsum("qhd,khd->hqk", queries, keys, preferred_element_type=jnp.float32) * head_scale
    )
    scores = jnp.where(same_seq, scores, -1e30)
    row_top = jnp.max(scores, axis=2, keepdims=True)
    weights_exp = jnp.exp(scores - row_top)
    row_total = jnp.sum(weights_exp, axis=2, keepdims=True)
    log_total = row_top + jnp.log(row_total)
    probs = (weights_exp / row_total).astype(jnp.bfloat16)
    mixed = jnp.einsum("hqk,khd->qhd", probs, values, preferred_element_type=jnp.float32)
    mixed = mixed.reshape(length, width).astype(jnp.bfloat16)
    middle = resid + jnp.dot(mixed, attn_full[2], preferred_element_type=jnp.float32)
    mlp_full = (
        lax.all_gather(g_mlp, "group", axis=0, tiled=True),
        lax.all_gather(w_in, "group", axis=0, tiled=True),
        lax.all_gather(w_down, "group", axis=0, tiled=True),
    )
    gain_two = mlp_full[0].astype(jnp.float32)
    normed_two, inverse_two = normalize(middle)
    mlp_in = (normed_two * gain_two).astype(jnp.bfloat16)
    gate_up = jnp.dot(mlp_in, mlp_full[1], preferred_element_type=jnp.float32)
    inputs_half = gate_up[:, :FF]
    gates_half = gate_up[:, FF:]
    hidden = geglu(inputs_half, gates_half).astype(jnp.bfloat16)
    output = (middle + jnp.dot(hidden, mlp_full[2], preferred_element_type=jnp.float32)).astype(
        jnp.bfloat16
    )
    mlp_full = (
        lax.all_gather(g_mlp, "group", axis=0, tiled=True),
        lax.all_gather(w_in, "group", axis=0, tiled=True),
        lax.all_gather(w_down, "group", axis=0, tiled=True),
    )
    upstream = grad_out.astype(jnp.float32)
    down_grad = jnp.einsum("nf,nd->fd", hidden, grad_out, preferred_element_type=jnp.float32)
    hidden_grad = jnp.einsum("nd,fd->nf", grad_out, mlp_full[2], preferred_element_type=jnp.float32)
    _, geglu_pull = jax.vjp(geglu, inputs_half, gates_half)
    input_grad, gate_grad = geglu_pull(hidden_grad)
    gate_up_grad = jnp.concatenate([input_grad, gate_grad], axis=1).astype(jnp.bfloat16)
    in_grad = jnp.einsum("nd,nf->df", mlp_in, gate_up_grad, preferred_element_type=jnp.float32)
    mlp_in_grad = jnp.einsum(
        "nf,df->nd", gate_up_grad, mlp_full[1], preferred_element_type=jnp.float32
    )
    middle_part, gain_two_grad = norm_back(mlp_in_grad, normed_two, inverse_two, gain_two)
    middle_grad = upstream + middle_part
    mlp_owned = (
        lax.psum_scatter(
            gain_two_grad.astype(jnp.bfloat16), "group", scatter_dimension=0, tiled=True
        ).astype(jnp.float32),
        lax.psum_scatter(
            in_grad.astype(jnp.bfloat16), "group", scatter_dimension=0, tiled=True
        ).astype(jnp.float32),
        lax.psum_scatter(
            down_grad.astype(jnp.bfloat16), "group", scatter_dimension=0, tiled=True
        ).astype(jnp.float32),
    )
    attn_full = (
        lax.all_gather(g_attn, "group", axis=0, tiled=True),
        lax.all_gather(w_qkv, "group", axis=0, tiled=True),
        lax.all_gather(w_out, "group", axis=0, tiled=True),
    )
    branch_grad = middle_grad.astype(jnp.bfloat16)
    out_grad = jnp.einsum("nd,ne->de", mixed, branch_grad, preferred_element_type=jnp.float32)
    mixed_grad = jnp.einsum(
        "ne,de->nd", branch_grad, attn_full[2], preferred_element_type=jnp.float32
    )
    mixed_grad = mixed_grad.astype(jnp.bfloat16).reshape(length, HEADS, HEAD_DIM)
    again_scores = (
        jnp.einsum("qhd,khd->hqk", queries, keys, preferred_element_type=jnp.float32) * head_scale
    )
    again_probs = jnp.where(same_seq, jnp.exp(again_scores - log_total), 0.0)
    value_grad = jnp.einsum(
        "hqk,qhd->khd",
        again_probs.astype(jnp.bfloat16),
        mixed_grad,
        preferred_element_type=jnp.float32,
    )
    prob_grad = jnp.einsum("qhd,khd->hqk", mixed_grad, values, preferred_element_type=jnp.float32)
    row_delta = jnp.sum(again_probs * prob_grad, axis=2, keepdims=True)
    score_grad = (again_probs * (prob_grad - row_delta)).astype(jnp.bfloat16)
    query_grad = (
        jnp.einsum("hqk,khd->qhd", score_grad, keys, preferred_element_type=jnp.float32)
        * head_scale
    )
    key_grad = (
        jnp.einsum("hqk,qhd->khd", score_grad, queries, preferred_element_type=jnp.float32)
        * head_scale
    )
    query_grad = query_grad * cosine - rotate_half(query_grad * sine)
    key_grad = key_grad * cosine - rotate_half(key_grad * sine)
    qkv_grad = jnp.concatenate(
        [
            query_grad.reshape(length, width),
            key_grad.reshape(length, width),
            value_grad.reshape(length, width),
        ],
        axis=1,
    ).astype(jnp.bfloat16)
    qkv_weight_grad = jnp.einsum("nd,nf->df", attn_in, qkv_grad, preferred_element_type=jnp.float32)
    attn_in_grad = jnp.einsum(
        "nf,df->nd", qkv_grad, attn_full[1], preferred_element_type=jnp.float32
    )
    resid_part, gain_one_grad = norm_back(attn_in_grad, normed_one, inverse_one, gain_one)
    tokens_grad = (middle_grad + resid_part).astype(jnp.bfloat16)
    attn_owned = (
        lax.psum_scatter(
            gain_one_grad.astype(jnp.bfloat16), "group", scatter_dimension=0, tiled=True
        ).astype(jnp.float32),
        lax.psum_scatter(
            qkv_weight_grad.astype(jnp.bfloat16), "group", scatter_dimension=0, tiled=True
        ).astype(jnp.float32),
        lax.psum_scatter(
            out_grad.astype(jnp.bfloat16), "group", scatter_dimension=0, tiled=True
        ).astype(jnp.float32),
    )
    summed = lax.psum(
        (attn_owned[0], attn_owned[1], attn_owned[2], mlp_owned[0], mlp_owned[1], mlp_owned[2]),
        "replica",
    )
    attn_owned = summed[:3]
    mlp_owned = summed[3:]
    return (
        output,
        tokens_grad,
        attn_owned[0],
        attn_owned[1],
        attn_owned[2],
        mlp_owned[0],
        mlp_owned[1],
        mlp_owned[2],
    )


def solution(mesh):
    in_specs = (
        P(("replica", "group"), None),
        P(("replica", "group")),
        P("group"),
        P("group", None),
        P("group", None),
        P("group"),
        P("group", None),
        P("group", None),
        P(("replica", "group"), None),
    )
    out_specs = (
        P(("replica", "group"), None),
        P(("replica", "group"), None),
        P("group"),
        P("group", None),
        P("group", None),
        P("group"),
        P("group", None),
        P("group", None),
    )
    return jax.shard_map(
        on_device, mesh=mesh, in_specs=in_specs, out_specs=out_specs, check_vma=False
    )
```

profile of v0, /device:TPU:9, one launch (start us, length us, event | category | flops | bytes accessed | tf_op | source)
XLA Modules:
  0.0 550.9 jit_solution(3476636655678913771)
XLA Ops:
  7.2 0.7 all-gather.5.cloned.1.call-update
  8.0 0.7 all-gather.7.cloned.1.call-update
  8.7 0.7 all-gather.9.cloned.1.call-update
  9.5 0.5 all-gather.11.cloned.1.call-update
  10.1 0.7 broadcast_compare_fusion
  12.0 0.6 fusion.63
  13.8 7.3 %all-reduce.6 = (bf16[768]{0:T(1024)(128)(2,1)S(1)}, bf16[768]{0:T(1024)(128)(2,1)S(1)}) all-reduce(bf16[768]{0:T(1024)(128)(2,1)S(1)} %dynamic-update-slice, bf16[768]{0:T(1024)(128)(2,1)S(1)} %dynamic-update-slice.1), channel_id=1, replica_groups=mesh['replica'=8,'group'=4] {'group'}, use_global_device_ids=true, to_apply=%add | all-reduce | flops 1536 | bytes 6144
  21.1 0.8 broadcast_multiply_fusion.3
  21.9 56.7 %all-gather.5.cloned.1.call-done = bf16[768,2304]{1,0:T(8,128)(2,1)} async-done(((bf16[192,2304]{1,0:T(8,128)(2,1)}), bf16[768,2304]{1,0:T(8,128)(2,1)}) %all-gather.5.cloned.1.call-update) | async-done | bytes 3538960 | tf_op jit(solution)/shard_map/all_gather | solution.py:67
  78.6 3.1 fusion.58
  82.2 0.9 copy.39
  84.4 0.7 select_reduce_fusion
  85.2 0.7 fusion
  85.8 0.6 copy-done.29
  86.4 1.7 fusion.13
  88.1 22.7 %all-gather.7.cloned.1.call-done = bf16[768,768]{1,0:T(8,128)(2,1)} async-done(((bf16[192,768]{1,0:T(8,128)(2,1)}), bf16[768,768]{1,0:T(8,128)(2,1)}) %all-gather.7.cloned.1.call-update) | async-done | bytes 1179664 | tf_op jit(solution)/shard_map/all_gather | solution.py:68
  110.8 2.0 fusion.64
  112.8 0.9 copy-done
  113.9 65.8 %all-gather.9.cloned.1.call-done = bf16[768,2304]{1,0:T(8,128)(2,1)} async-done(((bf16[192,2304]{1,0:T(8,128)(2,1)}), bf16[768,2304]{1,0:T(8,128)(2,1)}) %all-gather.9.cloned.1.call-update) | async-done | bytes 3538960 | tf_op jit(solution)/shard_map/all_gather | solution.py:93
  179.8 4.9 fusion.60
  184.6 36.6 %all-gather.11.cloned.1.call-done = bf16[1152,768]{1,0:T(8,128)(2,1)} async-done(((bf16[288,768]{1,0:T(8,128)(2,1)}), bf16[1152,768]{1,0:T(8,128)(2,1)}) %all-gather.11.cloned.1.call-update) | async-done | bytes 1769488 | tf_op jit(solution)/shard_map/all_gather | solution.py:94
  221.3 5.5 add_convert_fusion
  226.8 1.1 multiply_convert_fusion.1
  228.4 1.3 copy-done.8
  229.7 1.8 multiply_reduce_fusion.1
  231.8 0.9 copy-done.3
  232.7 1.5 convolution_convert_fusion.3
  234.3 3.1 convolution_convert_fusion.2
  237.6 4.5 convolution_convert_fusion
  242.2 2.8 convolution_convert_fusion.4
  245.0 1.9 copy.43
  246.9 0.7 log_add_fusion
  247.6 2.2 multiply_reduce_fusion
  249.9 0.9 multiply_convert_fusion
  250.9 0.6 convolution_bitcast_fusion
  252.5 0.8 copy-done.25
  253.7 0.6 copy-done.19
  254.3 0.7 fusion.10
  255.2 0.6 copy-done.41
  255.8 3.2 convolution_convert_fusion.1
  259.9 4.5 fusion.33
  264.5 8.6 %all-reduce.5 = (bf16[768]{0:T(1024)(128)(2,1)S(1)}, bf16[768]{0:T(1024)(128)(2,1)S(1)}) all-reduce(bf16[768]{0:T(1024)(128)(2,1)S(1)} %get-tuple-element.10, bf16[768]{0:T(1024)(128)(2,1)S(1)} %copy-done.38), channel_id=2, replica_groups=mesh['replica'=8,'group'=4] {'group'}, use_global_device_ids=true, to_apply=%region_14.15.clone | all-reduce | flops 1536 | bytes 6144
  273.2 2.3 fusion.32
  275.5 1.4 fusion.9
  277.0 24.8 %reduce-scatter.11.cloned.1.call-done = bf16[288,768]{1,0:T(8,128)(2,1)} async-done(((bf16[1152,768]{1,0:T(8,128)(2,1)}), bf16[288,768]{1,0:T(8,128)(2,1)}) %reduce-scatter.11.cloned.1.call-update) | async-done | bytes 442384 | tf_op jit(solution)/shard_map/reduce_scatter | solution.py:130
  301.8 69.7 %reduce-scatter.9.cloned.1.call-done = bf16[192,2304]{1,0:T(8,128)(2,1)} async-done(((bf16[768,2304]{1,0:T(8,128)(2,1)}), bf16[192,2304]{1,0:T(8,128)(2,1)}) %reduce-scatter.9.cloned.1.call-update) | async-done | bytes 884752 | tf_op jit(solution)/shard_map/reduce_scatter | solution.py:127
  371.5 69.1 %reduce-scatter.5.cloned.1.call-done = bf16[192,2304]{1,0:T(8,128)(2,1)} async-done(((bf16[768,2304]{1,0:T(8,128)(2,1)}), bf16[192,2304]{1,0:T(8,128)(2,1)}) %reduce-scatter.5.cloned.1.call-update) | async-done | bytes 884752 | tf_op jit(solution)/shard_map/reduce_scatter | solution.py:186
  440.6 103.5 %all-reduce.8 = (f32[192]{0:T(256)}, f32[192,2304]{1,0:T(8,128)}, f32[192,768]{1,0:T(8,128)}, f32[192]{0:T(256)}, f32[192,2304]{1,0:T(8,128)}, /*index=5*/f32[288,768]{1,0:T(8,128)}) all-reduce(f32[192]{0:T(256)S(1)} %dynamic-slice_convert_fusion.1, ...), channel_id=1, replica_groups=mesh['replica'=8,'group'=4] {'replica'}, use_global_device_ids=true, to_apply=%region_15.16 | all-reduce | flops 1253760 | bytes 7523328 | tf_op jit(solution)/shard_map/psum | solution.py:193
  (128 shorter events, 7.2 us)
Async XLA Ops:
  7.2 2.9 copy-start.34
  7.2 4.4 copy-start.5
  7.2 71.4 %all-gather.5.cloned.1.call-start = ((), (), s32[]{:S(2)}) async-start(), calls=%async_computation.4 | async-start | bytes 4423680 | tf_op jit(solution)/shard_map/all_gather | solution.py:67
  7.9 102.9 %all-gather.7.cloned.1.call-start = ((), (), s32[]{:S(2)}) async-start(), calls=%async_computation.5 | async-start | bytes 1474560 | tf_op jit(solution)/shard_map/all_gather | solution.py:68
  8.7 3.3 copy-start.37
  8.7 4.6 copy-start.39
  8.7 4.8 copy-start.40
  8.7 171.1 %all-gather.9.cloned.1.call-start = ((), (), s32[]{:S(2)}) async-start(), calls=%async_computation.6 | async-start | bytes 4423680 | tf_op jit(solution)/shard_map/all_gather | solution.py:93
  9.4 211.8 %all-gather.11.cloned.1.call-start = ((), (), s32[]{:S(2)}) async-start(), calls=%async_computation.7 | async-start | bytes 2211840 | tf_op jit(solution)/shard_map/all_gather | solution.py:94
  10.0 267.0 %reduce-scatter.7.cloned.1.call-start = ((), (), s32[]{:S(2)}) async-start(), calls=%async_computation.9 | async-start | bytes 1474560 | tf_op jit(solution)/shard_map/reduce_scatter | solution.py:189
  11.7 70.1 %copy-start.32 = (f32[256]{0:T(256)}, f32[256]{0:T(256)S(1)}, u32[]{:S(2)}) copy-start(f32[256]{0:T(256)S(1)} %broadcast_multiply_fusion.10) | copy-start | bytes 3076
  12.0 69.8 %copy-start.35 = (f32[256]{0:T(256)}, f32[256]{0:T(256)S(1)}, u32[]{:S(2)}) copy-start(f32[256]{0:T(256)S(1)} %add_rsqrt_fusion.1) | copy-start | bytes 3076
  21.0 60.7 %copy-start.30 = (f32[768]{0:T(1024)}, f32[768]{0:T(1024)S(1)}, u32[]{:S(2)}) copy-start(f32[768]{0:T(1024)S(1)} %convert_element_type.107) | copy-start | bytes 9220
  83.6 0.8 copy-start.15
  84.0 1.2 copy-start.9
  84.0 1.2 copy-start.11
  85.2 1.3 copy-start.18
  112.8 0.9 copy-start
  221.3 5.5 copy-start.6
  226.8 1.1 copy-start.21
  226.8 1.6 copy-start.1
  226.8 2.9 copy-start.8
  227.9 3.6 copy-start.13
  229.7 1.8 copy-start.20
  231.5 1.2 copy-start.17
  231.8 0.9 copy-start.3
  234.2 67.5 %reduce-scatter.11.cloned.1.call-start = ((), (), s32[]{:S(2)}) async-start(), calls=%async_computation.11 | async-start | bytes 2211840 | tf_op jit(solution)/shard_map/reduce_scatter | solution.py:130
  237.4 134.1 %reduce-scatter.9.cloned.1.call-start = ((), (), s32[]{:S(2)}) async-start(), calls=%async_computation.10 | async-start | bytes 4423680 | tf_op jit(solution)/shard_map/reduce_scatter | solution.py:127
  242.1 4.8 copy-start.28
  242.2 198.4 %reduce-scatter.5.cloned.1.call-start = ((), (), s32[]{:S(2)}) async-start(), calls=%async_computation.8 | async-start | bytes 4423680 | tf_op jit(solution)/shard_map/reduce_scatter | solution.py:186
  247.6 2.2 copy-start.16
  249.9 1.0 copy-start.12
  250.9 1.0 copy-start.10
  250.9 1.0 copy-start.26
  252.4 0.8 copy-start.25
  253.3 1.0 copy-start.19
  254.3 0.8 copy-start.22
  254.3 0.9 copy-start.24
  254.3 1.5 copy-start.31
  254.3 1.5 copy-start.33
  254.3 1.5 copy-start.36
  255.0 0.8 copy-start.41
  258.9 1.0 copy-start.23
  259.9 4.5 copy-start.38
  259.9 13.3 %copy-start.4 = (f32[256,768]{1,0:T(8,128)S(1)}, f32[256,768]{1,0:T(8,128)}, u32[]{:S(2)}) copy-start(f32[256,768]{1,0:T(8,128)} %copy-done.3) | copy-start | bytes 2359300
  259.9 15.6 %copy-start.14 = (bf16[1152,768]{1,0:T(8,128)(2,1)S(1)}, bf16[1152,768]{1,0:T(8,128)(2,1)}, u32[]{:S(2)}) copy-start(bf16[1152,768]{1,0:T(8,128)(2,1)} %all-gather.11.cloned.1.call-done) | copy-start | bytes 5308420
  273.2 2.3 copy-start.2
  273.2 2.3 copy-start.7
  (2 other events, 1.3 us)
Sparse Core Ops, SparseCore 0:
  9.6 68.9 all-gather.4
  80.1 30.6 all-gather.6
  112.4 67.3 all-gather.8
  181.2 40.0 all-gather.10
  234.3 27.4 reduce-scatter.6
  264.5 37.1 reduce-scatter.10
  304.2 67.2 reduce-scatter.8
  373.9 66.6 reduce-scatter.4
where the time goes:
time: 554 us; the launch traced here: 551 us
  waiting for transfers between devices  348 us (63%)
  blocking collectives  119 us (21%)
  matrix products  44.6 us (8%)
  between operations  16 us (3%)
  local copies, waits for them, and re-layouts  12.5 us (2%)
  other arithmetic  9.93 us (2%)
    psum x1, blocking collectives, on_device(): lax.psum((attn_owned[0], attn_owned[1], attn_owned[2], mlp_owned[0], mlp_...  103 us
    reduce_scatter x1, waiting for transfers between devices, on_device(): lax.psum_scatter(in_grad.astype(jnp.bfloat16), 'group', scatter_dimension...  69.7 us
    reduce_scatter x1, waiting for transfers between devices, on_device(): lax.psum_scatter(qkv_weight_grad.astype(jnp.bfloat16), 'group', scatter_d...  69.1 us
    all_gather x1, waiting for transfers between devices, on_device(): lax.all_gather(w_in, 'group', axis=0, tiled=True)  65.8 us
    all_gather x1, waiting for transfers between devices, on_device(): lax.all_gather(w_qkv, 'group', axis=0, tiled=True)  56.7 us
    all_gather x1, waiting for transfers between devices, on_device(): lax.all_gather(w_down, 'group', axis=0, tiled=True)  36.6 us
    reduce_scatter x1, waiting for transfers between devices, on_device(): lax.psum_scatter(down_grad.astype(jnp.bfloat16), 'group', scatter_dimensi...  24.8 us
    all_gather x1, waiting for transfers between devices, on_device(): lax.all_gather(w_out, 'group', axis=0, tiled=True)  22.7 us
  transfers between devices with their start and end apart: 8, of which 7 were waited for; matrix products, arithmetic and copies ran while one was open for 9% of the time, Pallas kernels for 0%

commit v1 on v0

v1 whole, which is shorter than its diff:
```python
import functools

import jax
import jax.numpy as jnp
from jax import lax
from jax.experimental import pallas as pl
from jax.experimental.pallas import tpu as pltpu
from jax.sharding import PartitionSpec as P

HEADS = 12
HEAD_DIM = 64
FF = 1152
D = 768
TILE = 384
PAIR = 128

norm_eps = 1e-05
rope_base = 160000.0
head_scale = HEAD_DIM ** (-0.5)
f32 = jnp.float32
bf16 = jnp.bfloat16

VMEM = pl.BlockSpec(memory_space=pltpu.VMEM)
SMEM = pl.BlockSpec(memory_space=pltpu.SMEM)


def run(body, name, outs, place, ins, scratch=(), flops=0):
    moved = sum(a.size * a.dtype.itemsize for a in ins)
    moved += sum(o.size * o.dtype.itemsize for o in outs)
    return pl.pallas_call(
        body,
        out_shape=outs,
        in_specs=[SMEM] + [VMEM] * len(ins),
        out_specs=[VMEM] * len(outs),
        scratch_shapes=list(scratch),
        compiler_params=pltpu.CompilerParams(vmem_limit_bytes=44 * 1024 * 1024),
        cost_estimate=pl.CostEstimate(flops=flops, bytes_accessed=moved, transcendentals=0),
        name=name,
    )(place, *ins)


def shape(dims, dtype=bf16):
    return jax.ShapeDtypeStruct(dims, dtype)


def dot(a, b):
    return lax.dot_general(a, b, (((1,), (0,)), ((), ())), preferred_element_type=f32)


def dot_bt(a, b):
    return lax.dot_general(a, b, (((1,), (1,)), ((), ())), preferred_element_type=f32)


def dot_at(a, b):
    return lax.dot_general(a, b, (((0,), (0,)), ((), ())), preferred_element_type=f32)


def token_positions(segment):
    length = segment.shape[0]
    index = jnp.arange(length, dtype=jnp.int32)
    before = jnp.concatenate([jnp.full((1,), -1, jnp.int32), segment[:-1]])
    first = lax.cummax(jnp.where(segment != before, index, 0), axis=0)
    return index - first


def rotary_tables(position):
    half_dim = HEAD_DIM // 2
    inverse = rope_base ** (-(jnp.arange(half_dim, dtype=f32) * 2.0 / HEAD_DIM))
    angles = position.astype(f32)[:, None] * inverse[None, :]
    cosine, sine = jnp.cos(angles), jnp.sin(angles)
    return (
        jnp.concatenate([cosine] * 4, axis=1),
        jnp.concatenate([-sine, sine, -sine, sine], axis=1),
    )


def rows(start, size, step=16):
    return pl.ds(pl.multiple_of(start, step), size)


def columns(start, size):
    return pl.ds(pl.multiple_of(start, 128), size)


def assemble(place, parts, full, own, groups, high, low, width, start):
    z, hb, lb, core = place[0], place[1], place[2], place[3]
    shard = own.shape[0]
    full[rows(z * shard, shard), :] = own[...]
    for index, part in enumerate(parts):
        flip_low, flip_high, other = index & 1, (index >> 1) & 1, index >> 2
        hi = (lb if other else hb) ^ flip_high
        lo = (hb if other else lb) ^ flip_low
        half = core ^ other
        for k in range(1, groups):
            group = lax.rem(z + groups - k, groups)
            at = group * shard + hi * high + lo * low
            full[rows(at, part.shape[1]), columns(half * width, width)] = part[
                k - 1, :, start : start + width
            ]


def norm_parts(values):
    centred = values - jnp.mean(values, axis=1, keepdims=True)
    inverse = lax.rsqrt(jnp.mean(centred * centred, axis=1, keepdims=True) + norm_eps)
    return centred * inverse, inverse


def norm_back(upstream, normed, inverse, gain):
    gain_grad = jnp.sum(upstream * normed, axis=0, keepdims=True)
    scaled = upstream * gain
    inner = (
        scaled
        - jnp.mean(scaled, axis=1, keepdims=True)
        - normed * jnp.mean(scaled * normed, axis=1, keepdims=True)
    )
    return inverse * inner, gain_grad


def swap_halves(u):
    lane = lax.broadcasted_iota(jnp.int32, u.shape, 1)
    return jnp.where(lane % HEAD_DIM < HEAD_DIM // 2, pltpu.roll(u, PAIR - 32, 1), pltpu.roll(u, 32, 1))


def head_masks():
    lane = lax.broadcasted_iota(jnp.int32, (1, PAIR), 1)
    first = (lane < HEAD_DIM).astype(f32)
    return first.astype(bf16), (1.0 - first).astype(bf16)


def attn_forward(groups, place, tok, gains, cosine, sine, seg_col, seg_row, own, *rest):
    parts, (attn_in, qkv, mixed, lse, w_full) = rest[:8], rest[8:]
    assemble(place, parts, w_full, own, groups, 96, 48, 3 * D // 2, 0)
    normed, _ = norm_parts(tok[...].astype(f32))
    attn_in[...] = (normed * gains[0:1, :]).astype(bf16)

    def turned(j, _):
        at = columns(j * TILE, TILE)
        raw = dot(attn_in[...], w_full[:, at])
        turned_parts = []
        for i in range(TILE // PAIR):
            u = raw[:, i * PAIR : (i + 1) * PAIR]
            turned_parts.append(u * cosine[...] + swap_halves(u) * sine[...])
        qkv[:, at] = jnp.concatenate(turned_parts, axis=1).astype(bf16)
        return 0

    lax.fori_loop(0, 4, turned, 0)

    def plain(j, _):
        at = columns(j * TILE, TILE)
        qkv[:, at] = dot(attn_in[...], w_full[:, at]).astype(bf16)
        return 0

    lax.fori_loop(4, 6, plain, 0)
    masks = head_masks()
    same = seg_col[...] == seg_row[...]
    lane = lax.broadcasted_iota(jnp.int32, (tok.shape[0], PAIR), 1)

    def pair(j, kept):
        q = qkv[:, columns(j * PAIR, PAIR)]
        k = qkv[:, columns(D + j * PAIR, PAIR)]
        v = qkv[:, columns(2 * D + j * PAIR, PAIR)]
        made = []
        for a in range(2):
            scores = dot_bt(q * masks[a], k) * head_scale
            scores = jnp.where(same, scores, -1e30)
            top = jnp.max(scores, axis=1, keepdims=True)
            e = jnp.exp(scores - top)
            total = jnp.sum(e, axis=1, keepdims=True)
            probs = (e * (1.0 / total)).astype(bf16)
            made.append(dot(probs, v))
            kept = jnp.where(lane == 2 * j + a, top + jnp.log(total), kept)
        mixed[:, columns(j * PAIR, PAIR)] = jnp.where(lane < HEAD_DIM, made[0], made[1]).astype(bf16)
        return kept

    lse[...] = lax.fori_loop(0, HEADS // 2, pair, jnp.zeros((tok.shape[0], PAIR), f32))


def mlp_forward(groups, place, tok, mixed, gains, own_in, own_out, *rest):
    parts, rest = rest[:8], rest[8:]
    middle, mlp_in, hidden, act, slope, w_in, w_out = rest
    assemble(place, parts, w_out, own_out, groups, 96, 48, D // 2, FF)
    assemble(place, parts, w_in, own_in, groups, 96, 48, FF, 0)
    for j in range(2):
        at = slice(j * TILE, (j + 1) * TILE)
        middle[:, at] = tok[:, at].astype(f32) + dot(mixed[...], w_out[:, at])
    normed, _ = norm_parts(middle[...])
    mlp_in[...] = (normed * gains[1:2, :]).astype(bf16)

    def step(j, _):
        at = columns(j * TILE, TILE)
        u = dot(mlp_in[...], w_in[:, at])
        gate = dot(mlp_in[...], w_in[:, columns(FF + j * TILE, TILE)])
        cdf = 0.5 + 0.5 * lax.erf(u * 0.7071067811865476)
        a = u * cdf
        act[:, at] = a
        slope[:, at] = gate * (cdf + u * (0.3989422804014327 * jnp.exp(-0.5 * u * u)))
        hidden[:, at] = (a * gate).astype(bf16)
        return 0

    lax.fori_loop(0, FF // TILE, step, 0)


def down_backward(groups, place, grad_out, hidden, middle, act, slope, own, *rest):
    parts, (output, gate_up_grad, w_down) = rest[:8], rest[8:]
    assemble(place, parts, w_down, own, groups, 144, 64, D // 2, 0)

    def step(j, _):
        at = columns(j * TILE, TILE)
        hidden_grad = dot_bt(grad_out[...], w_down[rows(j * TILE, TILE), :])
        gate_up_grad[:, at] = (hidden_grad * slope[:, at]).astype(bf16)
        gate_up_grad[:, columns(FF + j * TILE, TILE)] = (hidden_grad * act[:, at]).astype(bf16)
        return 0

    lax.fori_loop(0, FF // TILE, step, 0)
    for j in range(2):
        at = slice(j * TILE, (j + 1) * TILE)
        output[:, at] = (middle[:, at] + dot(hidden[...], w_down[:, at])).astype(bf16)


def mlp_backward(groups, place, gate_up_grad, grad_out, middle, gains, own_in, own_out, *rest):
    parts, rest = rest[:8], rest[8:]
    middle_grad, branch_grad, mixed_grad, gain_grad, w_in, w_out, total = rest
    assemble(place, parts, w_in, own_in, groups, 96, 48, FF, 0)
    assemble(place, parts, w_out, own_out, groups, 96, 48, D // 2, FF)

    def step(j, _):
        total[:, columns(j * 256, 256)] = dot_bt(gate_up_grad[...], w_in[rows(j * 256, 256), :])
        return 0

    lax.fori_loop(0, D // 256, step, 0)
    normed, inverse = norm_parts(middle[...])
    part, gain_grad[...] = norm_back(total[...], normed, inverse, gains[1:2, :])
    whole = grad_out[...].astype(f32) + part
    middle_grad[...] = whole
    branch_grad[...] = whole.astype(bf16)

    def back(j, _):
        mixed_grad[:, columns(j * 256, 256)] = dot_bt(
            branch_grad[...], w_out[rows(j * 256, 256), :]
        ).astype(bf16)
        return 0

    lax.fori_loop(0, D // 256, back, 0)


def attn_backward(place, qkv, lse, mixed_grad, cosine, sine, seg_col, seg_row, qkv_grad):
    masks = head_masks()
    same = seg_col[...] == seg_row[...]
    length = qkv.shape[0]
    lane = lax.broadcasted_iota(jnp.int32, (length, PAIR), 1)

    def pair(j, _):
        q = qkv[:, columns(j * PAIR, PAIR)]
        k = qkv[:, columns(D + j * PAIR, PAIR)]
        v = qkv[:, columns(2 * D + j * PAIR, PAIR)]
        upstream = mixed_grad[:, columns(j * PAIR, PAIR)]
        made = []
        for a in range(2):
            scores = dot_bt(q * masks[a], k) * head_scale
            log_total = jnp.sum(jnp.where(lane == 2 * j + a, lse[...], 0.0), axis=1, keepdims=True)
            probs = jnp.where(same, jnp.exp(scores - log_total), 0.0)
            prob_grad = dot_bt(upstream * masks[a], v)
            delta = jnp.sum(probs * prob_grad, axis=1, keepdims=True)
            score_grad = (probs * (prob_grad - delta)).astype(bf16)
            made.append(
                (
                    dot(score_grad, k),
                    dot_at(score_grad, q),
                    dot_at(probs.astype(bf16), upstream),
                )
            )
        first = lane < HEAD_DIM
        for i in range(2):
            u = jnp.where(first, made[0][i], made[1][i]) * head_scale
            u = u * cosine[...] - swap_halves(u) * sine[...]
            qkv_grad[:, columns(i * D + j * PAIR, PAIR)] = u.astype(bf16)
        qkv_grad[:, columns(2 * D + j * PAIR, PAIR)] = jnp.where(first, made[0][2], made[1][2]).astype(bf16)
        return 0

    lax.fori_loop(0, HEADS // 2, pair, 0)


def attn_in_backward(groups, place, qkv_grad, tok, middle_grad, gains, own, *rest):
    parts, (tokens_grad, gain_grad, w_full, total) = rest[:8], rest[8:]
    assemble(place, parts, w_full, own, groups, 96, 48, 3 * D // 2, 0)

    def step(j, _):
        total[:, columns(j * 256, 256)] = dot_bt(qkv_grad[...], w_full[rows(j * 256, 256), :])
        return 0

    lax.fori_loop(0, D // 256, step, 0)
    normed, inverse = norm_parts(tok[...].astype(f32))
    part, gain_grad[...] = norm_back(total[...], normed, inverse, gains[0:1, :])
    tokens_grad[...] = (middle_grad[...] + part).astype(bf16)


def grad_for_other(pairs, place, *refs):
    ins, out, flipped = refs[: 2 * pairs], refs[2 * pairs], refs[2 * pairs + 1]
    core = place[3]
    start = 0
    for i in range(pairs):
        x, dy = ins[2 * i], ins[2 * i + 1]
        half = dy.shape[1] // 2
        flipped[...] = x[...].T

        def step(t, _, dy=dy, half=half, start=start):
            made = dot(flipped[...], dy[:, columns((1 - core) * half + t * TILE, TILE)])
            out[:, columns(start + t * TILE, TILE)] = made.astype(bf16)
            return 0

        lax.fori_loop(0, half // TILE, step, 0)
        start += half


def grad_for_self(pairs, groups, place, *refs):
    ins, got, keep, send, natural, ordered = refs[: 2 * pairs], *refs[2 * pairs :]
    hb, core = place[1], place[3]
    high = keep.shape[1]
    cut = groups * high
    start = 0
    for i in range(pairs):
        x, dy = ins[2 * i], ins[2 * i + 1]
        half = dy.shape[1] // 2
        natural[...] = x[...].T
        for side in range(2):
            for g in range(groups):
                at = g * 2 * high + (hb ^ side) * high
                ordered[side * cut + g * high : side * cut + (g + 1) * high, :] = natural[rows(at, high), :]

        def step(t, _, dy=dy, half=half, start=start):
            made = dot(ordered[...], dy[:, columns(core * half + t * TILE, TILE)])
            out_at = columns(start + t * TILE, TILE)
            for side, target in enumerate((keep, send)):
                for g in range(groups):
                    at = g * 2 * high + (hb ^ side) * high
                    mine = made[side * cut + g * high : side * cut + (g + 1) * high, :]
                    target[g, :, out_at] = (mine + got[rows(at, high), out_at].astype(f32)).astype(bf16)
            return 0

        lax.fori_loop(0, half // TILE, step, 0)
        start += half


def add_split(groups, place, mine, got, keep, send):
    lb = place[2]
    low = keep.shape[1]
    step = mine.shape[1] - low
    for side, target in enumerate((keep, send)):
        at = rows((lb ^ side) * step, low)
        for g in range(groups):
            target[g] = (mine[g, at, :].astype(f32) + got[g, at, :].astype(f32)).astype(bf16)


def add_owners(groups, place, mine, got, *outs):
    z = place[0]
    for k in range(groups):
        g = lax.rem(z + k, groups)
        outs[k][...] = (mine[g].astype(f32) + got[g].astype(f32)).astype(outs[k].dtype)


def place_pieces(high, low, widths, place, *refs):
    parts, outs = refs[:8], refs[8:]
    hb, lb, core = place[1], place[2], place[3]
    size = parts[0].shape[0]
    for other in range(2):
        for flip_high in range(2):
            hi = (lb if other else hb) ^ flip_high
            lo = hb if other else lb
            one = parts[other * 4 + flip_high * 2]
            two = parts[other * 4 + flip_high * 2 + 1]
            start = 0
            for out, width in zip(outs, widths):
                at = columns((core ^ other) * width, width)
                a = one[:, start : start + width].astype(f32)
                b = two[:, start : start + width].astype(f32)
                out[rows(hi * high + low, size, 8), at] = jnp.where(lo == 0, b, a)
                out[rows(hi * high, size, 8), at] = jnp.where(lo == 0, a, b)
                start += width


def make(mesh):
    groups, copies = mesh.shape["group"], mesh.shape["replica"]
    swap_core = [(i, i ^ 1) for i in range(copies)]
    swap_two = [(i, i ^ 2) for i in range(copies)]
    swap_four = [(i, i ^ 4) for i in range(copies)]
    swap_high = [(i, i ^ (4 if i & 1 else 2)) for i in range(copies)]
    swap_low = [(i, i ^ (2 if i & 1 else 4)) for i in range(copies)]

    def across(a, perm):
        return lax.ppermute(a, "replica", perm)

    def shifted(a, k):
        return lax.ppermute(a, "group", [(i, (i + k) % groups) for i in range(groups)])

    def far_sum(a):
        if copies == 8:
            return a
        same = [[j + 8 * m for m in range(copies // 8)] for j in range(8)]
        return lax.psum(a, "replica", axis_index_groups=same)

    def spread(piece):
        a = jnp.stack([shifted(piece, k) for k in range(1, groups)])
        b = across(a, swap_high)
        c, d = across(a, swap_low), across(b, swap_low)
        here = [a, c, b, d]
        return here + [across(t, swap_core) for t in here], a

    def reduced(pairs, high, low, size, widths, place):
        flat = [t for pair in pairs for t in pair]
        depth, width = pairs[0][0].shape[1], sum(widths)
        length = pairs[0][0].shape[0]
        cost = 2 * length * depth * width
        turned = pltpu.VMEM((depth, length), bf16)
        (for_other,) = run(
            functools.partial(grad_for_other, len(pairs)), "grad_for_other",
            [shape((depth, width))], place, flat, [turned], cost,
        )
        got = across(for_other, swap_core)
        keep, send = run(
            functools.partial(grad_for_self, len(pairs), groups), "grad_for_self",
            [shape((groups, high, width))] * 2, place, flat + [got], [turned, turned], cost,
        )
        got = across(send, swap_high)
        keep, send = run(
            functools.partial(add_split, groups), "add_split",
            [shape((groups, size, width))] * 2, place, [keep, got],
        )
        got = across(send, swap_low)
        mine, *others = run(
            functools.partial(add_owners, groups), "add_owners",
            [shape((size, width), f32)] + [shape((size, width))] * (groups - 1), place, [keep, got],
        )
        for k, t in enumerate(others):
            mine = mine + shifted(t, k + 1).astype(f32)
        a = far_sum(mine).astype(bf16)
        c = across(a, swap_low)
        b, d = across(a, swap_high), across(c, swap_high)
        here = [a, c, b, d]
        parts = here + [across(t, swap_core) for t in here]
        return run(
            functools.partial(place_pieces, high, low, widths), "place_pieces",
            [shape((2 * high, 2 * w), f32) for w in widths], place, parts,
        )

    def on_device(tokens, segment, g_attn, w_qkv, w_out, g_mlp, w_in, w_down, grad_out):
        length = tokens.shape[0]
        z = lax.axis_index("group")
        r = lax.axis_index("replica")
        core, two, four = r & 1, (r >> 1) & 1, (r >> 2) & 1
        hb = jnp.where(core == 1, four, two)
        lb = jnp.where(core == 1, two, four)
        place = jnp.stack([z, hb, lb, core]).astype(jnp.int32)

        def cut(w, high, low, size):
            half = w.shape[1] // 2
            return lax.dynamic_slice(w, (high * hb + low * lb, half * core), (size, half))

        qkv_parts, ahead = spread(cut(w_qkv, 96, 48, 48))
        piece = jnp.concatenate([cut(w_in, 96, 48, 48), cut(w_out, 96, 48, 48)], axis=1)
        piece, _ = lax.optimization_barrier((piece, ahead))
        in_parts, ahead = spread(piece)
        piece, _ = lax.optimization_barrier((cut(w_down, 144, 64, 80), ahead))
        down_parts, _ = spread(piece)
        own_gains = jnp.stack([g_attn, g_mlp]).astype(f32)
        by_distance = jnp.stack([own_gains] + [shifted(own_gains, k) for k in range(1, groups)])
        gains = jnp.concatenate(
            [
                lax.dynamic_index_in_dim(by_distance, lax.rem(z + groups - g, groups), keepdims=False)
                for g in range(groups)
            ],
            axis=1,
        )
        cosine, sine = rotary_tables(token_positions(segment))
        seg_col, seg_row = segment[:, None], segment[None, :]

        attn_in, qkv, mixed, lse = run(
            functools.partial(attn_forward, groups), "attn_forward",
            [shape((length, D)), shape((length, 3 * D)), shape((length, D)), shape((length, PAIR), f32)],
            place, [tokens, gains, cosine, sine, seg_col, seg_row, w_qkv] + qkv_parts,
            [pltpu.VMEM((D, 3 * D), bf16)], 2 * length * D * 3 * D * 2,
        )
        middle, mlp_in, hidden, act, slope = run(
            functools.partial(mlp_forward, groups), "mlp_forward",
            [shape((length, D), f32), shape((length, D)), shape((length, FF)), shape((length, FF), f32), shape((length, FF), f32)],
            place, [tokens, mixed, gains, w_in, w_out] + in_parts,
            [pltpu.VMEM((D, 2 * FF), bf16), pltpu.VMEM((D, D), bf16)], 2 * length * D * (2 * FF + D),
        )

        (down_grad,) = reduced([(hidden, grad_out)], 144, 64, 80, [D // 2], place)
        output, gate_up_grad = run(
            functools.partial(down_backward, groups), "down_backward",
            [shape((length, D)), shape((length, 2 * FF))],
            place, [grad_out, hidden, middle, act, slope, w_down] + down_parts,
            [pltpu.VMEM((FF, D), bf16)], 4 * length * D * FF,
        )
        (in_grad,) = reduced([(mlp_in, gate_up_grad)], 96, 48, 48, [FF], place)
        middle_grad, branch_grad, mixed_grad, gain_two_grad = run(
            functools.partial(mlp_backward, groups), "mlp_backward",
            [shape((length, D), f32), shape((length, D)), shape((length, D)), shape((1, D), f32)],
            place, [gate_up_grad, grad_out, middle, gains, w_in, w_out] + in_parts,
            [pltpu.VMEM((D, 2 * FF), bf16), pltpu.VMEM((D, D), bf16), pltpu.VMEM((length, D), f32)],
            2 * length * D * (2 * FF + D),
        )
        (qkv_grad,) = run(
            attn_backward, "attn_backward", [shape((length, 3 * D))],
            place, [qkv, lse, mixed_grad, cosine, sine, seg_col, seg_row], (), 4 * length * D * 3 * D,
        )
        qkv_weight_grad, out_grad = reduced(
            [(attn_in, qkv_grad), (mixed, branch_grad)], 96, 48, 48, [3 * D // 2, D // 2], place
        )
        tokens_grad, gain_one_grad = run(
            functools.partial(attn_in_backward, groups), "attn_in_backward",
            [shape((length, D)), shape((1, D), f32)],
            place, [qkv_grad, tokens, middle_grad, gains, w_qkv] + qkv_parts,
            [pltpu.VMEM((D, 3 * D), bf16), pltpu.VMEM((length, D), f32)], 2 * length * D * 3 * D,
        )

        gain_grads = jnp.concatenate([gain_one_grad, gain_two_grad], axis=0)
        for perm in (swap_core, swap_two, swap_four):
            gain_grads = gain_grads + across(gain_grads, perm)
        gain_grads = far_sum(gain_grads)
        total = gain_grads
        for k in range(1, groups):
            total = total + shifted(gain_grads, k)
        shard = g_attn.shape[0]
        owned = lax.dynamic_slice(total, (0, z * shard), (2, shard))
        return (
            output, tokens_grad, owned[0], qkv_weight_grad, out_grad, owned[1], in_grad, down_grad,
        )

    return on_device


def solution(mesh):
    both = ("replica", "group")
    in_specs = (
        P(both, None), P(both), P("group"), P("group", None), P("group", None),
        P("group"), P("group", None), P("group", None), P(both, None),
    )
    out_specs = (
        P(both, None), P(both, None), P("group"), P("group", None),
        P("group", None), P("group"), P("group", None), P("group", None),
    )
    return jax.shard_map(
        make(mesh), mesh=mesh, in_specs=in_specs, out_specs=out_specs, check_vma=False
    )
```

time: 554 us -> 226 us (0.41)
  waiting for transfers between devices: 348 us -> 70 us
  blocking collectives: 119 us -> 0 us
  starting transfers between devices: 0.5 us -> 84.3 us
  Pallas kernels: 0 us -> 53.2 us
  matrix products: 44.6 us -> 0 us
  between operations: 16 us -> 1.23 us
    all_gather x4 -> x0, waiting for transfers between devices: 182 us -> none  [the longest x1 65.8 us: on_device(): lax.all_gather(w_in, 'group', axis=0, tiled=True)]
    reduce_scatter x4 -> x0, waiting for transfers between devices: 164 us -> none  [the longest x1 69.7 us: on_device(): lax.psum_scatter(in_grad.astype(jnp.bfloat16), 'group', scatter_dimension...]
    psum x1 -> x0, blocking collectives: 103 us -> none  [on_device(): lax.psum((attn_owned[0], attn_owned[1], attn_owned[2], mlp_owned[0], mlp_...]
    ppermute x0 -> x78, starting transfers between devices: none -> 84.3 us  [the longest x54 54.8 us: across(): return lax.ppermute(a, 'replica', perm)]
    ppermute x0 -> x78, waiting for transfers between devices: none -> 70 us  [the longest x54 43.7 us: across(): return lax.ppermute(a, 'replica', perm)]
    pallas_call x0 -> x21, Pallas kernels: none -> 53.2 us  [run(): pl.pallas_call(body, out_shape=outs, in_specs=[SMEM] + [VMEM] * len(ins),...]
    dot_general x18 -> x0, matrix products: 44.6 us -> none  [the longest x1 5.49 us: on_device(): jnp.einsum('nd,fd->nf', grad_out, mlp_full[2], preferred_element_type=jnp...]
    unnamed x2 -> x0, blocking collectives: 15.9 us -> none
  transfers between devices with their start and end apart: 8 -> 78, of which waited for: 7 -> 20; matrix products, arithmetic and copies ran while one was open for 9% -> 4% of each run, Pallas kernels for 0% -> 15%
where the time goes in v1:
time: 226 us; the launch traced here: 225 us
  starting transfers between devices  84.3 us (37%)
  waiting for transfers between devices  70 us (31%)
  Pallas kernels  53.2 us (24%)
  local copies, waits for them, and re-layouts  11.3 us (5%)
  other arithmetic  4.63 us (2%)
    ppermute x54, starting transfers between devices, across(): return lax.ppermute(a, 'replica', perm)  54.8 us
    pallas_call x21, Pallas kernels, run(): pl.pallas_call(body, out_shape=outs, in_specs=[SMEM] + [VMEM] * len(ins),...  53.2 us
    ppermute x54, waiting for transfers between devices, across(): return lax.ppermute(a, 'replica', perm)  43.7 us
    ppermute x24, starting transfers between devices, shifted(): lax.ppermute(a, 'group', [(i, (i + k) % groups) for i in range(groups)])  29.5 us
    ppermute x24, waiting for transfers between devices, shifted(): lax.ppermute(a, 'group', [(i, (i + k) % groups) for i in range(groups)])  26.3 us
    unnamed x60, local copies, waits for them, and re-layouts  5 us
  transfers between devices with their start and end apart: 78, of which 20 were waited for; matrix products, arithmetic and copies ran while one was open for 4% of the time, Pallas kernels for 15%

profile of v1, /device:TPU:9, one launch (start us, length us, event | category | flops | bytes accessed | tf_op | source)
XLA Modules:
  0.0 224.6 jit_solution(7452121182649551823)
XLA Ops:
  2.0 2.5 %collective-permute-start.1 = (f32[2,192]{1,0:T(2,128)S(1)}, f32[2,192]{1,0:T(2,128)S(1)}, u32[]{:S(2)}, u32[]{:S(2)}) collective-permute-start(f32[2,192]{1,0:T(2,128)S(1)} %maximum_convert_fusion.1), channel_id=1, source_target_pairs={{0,2},{1,3},{2,0},{3,1},{4,6},{5,7},{6,4},{7,5},{8,10},{9,11},{10,... | collective-permute-start | bytes 4616 | tf_op jit(solution)/shard_map/ppermute | solution.py:393
  6.5 2.4 %collective-permute-start.4 = (bf16[48,1152]{1,0:T(8,128)(2,1)S(1)}, bf16[48,1152]{1,0:T(8,128)(2,1)S(1)}, u32[]{:S(2)}, u32[]{:S(2)}) collective-permute-start(bf16[48,1152]{1,0:T(8,128)(2,1)S(1)} %dynamic_slice.32), channel_id=1, source_target_pairs={{0,2},{1,3},{2,0},{3,1},{4,6},{5,7},{6,4},{7,5},{8,10},{9,11},{10,... | collective-permute-start | bytes 331784 | tf_op jit(solution)/shard_map/ppermute | solution.py:393
  10.6 3.0 %collective-permute-done.4 = bf16[48,1152]{1,0:T(8,128)(2,1)S(1)} collective-permute-done((bf16[48,1152]{1,0:T(8,128)(2,1)S(1)}, bf16[48,1152]{1,0:T(8,128)(2,1)S(1)}, u32[]{:S(2)}, u32[]{:S(2)}) %collective-permute-start.4) | collective-permute-done | bytes 110624 | tf_op jit(solution)/shard_map/ppermute | solution.py:393
  13.6 2.5 %collective-permute-done.3 = bf16[48,1152]{1,0:T(8,128)(2,1)S(1)} collective-permute-done((bf16[48,1152]{1,0:T(8,128)(2,1)S(1)}, bf16[48,1152]{1,0:T(8,128)(2,1)S(1)}, u32[]{:S(2)}, u32[]{:S(2)}) %collective-permute-start.3) | collective-permute-done | bytes 110624 | tf_op jit(solution)/shard_map/ppermute | solution.py:393
  16.5 3.1 %collective-permute-start.14 = (bf16[48,1536]{1,0:T(8,128)(2,1)S(1)}, bf16[48,1536]{1,0:T(8,128)(2,1)S(1)}, u32[]{:S(2)}, u32[]{:S(2)}) collective-permute-start(bf16[48,1536]{1,0:T(8,128)(2,1)S(1)} %pad_maximum_fusion.3), channel_id=1, source_target_pairs={{0,2},{1,3},{2,0},{3,1},{4,6},{5,7},{6,4},{7,5},{8,10},{9,11},{10,... | collective-permute-start | bytes 442376 | tf_op jit(solution)/shard_map/ppermute | solution.py:393
  21.7 6.0 %collective-permute-done.14 = bf16[48,1536]{1,0:T(8,128)(2,1)S(1)} collective-permute-done((bf16[48,1536]{1,0:T(8,128)(2,1)S(1)}, bf16[48,1536]{1,0:T(8,128)(2,1)S(1)}, u32[]{:S(2)}, u32[]{:S(2)}) %collective-permute-start.14) | collective-permute-done | bytes 147488 | tf_op jit(solution)/shard_map/ppermute | solution.py:393
  27.7 3.2 %collective-permute-done.13 = bf16[48,1536]{1,0:T(8,128)(2,1)S(1)} collective-permute-done((bf16[48,1536]{1,0:T(8,128)(2,1)S(1)}, bf16[48,1536]{1,0:T(8,128)(2,1)S(1)}, u32[]{:S(2)}, u32[]{:S(2)}) %collective-permute-start.13) | collective-permute-done | bytes 147488 | tf_op jit(solution)/shard_map/ppermute | solution.py:393
  30.9 1.5 collective-permute-start.25
  32.5 1.9 collective-permute-start.24
  34.4 2.0 collective-permute-start.17
  37.6 2.4 %collective-permute-start.9 = (bf16[3,48,1152]{2,1,0:T(8,128)(2,1)S(1)}, bf16[3,48,1152]{2,1,0:T(8,128)(2,1)S(1)}, u32[]{:S(2)}, u32[]{:S(2)}) collective-permute-start(bf16[3,48,1152]{2,1,0:T(8,128)(2,1)S(1)} %pad_maximum_fusion.1.rest_0_), channel_id=1, source_target_pairs={{0,4},{4,0},{8,12},{12,8},{16,20},{20,16},{24,28},{28,24},{1,5},{5... | collective-permute-start | bytes 995336 | tf_op jit(solution)/shard_map/ppermute | solution.py:390
  42.8 1.9 collective-permute-start.19
  44.7 2.9 %collective-permute-done.7.rest_2_ = bf16[3,48,1152]{2,1,0:T(8,128)(2,1)} collective-permute-done((bf16[3,48,1152]{2,1,0:T(8,128)(2,1)S(1)}, bf16[3,48,1152]{2,1,0:T(8,128)(2,1)}, u32[]{:S(2)}, u32[]{:S(2)}) %collective-permute-start.7) | collective-permute-done | bytes 331808 | tf_op jit(solution)/shard_map/ppermute | solution.py:390
  47.6 2.0 collective-permute-start.16
  55.1 4.6 %collective-permute-done.26.rest_1_ = bf16[3,80,384]{2,1,0:T(8,128)(2,1)} collective-permute-done((bf16[3,80,384]{2,1,0:T(8,128)(2,1)}, bf16[3,80,384]{2,1,0:T(8,128)(2,1)}, u32[]{:S(2)}, u32[]{:S(2)}) %collective-permute-start.26) | collective-permute-done | bytes 184352 | tf_op jit(solution)/shard_map/ppermute | solution.py:390
  59.7 3.1 %collective-permute-start.11 = (bf16[3,48,1152]{2,1,0:T(8,128)(2,1)}, bf16[3,48,1152]{2,1,0:T(8,128)(2,1)S(1)}, u32[]{:S(2)}, u32[]{:S(2)}) collective-permute-start(bf16[3,48,1152]{2,1,0:T(8,128)(2,1)} %collective-permute-done.7.rest_2_), channel_id=1, source_target_pairs={{0,4},{4,0},{8,12},{12,8},{16,20},{20,16},{24,28},{28,24},{1,5},{5... | collective-permute-start | bytes 995336 | tf_op jit(solution)/shard_map/ppermute | solution.py:390
  64.0 1.6 pad_maximum_fusion.4
  65.6 2.9 %collective-permute-start.21 = (bf16[3,48,1536]{2,1,0:T(8,128)(2,1)S(1)}, bf16[3,48,1536]{2,1,0:T(8,128)(2,1)S(1)}, u32[]{:S(2)}, u32[]{:S(2)}) collective-permute-start(bf16[3,48,1536]{2,1,0:T(8,128)(2,1)S(1)} %collective-permute-done.17.rest_2_), channel_id=1, source_target_pairs={{0,4},{4,0},{8,12},{12,8},{16,20},{20,16},{24,28},{28,24},{1,5},{5... | collective-permute-start | bytes 1327112 | tf_op jit(solution)/shard_map/ppermute | solution.py:390
  70.0 3.0 %collective-permute-start.12 = (bf16[3,48,1152]{2,1,0:T(8,128)(2,1)S(1)}, bf16[3,48,1152]{2,1,0:T(8,128)(2,1)S(1)}, u32[]{:S(2)}, u32[]{:S(2)}) collective-permute-start(bf16[3,48,1152]{2,1,0:T(8,128)(2,1)S(1)} %collective-permute-done.8.rest_3_), channel_id=1, source_target_pairs={{0,4},{4,0},{8,12},{12,8},{16,20},{20,16},{24,28},{28,24},{1,5},{5... | collective-permute-start | bytes 995336 | tf_op jit(solution)/shard_map/ppermute | solution.py:390
  79.1 10.4 %attn_forward.1 = (bf16[256,768]{1,0:T(8,128)(2,1)S(1)}, bf16[256,2304]{1,0:T(8,128)(2,1)S(1)}, bf16[256,768]{1,0:T(8,128)(2,1)S(1)}, f32[256,128]{1,0:T(8,128)S(1)}) custom-call(s32[4]{0:T(128)S(1)} %pad_add_fusion.place, bf16[256,768]{1,0:T(8,128)(2,1)S(1)} %copy-done.2, f32[2,768]{1,0:T(2,128)S(1)} %pad_maximum_fusion.7.gains, ...), custom_call_target="tpu_custom_call" | custom-call | flops 1811939328 | bytes 6299648 | tf_op jit(solution)/shard_map/attn_forward/pallas_call | solution.py:30
  89.6 3.4 %mlp_forward.1 = (f32[256,768]{1,0:T(8,128)S(1)}, bf16[256,768]{1,0:T(8,128)(2,1)S(1)}, bf16[256,1152]{1,0:T(8,128)(2,1)S(1)}, f32[256,1152]{1,0:T(8,128)S(1)}, f32[256,1152]{1,0:T(8,128)S(1)}) custom-call(s32[4]{0:T(128)S(1)} %pad_add_fusion.place, bf16[256,768]{1,0:T(8,128)(2,1)S(1)} %copy-done.2, bf16[256,768]{1,0:T(8,128)(2,1)S(1)} %get-tuple-element.53.mixed.refs_2_, ...), custom_call_target="tpu_custom_call" | custom-call | flops 1207959552 | bytes 9639936 | tf_op jit(solution)/shard_map/mlp_forward/pallas_call | solution.py:30
  93.2 4.0 %down_backward.1 = (bf16[256,768]{1,0:T(8,128)(2,1)}, bf16[256,2304]{1,0:T(8,128)(2,1)S(1)}) custom-call(s32[4]{0:T(128)S(1)} %pad_add_fusion.place, bf16[256,768]{1,0:T(8,128)(2,1)S(1)} %copy-done, bf16[256,1152]{1,0:T(8,128)(2,1)S(1)} %get-tuple-element.55.hidden.refs_0_, f32[256,768]{1,0:T(8,128)S(1)} %get-tuple-element.56.middle, ...), custom_call_target="tpu_custom_call" | custom-call | flops 905969664 | bytes 7618560 | tf_op jit(solution)/shard_map/down_backward/pallas_call | solution.py:30
  97.2 3.9 %mlp_backward.1 = (f32[256,768]{1,0:T(8,128)S(1)}, bf16[256,768]{1,0:T(8,128)(2,1)S(1)}, bf16[256,768]{1,0:T(8,128)(2,1)S(1)}, f32[1,768]{1,0:T(1,128)S(1)}) custom-call(s32[4]{0:T(128)S(1)} %pad_add_fusion.place, bf16[256,2304]{1,0:T(8,128)(2,1)S(1)} %get-tuple-element.63.gate_up_grad.refs_1_, bf16[256,768]{1,0:T(8,128)(2,1)S(1)} %copy-done, ...), custom_call_target="tpu_custom_call" | custom-call | flops 1207959552 | bytes 8659968 | tf_op jit(solution)/shard_map/mlp_backward/pallas_call | solution.py:30
  102.0 7.0 %attn_backward.1.qkv_grad.refs_1_ = bf16[256,2304]{1,0:T(8,128)(2,1)S(1)} custom-call(s32[4]{0:T(128)S(1)} %pad_add_fusion.place, bf16[256,2304]{1,0:T(8,128)(2,1)S(1)} %get-tuple-element.61.qkv, f32[256,128]{1,0:T(8,128)S(1)} %get-tuple-element.62.lse, bf16[256,768]{1,0:T(8,128)(2,1)S(1)} %get-tuple-element.64.mixed_grad, ...), custom_call_target="tpu_custom_call" | custom-call | flops 1811939328 | bytes 3147776 | tf_op jit(solution)/shard_map/attn_backward/pallas_call | solution.py:30
  109.0 2.2 grad_for_other.3
  111.4 1.8 grad_for_other.4
  115.8 2.3 %grad_for_self.3 = (bf16[4,96,1536]{2,1,0:T(8,128)(2,1)S(1)}, bf16[4,96,1536]{2,1,0:T(8,128)(2,1)S(1)}) custom-call(s32[4]{0:T(128)S(1)} %pad_add_fusion.place, bf16[256,768]{1,0:T(8,128)(2,1)S(1)} %get-tuple-element.69.refs_0_, bf16[256,2304]{1,0:T(8,128)(2,1)S(1)} %attn_backward.1.qkv_grad.refs_1_, bf16[256,768]{1,0:T(8,128)(2,1)S(1)} %get-tuple-element.53.mixed.refs_2_, ...), custom_call_target="tpu_custom_call" | custom-call | flops 603979776 | bytes 7077888 | tf_op jit(solution)/shard_map/grad_for_self/pallas_call | solution.py:30
  118.1 1.8 collective-permute-start.40
  120.0 1.8 grad_for_self.4
  124.7 4.3 %attn_in_backward.1 = (bf16[256,768]{1,0:T(8,128)(2,1)}, f32[1,768]{1,0:T(1,128)S(1)}) custom-call(s32[4]{0:T(128)S(1)} %pad_add_fusion.place, bf16[256,2304]{1,0:T(8,128)(2,1)S(1)} %attn_backward.1.qkv_grad.refs_1_, bf16[256,768]{1,0:T(8,128)(2,1)S(1)} %copy-done.2, f32[256,768]{1,0:T(8,128)S(1)} %copy-done.9, f32[2,768]{1,0:T(2,128)S(1)} %pad_maximum_fusion.7.gains, ...), custom_call_target="tpu_custom_call" | custom-call | flops 905969664 | bytes 6300672 | tf_op jit(solution)/shard_map/attn_in_backward/pallas_call | solution.py:30
  129.0 4.8 %collective-permute-done.40.got = bf16[4,96,1536]{2,1,0:T(8,128)(2,1)S(1)} collective-permute-done((bf16[4,96,1536]{2,1,0:T(8,128)(2,1)S(1)}, bf16[4,96,1536]{2,1,0:T(8,128)(2,1)S(1)}, u32[]{:S(2)}, u32[]{:S(2)}) %collective-permute-start.40) | collective-permute-done | bytes 1179680 | tf_op jit(solution)/shard_map/ppermute | solution.py:390
  135.7 1.8 collective-permute-start.33
  137.5 16.8 %collective-permute-done.66.got = bf16[4,144,384]{2,1,0:T(8,128)(2,1)S(1)} collective-permute-done((bf16[4,144,384]{2,1,0:T(8,128)(2,1)S(1)}, bf16[4,144,384]{2,1,0:T(8,128)(2,1)S(1)}, u32[]{:S(2)}, u32[]{:S(2)}) %collective-permute-start.66) | collective-permute-done | bytes 442400 | tf_op jit(solution)/shard_map/ppermute | solution.py:390
  158.4 6.9 %collective-permute-done.34 = f32[2,768]{1,0:T(2,128)S(1)} collective-permute-done((f32[2,768]{1,0:T(2,128)S(1)}, f32[2,768]{1,0:T(2,128)S(1)}, u32[]{:S(2)}, u32[]{:S(2)}) %collective-permute-start.34) | collective-permute-done | bytes 6176 | tf_op jit(solution)/shard_map/ppermute | solution.py:390
  167.5 2.2 collective-permute-start.68
  169.7 1.7 collective-permute-start.69
  171.4 1.9 collective-permute-start.38
  174.0 1.6 collective-permute-done.38
  178.2 2.4 %collective-permute-start.43 = (bf16[48,1536]{1,0:T(8,128)(2,1)S(1)}, bf16[48,1536]{1,0:T(8,128)(2,1)S(1)}, u32[]{:S(2)}, u32[]{:S(2)}) collective-permute-start(bf16[48,1536]{1,0:T(8,128)(2,1)S(1)} %get-tuple-element.77), channel_id=1, source_target_pairs={{0,2},{1,3},{2,0},{3,1},{4,6},{5,7},{6,4},{7,5},{8,10},{9,11},{10,... | collective-permute-start | bytes 442376 | tf_op jit(solution)/shard_map/ppermute | solution.py:393
  184.3 6.3 %collective-permute-done.43 = bf16[48,1536]{1,0:T(8,128)(2,1)S(1)} collective-permute-done((bf16[48,1536]{1,0:T(8,128)(2,1)S(1)}, bf16[48,1536]{1,0:T(8,128)(2,1)S(1)}, u32[]{:S(2)}, u32[]{:S(2)}) %collective-permute-start.43) | collective-permute-done | bytes 147488 | tf_op jit(solution)/shard_map/ppermute | solution.py:393
  190.7 3.1 %collective-permute-start.56 = (bf16[48,1152]{1,0:T(8,128)(2,1)S(1)}, bf16[48,1152]{1,0:T(8,128)(2,1)S(1)}, u32[]{:S(2)}, u32[]{:S(2)}) collective-permute-start(bf16[48,1152]{1,0:T(8,128)(2,1)S(1)} %get-tuple-element.88), channel_id=1, source_target_pairs={{0,2},{1,3},{2,0},{3,1},{4,6},{5,7},{6,4},{7,5},{8,10},{9,11},{10,... | collective-permute-start | bytes 331784 | tf_op jit(solution)/shard_map/ppermute | solution.py:393
  193.8 2.7 %collective-permute-done.44 = bf16[48,1536]{1,0:T(8,128)(2,1)S(1)} collective-permute-done((bf16[48,1536]{1,0:T(8,128)(2,1)S(1)}, bf16[48,1536]{1,0:T(8,128)(2,1)S(1)}, u32[]{:S(2)}, u32[]{:S(2)}) %collective-permute-start.44) | collective-permute-done | bytes 147488 | tf_op jit(solution)/shard_map/ppermute | solution.py:393
  196.5 2.3 %collective-permute-start.74 = (bf16[80,384]{1,0:T(8,128)(2,1)S(1)}, bf16[80,384]{1,0:T(8,128)(2,1)S(1)}, u32[]{:S(2)}, u32[]{:S(2)}) collective-permute-start(bf16[80,384]{1,0:T(8,128)(2,1)S(1)} %add_convert_fusion.2.refs_0_), channel_id=1, source_target_pairs={{0,4},{4,0},{8,12},{12,8},{16,20},{20,16},{24,28},{28,24},{1,5},{5... | collective-permute-start | bytes 184328 | tf_op jit(solution)/shard_map/ppermute | solution.py:390
  200.3 1.6 collective-permute-start.76
  203.8 2.0 collective-permute-start.61
  213.4 2.8 %collective-permute-done.60.refs_3_ = bf16[48,1152]{1,0:T(8,128)(2,1)S(1)} collective-permute-done((bf16[48,1152]{1,0:T(8,128)(2,1)S(1)}, bf16[48,1152]{1,0:T(8,128)(2,1)S(1)}, u32[]{:S(2)}, u32[]{:S(2)}) %collective-permute-start.60) | collective-permute-done | bytes 110624 | tf_op jit(solution)/shard_map/ppermute | solution.py:390
  220.6 1.9 place_pieces.4
  222.5 2.1 place_pieces.3
  (226 shorter events, 63.1 us)
Async XLA Ops:
  2.0 32.4 %collective-permute-start.2 = (f32[2,192]{1,0:T(2,128)S(1)}, f32[2,192]{1,0:T(2,128)S(1)}, u32[]{:S(2)}, u32[]{:S(2)}) collective-permute-start(f32[2,192]{1,0:T(2,128)S(1)} %maximum_convert_fusion.1), channel_id=1, source_target_pairs={{0,3},{1,0},{2,1},{3,2},{4,7},{5,4},{6,5},{7,6},{8,11},{9,8},{10,9... | collective-permute-start | bytes 4616 | tf_op jit(solution)/shard_map/ppermute | solution.py:393
  2.0 34.3 %collective-permute-start.1 = (f32[2,192]{1,0:T(2,128)S(1)}, f32[2,192]{1,0:T(2,128)S(1)}, u32[]{:S(2)}, u32[]{:S(2)}) collective-permute-start(f32[2,192]{1,0:T(2,128)S(1)} %maximum_convert_fusion.1), channel_id=1, source_target_pairs={{0,2},{1,3},{2,0},{3,1},{4,6},{5,7},{6,4},{7,5},{8,10},{9,11},{10,... | collective-permute-start | bytes 4616 | tf_op jit(solution)/shard_map/ppermute | solution.py:393
  6.5 7.1 %collective-permute-start.4 = (bf16[48,1152]{1,0:T(8,128)(2,1)S(1)}, bf16[48,1152]{1,0:T(8,128)(2,1)S(1)}, u32[]{:S(2)}, u32[]{:S(2)}) collective-permute-start(bf16[48,1152]{1,0:T(8,128)(2,1)S(1)} %dynamic_slice.32), channel_id=1, source_target_pairs={{0,2},{1,3},{2,0},{3,1},{4,6},{5,7},{6,4},{7,5},{8,10},{9,11},{10,... | collective-permute-start | bytes 331784 | tf_op jit(solution)/shard_map/ppermute | solution.py:393
  8.8 7.2 %collective-permute-start.3 = (bf16[48,1152]{1,0:T(8,128)(2,1)S(1)}, bf16[48,1152]{1,0:T(8,128)(2,1)S(1)}, u32[]{:S(2)}, u32[]{:S(2)}) collective-permute-start(bf16[48,1152]{1,0:T(8,128)(2,1)S(1)} %dynamic_slice.32), channel_id=1, source_target_pairs={{0,1},{1,2},{2,3},{3,0},{4,5},{5,6},{6,7},{7,4},{8,9},{9,10},{10,1... | collective-permute-start | bytes 331784 | tf_op jit(solution)/shard_map/ppermute | solution.py:393
  16.5 11.2 %collective-permute-start.14 = (bf16[48,1536]{1,0:T(8,128)(2,1)S(1)}, bf16[48,1536]{1,0:T(8,128)(2,1)S(1)}, u32[]{:S(2)}, u32[]{:S(2)}) collective-permute-start(bf16[48,1536]{1,0:T(8,128)(2,1)S(1)} %pad_maximum_fusion.3), channel_id=1, source_target_pairs={{0,2},{1,3},{2,0},{3,1},{4,6},{5,7},{6,4},{7,5},{8,10},{9,11},{10,... | collective-permute-start | bytes 442376 | tf_op jit(solution)/shard_map/ppermute | solution.py:393
  19.6 11.3 %collective-permute-start.13 = (bf16[48,1536]{1,0:T(8,128)(2,1)S(1)}, bf16[48,1536]{1,0:T(8,128)(2,1)S(1)}, u32[]{:S(2)}, u32[]{:S(2)}) collective-permute-start(bf16[48,1536]{1,0:T(8,128)(2,1)S(1)} %pad_maximum_fusion.3), channel_id=1, source_target_pairs={{0,1},{1,2},{2,3},{3,0},{4,5},{5,6},{6,7},{7,4},{8,9},{9,10},{10,1... | collective-permute-start | bytes 442376 | tf_op jit(solution)/shard_map/ppermute | solution.py:393
  32.5 7.6 %collective-permute-start.24 = (bf16[80,384]{1,0:T(8,128)(2,1)S(1)}, bf16[80,384]{1,0:T(8,128)(2,1)S(1)}, u32[]{:S(2)}, u32[]{:S(2)}) collective-permute-start(bf16[80,384]{1,0:T(8,128)(2,1)S(1)} %dynamic_slice.35), channel_id=1, source_target_pairs={{0,2},{1,3},{2,0},{3,1},{4,6},{5,7},{6,4},{7,5},{8,10},{9,11},{10,... | collective-permute-start | bytes 184328 | tf_op jit(solution)/shard_map/ppermute | solution.py:393
  34.4 18.6 %collective-permute-start.17 = (bf16[3,48,1536]{2,1,0:T(8,128)(2,1)S(1)}, bf16[3,48,1536]{2,1,0:T(8,128)(2,1)S(1)}, u32[]{:S(2)}, u32[]{:S(2)}) collective-permute-start(bf16[3,48,1536]{2,1,0:T(8,128)(2,1)S(1)} %pad_maximum_fusion.rest_0_), channel_id=1, source_target_pairs={{0,8},{4,20},{8,0},{12,28},{16,24},{20,4},{24,16},{28,12},{1,9},{5... | collective-permute-start | bytes 1327112 | tf_op jit(solution)/shard_map/ppermute | solution.py:390
  40.0 7.6 %collective-permute-start.7 = (bf16[3,48,1152]{2,1,0:T(8,128)(2,1)S(1)}, bf16[3,48,1152]{2,1,0:T(8,128)(2,1)}, u32[]{:S(2)}, u32[]{:S(2)}) collective-permute-start(bf16[3,48,1152]{2,1,0:T(8,128)(2,1)S(1)} %pad_maximum_fusion.1.rest_0_), channel_id=1, source_target_pairs={{0,8},{4,20},{8,0},{12,28},{16,24},{20,4},{24,16},{28,12},{1,9},{5... | collective-permute-start | bytes 995336 | tf_op jit(solution)/shard_map/ppermute | solution.py:390
  41.3 9.9 %collective-permute-start.6 = (bf16[3,48,1152]{2,1,0:T(8,128)(2,1)S(1)}, bf16[3,48,1152]{2,1,0:T(8,128)(2,1)S(1)}, u32[]{:S(2)}, u32[]{:S(2)}) collective-permute-start(bf16[3,48,1152]{2,1,0:T(8,128)(2,1)S(1)} %pad_maximum_fusion.1.rest_0_), channel_id=1, source_target_pairs={{0,16},{4,12},{8,24},{12,4},{16,0},{20,28},{24,8},{28,20},{1,17},{... | collective-permute-start | bytes 995336 | tf_op jit(solution)/shard_map/ppermute | solution.py:390
  42.2 9.3 %collective-permute-start.27 = (bf16[3,80,384]{2,1,0:T(8,128)(2,1)}, bf16[3,80,384]{2,1,0:T(8,128)(2,1)S(1)}, u32[]{:S(2)}, u32[]{:S(2)}) collective-permute-start(bf16[3,80,384]{2,1,0:T(8,128)(2,1)} %pad_maximum_fusion.2.rest_0_), channel_id=1, source_target_pairs={{0,8},{4,20},{8,0},{12,28},{16,24},{20,4},{24,16},{28,12},{1,9},{5... | collective-permute-start | bytes 552968 | tf_op jit(solution)/shard_map/ppermute | solution.py:390
  42.8 22.7 %collective-permute-start.19 = (bf16[3,48,1536]{2,1,0:T(8,128)(2,1)S(1)}, bf16[3,48,1536]{2,1,0:T(8,128)(2,1)S(1)}, u32[]{:S(2)}, u32[]{:S(2)}) collective-permute-start(bf16[3,48,1536]{2,1,0:T(8,128)(2,1)S(1)} %pad_maximum_fusion.rest_0_), channel_id=1, source_target_pairs={{0,4},{4,0},{8,12},{12,8},{16,20},{20,16},{24,28},{28,24},{1,5},{5... | collective-permute-start | bytes 1327112 | tf_op jit(solution)/shard_map/ppermute | solution.py:390
  47.6 20.8 %collective-permute-start.16 = (bf16[3,48,1536]{2,1,0:T(8,128)(2,1)S(1)}, bf16[3,48,1536]{2,1,0:T(8,128)(2,1)S(1)}, u32[]{:S(2)}, u32[]{:S(2)}) collective-permute-start(bf16[3,48,1536]{2,1,0:T(8,128)(2,1)S(1)} %pad_maximum_fusion.rest_0_), channel_id=1, source_target_pairs={{0,16},{4,12},{8,24},{12,4},{16,0},{20,28},{24,8},{28,20},{1,17},{... | collective-permute-start | bytes 1327112 | tf_op jit(solution)/shard_map/ppermute | solution.py:390
  51.2 8.5 %collective-permute-start.26 = (bf16[3,80,384]{2,1,0:T(8,128)(2,1)}, bf16[3,80,384]{2,1,0:T(8,128)(2,1)}, u32[]{:S(2)}, u32[]{:S(2)}) collective-permute-start(bf16[3,80,384]{2,1,0:T(8,128)(2,1)} %pad_maximum_fusion.2.rest_0_), channel_id=1, source_target_pairs={{0,16},{4,12},{8,24},{12,4},{16,0},{20,28},{24,8},{28,20},{1,17},{... | collective-permute-start | bytes 552968 | tf_op jit(solution)/shard_map/ppermute | solution.py:390
  51.5 11.3 %collective-permute-start.28 = (bf16[3,80,384]{2,1,0:T(8,128)(2,1)S(1)}, bf16[3,80,384]{2,1,0:T(8,128)(2,1)}, u32[]{:S(2)}, u32[]{:S(2)}) collective-permute-start(bf16[3,80,384]{2,1,0:T(8,128)(2,1)S(1)} %collective-permute-done.27.rest_2_), channel_id=1, source_target_pairs={{0,16},{4,12},{8,24},{12,4},{16,0},{20,28},{24,8},{28,20},{1,17},{... | collective-permute-start | bytes 552968 | tf_op jit(solution)/shard_map/ppermute | solution.py:390
  52.9 20.0 %collective-permute-start.18 = (bf16[3,48,1536]{2,1,0:T(8,128)(2,1)S(1)}, bf16[3,48,1536]{2,1,0:T(8,128)(2,1)S(1)}, u32[]{:S(2)}, u32[]{:S(2)}) collective-permute-start(bf16[3,48,1536]{2,1,0:T(8,128)(2,1)S(1)} %collective-permute-done.17.rest_2_), channel_id=1, source_target_pairs={{0,16},{4,12},{8,24},{12,4},{16,0},{20,28},{24,8},{28,20},{1,17},{... | collective-permute-start | bytes 1327112 | tf_op jit(solution)/shard_map/ppermute | solution.py:390
  59.7 8.9 %collective-permute-start.11 = (bf16[3,48,1152]{2,1,0:T(8,128)(2,1)}, bf16[3,48,1152]{2,1,0:T(8,128)(2,1)S(1)}, u32[]{:S(2)}, u32[]{:S(2)}) collective-permute-start(bf16[3,48,1152]{2,1,0:T(8,128)(2,1)} %collective-permute-done.7.rest_2_), channel_id=1, source_target_pairs={{0,4},{4,0},{8,12},{12,8},{16,20},{20,16},{24,28},{28,24},{1,5},{5... | collective-permute-start | bytes 995336 | tf_op jit(solution)/shard_map/ppermute | solution.py:390
  62.8 7.2 %collective-permute-start.8 = (bf16[3,48,1152]{2,1,0:T(8,128)(2,1)}, bf16[3,48,1152]{2,1,0:T(8,128)(2,1)S(1)}, u32[]{:S(2)}, u32[]{:S(2)}) collective-permute-start(bf16[3,48,1152]{2,1,0:T(8,128)(2,1)} %collective-permute-done.7.rest_2_), channel_id=1, source_target_pairs={{0,16},{4,12},{8,24},{12,4},{16,0},{20,28},{24,8},{28,20},{1,17},{... | collective-permute-start | bytes 995336 | tf_op jit(solution)/shard_map/ppermute | solution.py:390
  65.6 9.0 %collective-permute-start.21 = (bf16[3,48,1536]{2,1,0:T(8,128)(2,1)S(1)}, bf16[3,48,1536]{2,1,0:T(8,128)(2,1)S(1)}, u32[]{:S(2)}, u32[]{:S(2)}) collective-permute-start(bf16[3,48,1536]{2,1,0:T(8,128)(2,1)S(1)} %collective-permute-done.17.rest_2_), channel_id=1, source_target_pairs={{0,4},{4,0},{8,12},{12,8},{16,20},{20,16},{24,28},{28,24},{1,5},{5... | collective-permute-start | bytes 1327112 | tf_op jit(solution)/shard_map/ppermute | solution.py:390
  72.9 16.7 %collective-permute-start.22 = (bf16[3,48,1536]{2,1,0:T(8,128)(2,1)S(1)}, bf16[3,48,1536]{2,1,0:T(8,128)(2,1)S(1)}, u32[]{:S(2)}, u32[]{:S(2)}) collective-permute-start(bf16[3,48,1536]{2,1,0:T(8,128)(2,1)S(1)} %collective-permute-done.18.rest_3_), channel_id=1, source_target_pairs={{0,4},{4,0},{8,12},{12,8},{16,20},{20,16},{24,28},{28,24},{1,5},{5... | collective-permute-start | bytes 1327112 | tf_op jit(solution)/shard_map/ppermute | solution.py:390
  73.1 20.0 %collective-permute-start.29 = (bf16[3,80,384]{2,1,0:T(8,128)(2,1)}, bf16[3,80,384]{2,1,0:T(8,128)(2,1)S(1)}, u32[]{:S(2)}, u32[]{:S(2)}) collective-permute-start(bf16[3,80,384]{2,1,0:T(8,128)(2,1)} %pad_maximum_fusion.2.rest_0_), channel_id=1, source_target_pairs={{0,4},{4,0},{8,12},{12,8},{16,20},{20,16},{24,28},{28,24},{1,5},{5... | collective-permute-start | bytes 552968 | tf_op jit(solution)/shard_map/ppermute | solution.py:390
  74.2 18.9 %collective-permute-start.31 = (bf16[3,80,384]{2,1,0:T(8,128)(2,1)S(1)}, bf16[3,80,384]{2,1,0:T(8,128)(2,1)S(1)}, u32[]{:S(2)}, u32[]{:S(2)}) collective-permute-start(bf16[3,80,384]{2,1,0:T(8,128)(2,1)S(1)} %collective-permute-done.27.rest_2_), channel_id=1, source_target_pairs={{0,4},{4,0},{8,12},{12,8},{16,20},{20,16},{24,28},{28,24},{1,5},{5... | collective-permute-start | bytes 552968 | tf_op jit(solution)/shard_map/ppermute | solution.py:390
  74.6 18.6 %collective-permute-start.30 = (bf16[3,80,384]{2,1,0:T(8,128)(2,1)}, bf16[3,80,384]{2,1,0:T(8,128)(2,1)S(1)}, u32[]{:S(2)}, u32[]{:S(2)}) collective-permute-start(bf16[3,80,384]{2,1,0:T(8,128)(2,1)} %collective-permute-done.26.rest_1_), channel_id=1, source_target_pairs={{0,4},{4,0},{8,12},{12,8},{16,20},{20,16},{24,28},{28,24},{1,5},{5... | collective-permute-start | bytes 552968 | tf_op jit(solution)/shard_map/ppermute | solution.py:390
  74.7 18.4 %collective-permute-start.32 = (bf16[3,80,384]{2,1,0:T(8,128)(2,1)}, bf16[3,80,384]{2,1,0:T(8,128)(2,1)S(1)}, u32[]{:S(2)}, u32[]{:S(2)}) collective-permute-start(bf16[3,80,384]{2,1,0:T(8,128)(2,1)} %collective-permute-done.28.rest_3_), channel_id=1, source_target_pairs={{0,4},{4,0},{8,12},{12,8},{16,20},{20,16},{24,28},{28,24},{1,5},{5... | collective-permute-start | bytes 552968 | tf_op jit(solution)/shard_map/ppermute | solution.py:390
  114.7 7.4 %collective-permute-start.65 = (bf16[1152,384]{1,0:T(8,128)(2,1)S(1)}, bf16[1152,384]{1,0:T(8,128)(2,1)S(1)}, u32[]{:S(2)}, u32[]{:S(2)}) collective-permute-start(bf16[1152,384]{1,0:T(8,128)(2,1)S(1)} %grad_for_other.5), channel_id=1, source_target_pairs={{0,4},{4,0},{8,12},{12,8},{16,20},{20,16},{24,28},{28,24},{1,5},{5... | collective-permute-start | bytes 2654216 | tf_op jit(solution)/shard_map/ppermute | solution.py:390
  118.1 15.7 %collective-permute-start.40 = (bf16[4,96,1536]{2,1,0:T(8,128)(2,1)S(1)}, bf16[4,96,1536]{2,1,0:T(8,128)(2,1)S(1)}, u32[]{:S(2)}, u32[]{:S(2)}) collective-permute-start(bf16[4,96,1536]{2,1,0:T(8,128)(2,1)S(1)} %get-tuple-element.72), channel_id=1, source_target_pairs={{0,8},{4,20},{8,0},{12,28},{16,24},{20,4},{24,16},{28,12},{1,9},{5... | collective-permute-start | bytes 3538952 | tf_op jit(solution)/shard_map/ppermute | solution.py:390
  121.9 34.2 %collective-permute-start.53 = (bf16[4,96,1152]{2,1,0:T(8,128)(2,1)S(1)}, bf16[4,96,1152]{2,1,0:T(8,128)(2,1)S(1)}, u32[]{:S(2)}, u32[]{:S(2)}) collective-permute-start(bf16[4,96,1152]{2,1,0:T(8,128)(2,1)S(1)} %get-tuple-element.83), channel_id=1, source_target_pairs={{0,8},{4,20},{8,0},{12,28},{16,24},{20,4},{24,16},{28,12},{1,9},{5... | collective-permute-start | bytes 2654216 | tf_op jit(solution)/shard_map/ppermute | solution.py:390
  123.2 31.1 %collective-permute-start.66 = (bf16[4,144,384]{2,1,0:T(8,128)(2,1)S(1)}, bf16[4,144,384]{2,1,0:T(8,128)(2,1)S(1)}, u32[]{:S(2)}, u32[]{:S(2)}) collective-permute-start(bf16[4,144,384]{2,1,0:T(8,128)(2,1)S(1)} %get-tuple-element.91), channel_id=1, source_target_pairs={{0,8},{4,20},{8,0},{12,28},{16,24},{20,4},{24,16},{28,12},{1,9},{5... | collective-permute-start | bytes 1327112 | tf_op jit(solution)/shard_map/ppermute | solution.py:390
  134.6 36.8 %collective-permute-start.41 = (bf16[4,48,1536]{2,1,0:T(8,128)(2,1)S(1)}, bf16[4,48,1536]{2,1,0:T(8,128)(2,1)S(1)}, u32[]{:S(2)}, u32[]{:S(2)}) collective-permute-start(bf16[4,48,1536]{2,1,0:T(8,128)(2,1)S(1)} %get-tuple-element.74), channel_id=1, source_target_pairs={{0,16},{4,12},{8,24},{12,4},{16,0},{20,28},{24,8},{28,20},{1,17},{... | collective-permute-start | bytes 1769480 | tf_op jit(solution)/shard_map/ppermute | solution.py:390
  135.7 21.7 %collective-permute-start.33 = (f32[2,768]{1,0:T(2,128)S(1)}, f32[2,768]{1,0:T(2,128)S(1)}, u32[]{:S(2)}, u32[]{:S(2)}) collective-permute-start(f32[2,768]{1,0:T(2,128)S(1)} %pad_maximum_fusion.8), channel_id=1, source_target_pairs={{0,4},{4,0},{8,12},{12,8},{16,20},{20,16},{24,28},{28,24},{1,5},{5... | collective-permute-start | bytes 18440 | tf_op jit(solution)/shard_map/ppermute | solution.py:390
  155.0 11.8 %collective-permute-start.67 = (bf16[4,80,384]{2,1,0:T(8,128)(2,1)S(1)}, bf16[4,80,384]{2,1,0:T(8,128)(2,1)S(1)}, u32[]{:S(2)}, u32[]{:S(2)}) collective-permute-start(bf16[4,80,384]{2,1,0:T(8,128)(2,1)S(1)} %get-tuple-element.93), channel_id=1, source_target_pairs={{0,16},{4,12},{8,24},{12,4},{16,0},{20,28},{24,8},{28,20},{1,17},{... | collective-permute-start | bytes 737288 | tf_op jit(solution)/shard_map/ppermute | solution.py:390
  156.8 23.8 %collective-permute-start.54 = (bf16[4,48,1152]{2,1,0:T(8,128)(2,1)S(1)}, bf16[4,48,1152]{2,1,0:T(8,128)(2,1)S(1)}, u32[]{:S(2)}, u32[]{:S(2)}) collective-permute-start(bf16[4,48,1152]{2,1,0:T(8,128)(2,1)S(1)} %get-tuple-element.85), channel_id=1, source_target_pairs={{0,16},{4,12},{8,24},{12,4},{16,0},{20,28},{24,8},{28,20},{1,17},{... | collective-permute-start | bytes 1327112 | tf_op jit(solution)/shard_map/ppermute | solution.py:390
  157.4 7.9 %collective-permute-start.34 = (f32[2,768]{1,0:T(2,128)S(1)}, f32[2,768]{1,0:T(2,128)S(1)}, u32[]{:S(2)}, u32[]{:S(2)}) collective-permute-start(f32[2,768]{1,0:T(2,128)S(1)} %fusion.3), channel_id=1, source_target_pairs={{0,8},{4,12},{8,0},{12,4},{16,24},{20,28},{24,16},{28,20},{1,9},{5... | collective-permute-start | bytes 18440 | tf_op jit(solution)/shard_map/ppermute | solution.py:390
  167.5 9.6 %collective-permute-start.68 = (bf16[80,384]{1,0:T(8,128)(2,1)S(1)}, bf16[80,384]{1,0:T(8,128)(2,1)S(1)}, u32[]{:S(2)}, u32[]{:S(2)}) collective-permute-start(bf16[80,384]{1,0:T(8,128)(2,1)S(1)} %get-tuple-element.95), channel_id=1, source_target_pairs={{0,1},{1,2},{2,3},{3,0},{4,5},{5,6},{6,7},{7,4},{8,9},{9,10},{10,1... | collective-permute-start | bytes 184328 | tf_op jit(solution)/shard_map/ppermute | solution.py:393
  169.7 7.4 %collective-permute-start.69 = (bf16[80,384]{1,0:T(8,128)(2,1)S(1)}, bf16[80,384]{1,0:T(8,128)(2,1)S(1)}, u32[]{:S(2)}, u32[]{:S(2)}) collective-permute-start(bf16[80,384]{1,0:T(8,128)(2,1)S(1)} %get-tuple-element.96), channel_id=1, source_target_pairs={{0,2},{1,3},{2,0},{3,1},{4,6},{5,7},{6,4},{7,5},{8,10},{9,11},{10,... | collective-permute-start | bytes 184328 | tf_op jit(solution)/shard_map/ppermute | solution.py:393
  178.2 12.4 %collective-permute-start.43 = (bf16[48,1536]{1,0:T(8,128)(2,1)S(1)}, bf16[48,1536]{1,0:T(8,128)(2,1)S(1)}, u32[]{:S(2)}, u32[]{:S(2)}) collective-permute-start(bf16[48,1536]{1,0:T(8,128)(2,1)S(1)} %get-tuple-element.77), channel_id=1, source_target_pairs={{0,2},{1,3},{2,0},{3,1},{4,6},{5,7},{6,4},{7,5},{8,10},{9,11},{10,... | collective-permute-start | bytes 442376 | tf_op jit(solution)/shard_map/ppermute | solution.py:393
  180.7 15.8 %collective-permute-start.44 = (bf16[48,1536]{1,0:T(8,128)(2,1)S(1)}, bf16[48,1536]{1,0:T(8,128)(2,1)S(1)}, u32[]{:S(2)}, u32[]{:S(2)}) collective-permute-start(bf16[48,1536]{1,0:T(8,128)(2,1)S(1)} %get-tuple-element.78), channel_id=1, source_target_pairs={{0,3},{1,0},{2,1},{3,2},{4,7},{5,4},{6,5},{7,6},{8,11},{9,8},{10,9... | collective-permute-start | bytes 442376 | tf_op jit(solution)/shard_map/ppermute | solution.py:393
  181.4 15.1 %collective-permute-start.72 = (bf16[80,384]{1,0:T(8,128)(2,1)S(1)}, bf16[80,384]{1,0:T(8,128)(2,1)S(1)}, u32[]{:S(2)}, u32[]{:S(2)}) collective-permute-start(bf16[80,384]{1,0:T(8,128)(2,1)S(1)} %add_convert_fusion.2.refs_0_), channel_id=1, source_target_pairs={{0,8},{4,20},{8,0},{12,28},{16,24},{20,4},{24,16},{28,12},{1,9},{5... | collective-permute-start | bytes 184328 | tf_op jit(solution)/shard_map/ppermute | solution.py:390
  181.7 17.1 %collective-permute-start.71 = (bf16[80,384]{1,0:T(8,128)(2,1)S(1)}, bf16[80,384]{1,0:T(8,128)(2,1)S(1)}, u32[]{:S(2)}, u32[]{:S(2)}) collective-permute-start(bf16[80,384]{1,0:T(8,128)(2,1)S(1)} %add_convert_fusion.2.refs_0_), channel_id=1, source_target_pairs={{0,16},{4,12},{8,24},{12,4},{16,0},{20,28},{24,8},{28,20},{1,17},{... | collective-permute-start | bytes 184328 | tf_op jit(solution)/shard_map/ppermute | solution.py:390
  182.8 16.0 %collective-permute-start.55 = (bf16[48,1152]{1,0:T(8,128)(2,1)S(1)}, bf16[48,1152]{1,0:T(8,128)(2,1)S(1)}, u32[]{:S(2)}, u32[]{:S(2)}) collective-permute-start(bf16[48,1152]{1,0:T(8,128)(2,1)S(1)} %get-tuple-element.87), channel_id=1, source_target_pairs={{0,1},{1,2},{2,3},{3,0},{4,5},{5,6},{6,7},{7,4},{8,9},{9,10},{10,1... | collective-permute-start | bytes 331784 | tf_op jit(solution)/shard_map/ppermute | solution.py:393
  190.7 9.7 %collective-permute-start.56 = (bf16[48,1152]{1,0:T(8,128)(2,1)S(1)}, bf16[48,1152]{1,0:T(8,128)(2,1)S(1)}, u32[]{:S(2)}, u32[]{:S(2)}) collective-permute-start(bf16[48,1152]{1,0:T(8,128)(2,1)S(1)} %get-tuple-element.88), channel_id=1, source_target_pairs={{0,2},{1,3},{2,0},{3,1},{4,6},{5,7},{6,4},{7,5},{8,10},{9,11},{10,... | collective-permute-start | bytes 331784 | tf_op jit(solution)/shard_map/ppermute | solution.py:393
  198.8 7.0 %collective-permute-start.75 = (bf16[80,384]{1,0:T(8,128)(2,1)S(1)}, bf16[80,384]{1,0:T(8,128)(2,1)S(1)}, u32[]{:S(2)}, u32[]{:S(2)}) collective-permute-start(bf16[80,384]{1,0:T(8,128)(2,1)S(1)} %collective-permute-done.71.refs_1_), channel_id=1, source_target_pairs={{0,4},{4,0},{8,12},{12,8},{16,20},{20,16},{24,28},{28,24},{1,5},{5... | collective-permute-start | bytes 184328 | tf_op jit(solution)/shard_map/ppermute | solution.py:390
  198.9 8.1 %collective-permute-start.73 = (bf16[80,384]{1,0:T(8,128)(2,1)S(1)}, bf16[80,384]{1,0:T(8,128)(2,1)S(1)}, u32[]{:S(2)}, u32[]{:S(2)}) collective-permute-start(bf16[80,384]{1,0:T(8,128)(2,1)S(1)} %collective-permute-done.71.refs_1_), channel_id=1, source_target_pairs={{0,8},{4,20},{8,0},{12,28},{16,24},{20,4},{24,16},{28,12},{1,9},{5... | collective-permute-start | bytes 184328 | tf_op jit(solution)/shard_map/ppermute | solution.py:390
  202.2 7.2 %collective-permute-start.45 = (bf16[48,1536]{1,0:T(8,128)(2,1)S(1)}, bf16[48,1536]{1,0:T(8,128)(2,1)S(1)}, u32[]{:S(2)}, u32[]{:S(2)}) collective-permute-start(bf16[48,1536]{1,0:T(8,128)(2,1)S(1)} %add_convert_fusion.refs_0_), channel_id=1, source_target_pairs={{0,16},{4,12},{8,24},{12,4},{16,0},{20,28},{24,8},{28,20},{1,17},{... | collective-permute-start | bytes 442376 | tf_op jit(solution)/shard_map/ppermute | solution.py:390
  203.0 7.6 %collective-permute-start.58 = (bf16[48,1152]{1,0:T(8,128)(2,1)S(1)}, bf16[48,1152]{1,0:T(8,128)(2,1)S(1)}, u32[]{:S(2)}, u32[]{:S(2)}) collective-permute-start(bf16[48,1152]{1,0:T(8,128)(2,1)S(1)} %add_convert_fusion.1.refs_0_), channel_id=1, source_target_pairs={{0,16},{4,12},{8,24},{12,4},{16,0},{20,28},{24,8},{28,20},{1,17},{... | collective-permute-start | bytes 331784 | tf_op jit(solution)/shard_map/ppermute | solution.py:390
  203.8 7.7 %collective-permute-start.61 = (bf16[48,1152]{1,0:T(8,128)(2,1)S(1)}, bf16[48,1152]{1,0:T(8,128)(2,1)S(1)}, u32[]{:S(2)}, u32[]{:S(2)}) collective-permute-start(bf16[48,1152]{1,0:T(8,128)(2,1)S(1)} %add_convert_fusion.1.refs_0_), channel_id=1, source_target_pairs={{0,4},{4,0},{8,12},{12,8},{16,20},{20,16},{24,28},{28,24},{1,5},{5... | collective-permute-start | bytes 331784 | tf_op jit(solution)/shard_map/ppermute | solution.py:390
  209.2 8.8 %collective-permute-start.46 = (bf16[48,1536]{1,0:T(8,128)(2,1)S(1)}, bf16[48,1536]{1,0:T(8,128)(2,1)S(1)}, u32[]{:S(2)}, u32[]{:S(2)}) collective-permute-start(bf16[48,1536]{1,0:T(8,128)(2,1)S(1)} %add_convert_fusion.refs_0_), channel_id=1, source_target_pairs={{0,8},{4,20},{8,0},{12,28},{16,24},{20,4},{24,16},{28,12},{1,9},{5... | collective-permute-start | bytes 442376 | tf_op jit(solution)/shard_map/ppermute | solution.py:390
  209.4 8.6 %collective-permute-start.47 = (bf16[48,1536]{1,0:T(8,128)(2,1)S(1)}, bf16[48,1536]{1,0:T(8,128)(2,1)S(1)}, u32[]{:S(2)}, u32[]{:S(2)}) collective-permute-start(bf16[48,1536]{1,0:T(8,128)(2,1)S(1)} %collective-permute-done.45.refs_1_), channel_id=1, source_target_pairs={{0,8},{4,20},{8,0},{12,28},{16,24},{20,4},{24,16},{28,12},{1,9},{5... | collective-permute-start | bytes 442376 | tf_op jit(solution)/shard_map/ppermute | solution.py:390
  (60 other events, 539.1 us)

commit v2 on v1

v2 whole, which is shorter than its diff:
```python
import functools

import jax
import jax.numpy as jnp
from jax import lax
from jax.experimental import pallas as pl
from jax.experimental.pallas import tpu as pltpu
from jax.sharding import PartitionSpec as P

HEADS = 12
HEAD_DIM = 64
FF = 1152
D = 768
TILE = 384
PAIR = 128
ROWS = 48
QKV = 3 * D // 2
IN_OUT = FF + D // 2
DOWN = 640
MLP = IN_OUT + DOWN

norm_eps = 1e-05
rope_base = 160000.0
head_scale = HEAD_DIM ** (-0.5)
f32 = jnp.float32
bf16 = jnp.bfloat16

VMEM = pl.BlockSpec(memory_space=pltpu.VMEM)
SMEM = pl.BlockSpec(memory_space=pltpu.SMEM)
ANY = pl.BlockSpec(memory_space=pl.ANY)


def run(body, name, outs, place, ins, scratch=(), after=()):
    count, extra = len(ins), len(after)

    def inner(place, *refs):
        body(place, *refs[:count], *refs[count + extra :])

    return pl.pallas_call(
        inner,
        out_shape=outs,
        in_specs=[SMEM] + [VMEM] * count + [ANY] * extra,
        out_specs=[VMEM] * len(outs),
        scratch_shapes=list(scratch),
        compiler_params=pltpu.CompilerParams(vmem_limit_bytes=44 * 1024 * 1024),
        cost_estimate=pl.CostEstimate(flops=0, bytes_accessed=0, transcendentals=0),
        name=name,
    )(place, *ins, *after)


def shape(dims, dtype=bf16):
    return jax.ShapeDtypeStruct(dims, dtype)


def dot(a, b):
    return lax.dot_general(a, b, (((1,), (0,)), ((), ())), preferred_element_type=f32)


def dot_bt(a, b):
    return lax.dot_general(a, b, (((1,), (1,)), ((), ())), preferred_element_type=f32)


def dot_at(a, b):
    return lax.dot_general(a, b, (((0,), (0,)), ((), ())), preferred_element_type=f32)


def token_positions(segment):
    length = segment.shape[0]
    index = jnp.arange(length, dtype=jnp.int32)
    before = jnp.concatenate([jnp.full((1,), -1, jnp.int32), segment[:-1]])
    first = lax.cummax(jnp.where(segment != before, index, 0), axis=0)
    return index - first


def rotary_tables(position):
    half_dim = HEAD_DIM // 2
    inverse = rope_base ** (-(jnp.arange(half_dim, dtype=f32) * 2.0 / HEAD_DIM))
    angles = position.astype(f32)[:, None] * inverse[None, :]
    cosine, sine = jnp.cos(angles), jnp.sin(angles)
    return (
        jnp.concatenate([cosine] * 4, axis=1),
        jnp.concatenate([-sine, sine, -sine, sine], axis=1),
    )


def rows(start, size, step=16):
    return pl.ds(pl.multiple_of(start, step), size)


def columns(start, size):
    return pl.ds(pl.multiple_of(start, 128), size)


def piece_rows(place, flip_high, flip_low, other):
    hb, lb = place[1], place[2]
    return (lb if other else hb) ^ flip_high, (hb if other else lb) ^ flip_low


def each_part(groups, place, parts):
    for index, part in enumerate(parts):
        flip_low, other = index & 1, index >> 1
        for flip_high in range(2):
            hi, lo = piece_rows(place, flip_high, flip_low, other)
            for k in range(1, groups):
                owner = lax.rem(place[0] + groups - k, groups)
                yield part, flip_high, k - 1, owner, hi, lo, place[3] ^ other


def assemble(groups, place, parts, own, full, width, start):
    shard = own.shape[0]
    full[rows(place[0] * shard, shard), :] = own[...]
    for part, i, j, owner, hi, lo, half in each_part(groups, place, parts):
        at = owner * shard + hi * 2 * ROWS + lo * ROWS
        full[rows(at, ROWS), columns(half * width, width)] = part[i, j, :, start : start + width]


def packed_blocks():
    for i in range(5):
        for j in range(3):
            n = 3 * i + j
            yield i, 16 * i, PAIR * j, 16 * (n % 3), PAIR * (n // 3)


def norm_parts(values):
    centred = values - jnp.mean(values, axis=1, keepdims=True)
    inverse = lax.rsqrt(jnp.mean(centred * centred, axis=1, keepdims=True) + norm_eps)
    return centred * inverse, inverse


def norm_back(upstream, normed, inverse, gain):
    scaled = upstream * gain
    inner = (
        scaled
        - jnp.mean(scaled, axis=1, keepdims=True)
        - normed * jnp.mean(scaled * normed, axis=1, keepdims=True)
    )
    return inverse * inner


def swap_halves(u):
    lane = lax.broadcasted_iota(jnp.int32, u.shape, 1)
    return jnp.where(lane % HEAD_DIM < HEAD_DIM // 2, pltpu.roll(u, PAIR - 32, 1), pltpu.roll(u, 32, 1))


def copy_half(place, whole, half):
    width = whole.shape[1] // 2
    half[...] = whole[:, columns((1 - place[3]) * width, width)]


def head_masks():
    lane = lax.broadcasted_iota(jnp.int32, (1, PAIR), 1)
    first = (lane < HEAD_DIM).astype(f32)
    return first.astype(bf16), (1.0 - first).astype(bf16)


def attn_forward(groups, place, gains, cosine, sine, seg_col, seg_row, tok, own, *rest):
    parts, (attn_in, qkv, mixed, lse, w_full) = rest[:4], rest[4:]
    assemble(groups, place, parts, own, w_full, QKV, 0)
    normed, _ = norm_parts(tok[...].astype(f32))
    attn_in[...] = (normed * gains[0:1, :]).astype(bf16)

    def turned(j, _):
        at = columns(j * TILE, TILE)
        raw = dot(attn_in[...], w_full[:, at])
        turned_parts = []
        for i in range(TILE // PAIR):
            u = raw[:, i * PAIR : (i + 1) * PAIR]
            turned_parts.append(u * cosine[...] + swap_halves(u) * sine[...])
        qkv[:, at] = jnp.concatenate(turned_parts, axis=1).astype(bf16)
        return 0

    lax.fori_loop(0, 4, turned, 0)

    def plain(j, _):
        at = columns(j * TILE, TILE)
        qkv[:, at] = dot(attn_in[...], w_full[:, at]).astype(bf16)
        return 0

    lax.fori_loop(4, 6, plain, 0)
    masks = head_masks()
    same = seg_col[...] == seg_row[...]
    length = tok.shape[0]
    lane = lax.broadcasted_iota(jnp.int32, (length, PAIR), 1)

    def pair(j, kept):
        q = qkv[:, columns(j * PAIR, PAIR)]
        k = qkv[:, columns(D + j * PAIR, PAIR)]
        v = qkv[:, columns(2 * D + j * PAIR, PAIR)]
        made = []
        for a in range(2):
            scores = dot_bt(q * masks[a], k) * head_scale
            scores = jnp.where(same, scores, -1e30)
            top = jnp.max(scores, axis=1, keepdims=True)
            e = jnp.exp(scores - top)
            total = jnp.sum(e, axis=1, keepdims=True)
            probs = (e * (1.0 / total)).astype(bf16)
            made.append(dot(probs, v))
            kept = jnp.where(lane == 2 * j + a, top + jnp.log(total), kept)
        mixed[:, columns(j * PAIR, PAIR)] = jnp.where(lane < HEAD_DIM, made[0], made[1]).astype(bf16)
        return kept

    lse[...] = lax.fori_loop(0, HEADS // 2, pair, jnp.zeros((length, PAIR), f32), unroll=2)


def feed_forward(groups, place, gains, mixed, attn_in, tok, grad_out, own_in, own_out, own_down, *rest):
    parts, rest = rest[:4], rest[4:]
    output, middle_grad, mixed_grad, branch_grad, hidden, mlp_in, gate_up_grad, for_other = rest[:8]
    w_in, w_out, w_down, middle, act, slope, total = rest[8:]
    assemble(groups, place, parts, own_out, w_out, D // 2, FF)
    assemble(groups, place, parts, own_in, w_in, FF, 0)
    shard = own_down.shape[0]
    w_down[rows(place[0] * shard, shard), :] = own_down[...]
    for part, i, j, owner, hi, lo, half in each_part(groups, place, parts):
        base = owner * shard + hi * 144 + lo * 64
        for _, r, c, pr, pc in packed_blocks():
            block = part[i, j, pr : pr + 16, IN_OUT + pc : IN_OUT + pc + PAIR]
            w_down[rows(base + r, 16), columns(half * (D // 2) + c, PAIR)] = block

    for j in range(2):
        at = slice(j * TILE, (j + 1) * TILE)
        middle[:, at] = tok[:, at].astype(f32) + dot(mixed[...], w_out[:, at])
    normed, inverse = norm_parts(middle[...])
    mlp_in[...] = (normed * gains[1:2, :]).astype(bf16)

    def forward(j, _):
        at = columns(j * TILE, TILE)
        u = dot(mlp_in[...], w_in[:, at])
        gate = dot(mlp_in[...], w_in[:, columns(FF + j * TILE, TILE)])
        cdf = 0.5 + 0.5 * lax.erf(u * 0.7071067811865476)
        a = u * cdf
        act[:, at] = a
        slope[:, at] = gate * (cdf + u * (0.3989422804014327 * jnp.exp(-0.5 * u * u)))
        hidden[:, at] = (a * gate).astype(bf16)
        return 0

    lax.fori_loop(0, FF // TILE, forward, 0)

    def backward(j, _):
        at = columns(j * TILE, TILE)
        hidden_grad = dot_bt(grad_out[...], w_down[rows(j * TILE, TILE), :])
        gate_up_grad[:, at] = (hidden_grad * slope[:, at]).astype(bf16)
        gate_up_grad[:, columns(FF + j * TILE, TILE)] = (hidden_grad * act[:, at]).astype(bf16)
        return 0

    lax.fori_loop(0, FF // TILE, backward, 0)
    for j in range(2):
        at = slice(j * TILE, (j + 1) * TILE)
        output[:, at] = (middle[:, at] + dot(hidden[...], w_down[:, at])).astype(bf16)

    def step(j, _):
        total[:, columns(j * 256, 256)] = dot_bt(gate_up_grad[...], w_in[rows(j * 256, 256), :])
        return 0

    lax.fori_loop(0, D // 256, step, 0)
    normed, inverse = norm_parts(middle[...])
    part = norm_back(total[...], normed, inverse, gains[1:2, :])
    whole = grad_out[...].astype(f32) + part
    middle_grad[...] = whole
    branch_grad[...] = whole.astype(bf16)

    def back(j, _):
        mixed_grad[:, columns(j * 256, 256)] = dot_bt(
            branch_grad[...], w_out[rows(j * 256, 256), :]
        ).astype(bf16)
        return 0

    lax.fori_loop(0, D // 256, back, 0)
    start = 0
    for whole in (hidden, mlp_in, mixed, attn_in):
        for_other[:, start : start + whole.shape[1]] = whole[...]
        start += whole.shape[1]
    for whole in (grad_out, gate_up_grad, branch_grad):
        width = whole.shape[1] // 2
        for_other[:, start : start + width] = whole[:, columns((1 - place[3]) * width, width)]
        start += width


HIDDEN, MLP_IN, MIXED, ATTN_IN, UPSTREAM, GATE_UP, BRANCH, SENT = (
    0, FF, FF + D, FF + 2 * D, FF + 3 * D, FF + 3 * D + D // 2, 2 * FF + 3 * D + D // 2, 2 * FF + 4 * D
)


def attn_backward(place, qkv, lse, mixed_grad, cosine, sine, seg_col, seg_row, qkv_grad, for_other):
    masks = head_masks()
    same = seg_col[...] == seg_row[...]
    length = qkv.shape[0]
    lane = lax.broadcasted_iota(jnp.int32, (length, PAIR), 1)

    def pair(j, _):
        q = qkv[:, columns(j * PAIR, PAIR)]
        k = qkv[:, columns(D + j * PAIR, PAIR)]
        v = qkv[:, columns(2 * D + j * PAIR, PAIR)]
        upstream = mixed_grad[:, columns(j * PAIR, PAIR)]
        made = []
        for a in range(2):
            scores = dot_bt(q * masks[a], k) * head_scale
            log_total = jnp.sum(jnp.where(lane == 2 * j + a, lse[...], 0.0), axis=1, keepdims=True)
            probs = jnp.where(same, jnp.exp(scores - log_total), 0.0)
            prob_grad = dot_bt(upstream * masks[a], v)
            delta = jnp.sum(probs * prob_grad, axis=1, keepdims=True)
            score_grad = (probs * (prob_grad - delta)).astype(bf16)
            made.append(
                (
                    dot(score_grad, k),
                    dot_at(score_grad, q),
                    dot_at(probs.astype(bf16), upstream),
                )
            )
        first = lane < HEAD_DIM
        for i in range(2):
            u = jnp.where(first, made[0][i], made[1][i]) * head_scale
            u = u * cosine[...] - swap_halves(u) * sine[...]
            qkv_grad[:, columns(i * D + j * PAIR, PAIR)] = u.astype(bf16)
        qkv_grad[:, columns(2 * D + j * PAIR, PAIR)] = jnp.where(first, made[0][2], made[1][2]).astype(bf16)
        return 0

    lax.fori_loop(0, HEADS // 2, pair, 0, unroll=2)
    copy_half(place, qkv_grad, for_other)


def attn_in_backward(groups, place, qkv_grad, middle_grad, gains, tok, own, *rest):
    parts, (tokens_grad, w_full, total) = rest[:4], rest[4:]
    assemble(groups, place, parts, own, w_full, QKV, 0)

    def step(j, _):
        total[:, columns(j * 256, 256)] = dot_bt(qkv_grad[...], w_full[rows(j * 256, 256), :])
        return 0

    lax.fori_loop(0, D // 256, step, 0)
    normed, inverse = norm_parts(tok[...].astype(f32))
    part = norm_back(total[...], normed, inverse, gains[0:1, :])
    tokens_grad[...] = (middle_grad[...] + part).astype(bf16)


def grad_for_self(plan, groups, place, *refs):
    ins, (keep, send, natural, ordered, right) = refs[:-5], refs[-5:]
    hb, core = place[1], place[3]
    high = keep.shape[1]
    cut = groups * high
    start = 0
    for x, (x_from, x_at), dy, (dy_from, dy_at) in plan:
        x, x_other, dy, dy_other = ins[x], ins[x_from], ins[dy], ins[dy_from]
        length, depth = x.shape
        half = dy.shape[1] // 2
        natural[:, :length] = x[...].T
        natural[:, length:] = x_other[:, x_at : x_at + depth].T
        for side in range(2):
            for g in range(groups):
                at = g * 2 * high + (hb ^ side) * high
                ordered[side * cut + g * high : side * cut + (g + 1) * high, :] = natural[rows(at, high), :]
        right[:length, :half] = dy[:, columns(core * half, half)]
        right[length:, :half] = dy_other[:, dy_at : dy_at + half]

        def step(t, _, start=start):
            made = dot(ordered[...], right[:, columns(t * TILE, TILE)])
            at = columns(start + t * TILE, TILE)
            for side, target in enumerate((keep, send)):
                for g in range(groups):
                    target[g, :, at] = made[side * cut + g * high : side * cut + (g + 1) * high, :].astype(bf16)
            return 0

        lax.fori_loop(0, half // TILE, step, 0)
        start += half


def split_mlp(groups, place, down, down_got, rest, rest_got, keep, send):
    lb = place[2]
    for side, target in enumerate((keep, send)):
        low, low_down = rows((lb ^ side) * ROWS, ROWS), rows((lb ^ side) * 64, 80)
        for g in range(groups):
            target[g, :, :IN_OUT] = (rest[g, low, :].astype(f32) + rest_got[g, low, :].astype(f32)).astype(bf16)
            made = (down[g, low_down, :].astype(f32) + down_got[g, low_down, :].astype(f32)).astype(bf16)
            for _, r, c, pr, pc in packed_blocks():
                target[g, pr : pr + 16, IN_OUT + pc : IN_OUT + pc + PAIR] = made[r : r + 16, c : c + PAIR]


def split_qkv(groups, place, mine, got, keep, send):
    for side, target in enumerate((keep, send)):
        low = rows((place[2] ^ side) * ROWS, ROWS)
        for g in range(groups):
            target[g] = (mine[g, low, :].astype(f32) + got[g, low, :].astype(f32)).astype(bf16)


def add_owners(groups, place, mine, got, *outs):
    for k in range(groups):
        g = lax.rem(place[0] + k, groups)
        outs[k][...] = (mine[g].astype(f32) + got[g].astype(f32)).astype(outs[k].dtype)


def sum_pieces(groups, place, mine, *refs):
    total = mine[...]
    for ref in refs[:-1]:
        total = total + ref[...].astype(f32)
    refs[-1][...] = total.astype(refs[-1].dtype)


def gain_grad(grad, weight, gain):
    return jnp.sum(grad * weight.astype(f32), axis=1, keepdims=True) / gain


def place_mlp(place, gain, here, other, weight, in_grad, out_grad, down_grad, gain_out):
    for core, part in enumerate((here, other)):
        for flip_high in range(2):
            hi, lo = piece_rows(place, flip_high, 0, core)
            half = place[3] ^ core
            for flip_low in range(2):
                at = rows(hi * 2 * ROWS + (lo ^ flip_low) * ROWS, ROWS)
                piece = part[flip_high, flip_low]
                in_grad[at, columns(half * FF, FF)] = piece[:, :FF].astype(f32)
                out_grad[at, columns(half * (D // 2), D // 2)] = piece[:, FF:IN_OUT].astype(f32)
            one = part[flip_high, 0, :, IN_OUT:].astype(f32)
            two = part[flip_high, 1, :, IN_OUT:].astype(f32)
            low, up = jnp.where(lo == 0, one, two), jnp.where(lo == 0, two, one)
            for i, r, c, pr, pc in packed_blocks():
                at = columns(half * (D // 2) + c, PAIR)
                down_grad[rows(hi * 144 + r, 16), at] = low[pr : pr + 16, pc : pc + PAIR]
                if i > 0:
                    down_grad[rows(hi * 144 + 64 + r, 16), at] = up[pr : pr + 16, pc : pc + PAIR]
    gain_out[...] = gain_grad(in_grad[...], weight[...], gain[...])


def place_qkv(place, gain, here, other, weight, grad, gain_out):
    for core, part in enumerate((here, other)):
        for flip_high in range(2):
            for flip_low in range(2):
                hi, lo = piece_rows(place, flip_high, flip_low, core)
                at = rows(hi * 2 * ROWS + lo * ROWS, ROWS)
                grad[at, columns((place[3] ^ core) * QKV, QKV)] = part[flip_high, flip_low].astype(f32)
    gain_out[...] = gain_grad(grad[...], weight[...], gain[...])


def stack_pieces(count, place, *refs):
    for k, ref in enumerate(refs[:count]):
        start = 0
        for out in refs[count:]:
            width = out.shape[2]
            out[k] = ref[:, start : start + width]
            start += width


def join(place, near, got, out):
    out[0] = near[...]
    out[1] = got[...]


def make(mesh):
    groups, copies = mesh.shape["group"], mesh.shape["replica"]
    swap_core = [(i, i ^ 1) for i in range(copies)]
    swap_high = [(i, i ^ (4 if i & 1 else 2)) for i in range(copies)]
    swap_low = [(i, i ^ (2 if i & 1 else 4)) for i in range(copies)]
    far_same = [[j + 8 * m for m in range(copies // 8)] for j in range(8)]

    def across(a, perm):
        return lax.ppermute(a, "replica", perm)

    def shifted(a, k):
        return lax.ppermute(a, "group", [(i, (i + k) % groups) for i in range(groups)])

    def on_device(tokens, segment, g_attn, w_qkv, w_out, g_mlp, w_in, w_down, grad_out):
        length = tokens.shape[0]
        z = lax.axis_index("group")
        r = lax.axis_index("replica")
        core, two, four = r & 1, (r >> 1) & 1, (r >> 2) & 1
        hb = jnp.where(core == 1, four, two)
        lb = jnp.where(core == 1, two, four)
        place = jnp.stack([z, hb, lb, core]).astype(jnp.int32)

        def joined(near, got, after=()):
            return run(join, "join", [shape((2,) + near.shape)], place, [near, got], (), after)[0]

        def spread(a, after=()):
            here = joined(a, across(a, swap_high), after)
            low = across(here, swap_low)
            return [here, low, across(here, swap_core), across(low, swap_core)]

        def grad_self(ins, plan, high, after=()):
            depth = ins[plan[0][0]].shape[1]
            widths = [ins[dy].shape[1] // 2 for _, _, dy, _ in plan]
            turned = pltpu.VMEM((depth, 2 * length), bf16)
            keep, send = run(
                functools.partial(grad_for_self, plan, groups), "grad_for_self",
                [shape((groups, high, sum(widths)))] * 2, place, ins,
                [turned, turned, pltpu.VMEM((2 * length, max(widths)), bf16)], after,
            )
            return keep, across(send, swap_high)

        def owners(keep, got, after=()):
            dims = keep.shape[1:]
            mine, *others = run(
                functools.partial(add_owners, groups), "add_owners",
                [shape(dims, f32)] + [shape(dims)] * (groups - 1), place, [keep, got],
                (), after,
            )
            return mine, [shifted(t, k + 1) for k, t in enumerate(others)]

        def summed(mine, got, after=()):
            kind = bf16 if copies == 8 else f32
            (total,) = run(
                functools.partial(sum_pieces, groups), "sum_pieces", [shape(mine.shape, kind)], place,
                [mine] + list(got), (), after,
            )
            if copies > 8:
                total = lax.psum(total, "replica", axis_index_groups=far_same).astype(bf16)
            return total

        count = 2 * g_attn.shape[0] // PAIR
        own_gains = jnp.pad(jnp.concatenate([g_attn, g_mlp]).reshape(count, PAIR), ((0, ROWS - count), (0, 0)))

        def cut(w, at, size):
            half = w.shape[1] // 2
            return lax.dynamic_slice(w, (at, half * core), (size, half))

        quarter = 2 * ROWS * hb + ROWS * lb
        qkv_piece = jnp.concatenate([cut(w_qkv, quarter, ROWS), own_gains], axis=1)
        down = cut(w_down, 144 * hb + 64 * lb, 80).reshape(5, 16, 3, PAIR).transpose(2, 1, 0, 3).reshape(ROWS, DOWN)
        mlp_piece = jnp.concatenate([cut(w_in, quarter, ROWS), cut(w_out, quarter, ROWS), down], axis=1)
        cosine, sine = rotary_tables(token_positions(segment))
        seg_col, seg_row = segment[:, None], segment[None, :]
        qkv_stack, far_gains = run(
            functools.partial(stack_pieces, groups - 1), "stack_pieces", [shape((groups - 1, ROWS, QKV)), shape((groups - 1, ROWS, PAIR))], place,
            [shifted(qkv_piece, k) for k in range(1, groups)], (), [cosine, sine],
        )
        mlp_far = [shifted(mlp_piece, k) for k in range(1, groups)]
        qkv_parts = spread(qkv_stack, mlp_far[:1])
        (mlp_stack,) = run(
            functools.partial(stack_pieces, groups - 1), "stack_pieces", [shape((groups - 1, ROWS, MLP))], place,
            list(mlp_far), (), qkv_parts[1:3],
        )
        by_distance = jnp.concatenate([own_gains[None], far_gains])[:, :count]
        by_distance = by_distance.reshape(groups, 2, g_attn.shape[0]).astype(f32)
        gains = jnp.concatenate(
            [
                lax.dynamic_index_in_dim(by_distance, lax.rem(z + groups - g, groups), keepdims=False)
                for g in range(groups)
            ],
            axis=1,
        )

        rope = [cosine, sine, seg_col, seg_row]
        attn_in, qkv, mixed, lse = run(
            functools.partial(attn_forward, groups), "attn_forward",
            [shape((length, D)), shape((length, 3 * D)), shape((length, D)), shape((length, PAIR), f32)],
            place, [gains] + rope + [tokens, w_qkv] + qkv_parts,
            [pltpu.VMEM((D, 3 * D), bf16)], [mlp_stack],
        )
        mlp_parts = spread(mlp_stack, [mixed])
        output, middle_grad, mixed_grad, branch_grad, hidden, mlp_in, gate_up_grad, for_other = run(
            functools.partial(feed_forward, groups), "feed_forward",
            [
                shape((length, D)), shape((length, D), f32), shape((length, D)), shape((length, D)),
                shape((length, FF)), shape((length, D)), shape((length, 2 * FF)), shape((length, SENT)),
            ],
            place, [gains, mixed, attn_in, tokens, grad_out, w_in, w_out, w_down] + mlp_parts,
            [
                pltpu.VMEM((D, 2 * FF), bf16), pltpu.VMEM((D, D), bf16), pltpu.VMEM((FF, D), bf16),
                pltpu.VMEM((length, D), f32), pltpu.VMEM((length, FF), f32), pltpu.VMEM((length, FF), f32),
                pltpu.VMEM((length, D), f32),
            ],
        )
        from_other = across(for_other, swap_core)

        qkv_grad, qkv_send = run(
            attn_backward, "attn_backward", [shape((length, 3 * D)), shape((length, QKV))],
            place, [qkv, lse, mixed_grad] + rope,
        )
        qkv_other = across(qkv_send, swap_core)
        down_keep, down_got = grad_self(
            [hidden, grad_out, from_other], [(0, (2, HIDDEN), 1, (2, UPSTREAM))], 144, [qkv_send]
        )
        rest_keep, rest_got = grad_self(
            [mlp_in, gate_up_grad, mixed, branch_grad, from_other],
            [(0, (4, MLP_IN), 1, (4, GATE_UP)), (2, (4, MIXED), 3, (4, BRANCH))], 96, [down_keep],
        )
        qkv_keep, qkv_got = grad_self(
            [attn_in, qkv_grad, from_other, qkv_other], [(0, (2, ATTN_IN), 1, (3, 0))], 96, [rest_keep]
        )
        mlp_keep, mlp_send = run(
            functools.partial(split_mlp, groups), "split_mlp", [shape((groups, ROWS, MLP))] * 2, place,
            [down_keep, down_got, rest_keep, rest_got],
            (), [qkv_keep],
        )
        mlp_got = across(mlp_send, swap_low)
        (tokens_grad,) = run(
            functools.partial(attn_in_backward, groups), "attn_in_backward", [shape((length, D))],
            place, [qkv_grad, middle_grad, gains] + [tokens, w_qkv] + qkv_parts,
            [pltpu.VMEM((D, 3 * D), bf16), pltpu.VMEM((length, D), f32)], [mlp_keep],
        )
        qkv_keep, qkv_send = run(
            functools.partial(split_qkv, groups), "split_qkv", [shape((groups, ROWS, QKV))] * 2, place,
            [qkv_keep, qkv_got], (), [tokens_grad],
        )
        qkv_got = across(qkv_send, swap_low)
        mlp_mine, mlp_others = owners(mlp_keep, mlp_got, [qkv_keep])
        qkv_mine, qkv_others = owners(qkv_keep, qkv_got, [mlp_mine])
        mlp_sum = summed(mlp_mine, mlp_others, [qkv_mine])
        mlp_pair = joined(mlp_sum, across(mlp_sum, swap_low))
        qkv_sum = summed(qkv_mine, qkv_others, [mlp_pair])
        mlp_quarters = joined(mlp_pair, across(mlp_pair, swap_high), [qkv_sum])
        qkv_pair = joined(qkv_sum, across(qkv_sum, swap_low), [mlp_quarters])
        qkv_quarters = joined(qkv_pair, across(qkv_pair, swap_high))
        shard = w_in.shape[0]
        in_grad, out_grad, down_grad, gain_two_grad = run(
            place_mlp, "place_mlp",
            [shape((shard, 2 * FF), f32), shape((shard, D), f32), shape((w_down.shape[0], D), f32), shape((shard, 1), f32)],
            place, [g_mlp.astype(f32)[:, None], mlp_quarters, across(mlp_quarters, swap_core), w_in],
            (), [qkv_pair],
        )
        qkv_weight_grad, gain_one_grad = run(
            place_qkv, "place_qkv", [shape((shard, 3 * D), f32), shape((shard, 1), f32)], place,
            [g_attn.astype(f32)[:, None], qkv_quarters, across(qkv_quarters, swap_core), w_qkv],
            (), [in_grad],
        )
        return (
            output, tokens_grad, gain_one_grad[:, 0], qkv_weight_grad, out_grad, gain_two_grad[:, 0], in_grad, down_grad,
        )

    return on_device


def solution(mesh):
    both = ("replica", "group")
    in_specs = (
        P(both, None), P(both), P("group"), P("group", None), P("group", None),
        P("group"), P("group", None), P("group", None), P(both, None),
    )
    out_specs = (
        P(both, None), P(both, None), P("group"), P("group", None),
        P("group", None), P("group"), P("group", None), P("group", None),
    )
    return jax.shard_map(
        make(mesh), mesh=mesh, in_specs=in_specs, out_specs=out_specs, check_vma=False
    )
```

time: 226 us -> 211 us (0.934)
  starting transfers between devices: 84.3 us -> 30.6 us
  waiting for transfers between devices: 70 us -> 106 us
    ppermute x54 -> x21, starting transfers between devices: 54.8 us -> 19.8 us  [across(): return lax.ppermute(a, 'replica', perm)]
    ppermute x24 -> x12, starting transfers between devices: 29.5 us -> 10.8 us  [shifted(): lax.ppermute(a, 'group', [(i, (i + k) % groups) for i in range(groups)])]
    ppermute x54 -> x21, waiting for transfers between devices: 43.7 us -> 61.8 us  [across(): return lax.ppermute(a, 'replica', perm)]
    ppermute x24 -> x12, waiting for transfers between devices: 26.3 us -> 44.3 us  [shifted(): lax.ppermute(a, 'group', [(i, (i + k) % groups) for i in range(groups)])]
    unnamed x60 -> x57, local copies, waits for them, and re-layouts: 5 us -> 8.85 us
    pallas_call x21 -> x23, Pallas kernels: 53.2 us -> 53.7 us  [run(): pl.pallas_call(inner, out_shape=outs, in_specs=[SMEM] + [VMEM] * count +...]
  transfers between devices with their start and end apart: 78 -> 33, of which waited for: 20 -> 22; matrix products, arithmetic and copies ran while one was open for 4% -> 2% of each run, Pallas kernels for 15% -> 14%
where the time goes in v2:
time: 211 us; the launch traced here: 210 us
  waiting for transfers between devices  106 us (50%)
  Pallas kernels  53.7 us (25%)
  starting transfers between devices  30.6 us (15%)
  local copies, waits for them, and re-layouts  12.6 us (6%)
  other arithmetic  5.95 us (3%)
    ppermute x21, waiting for transfers between devices, across(): return lax.ppermute(a, 'replica', perm)  61.8 us
    pallas_call x23, Pallas kernels, run(): pl.pallas_call(inner, out_shape=outs, in_specs=[SMEM] + [VMEM] * count +...  53.7 us
    ppermute x12, waiting for transfers between devices, shifted(): lax.ppermute(a, 'group', [(i, (i + k) % groups) for i in range(groups)])  44.3 us
    ppermute x21, starting transfers between devices, across(): return lax.ppermute(a, 'replica', perm)  19.8 us
    ppermute x12, starting transfers between devices, shifted(): lax.ppermute(a, 'group', [(i, (i + k) % groups) for i in range(groups)])  10.8 us
    unnamed x57, local copies, waits for them, and re-layouts  8.85 us
  transfers between devices with their start and end apart: 33, of which 22 were waited for; matrix products, arithmetic and copies ran while one was open for 2% of the time, Pallas kernels for 14%

profile of v2, /device:TPU:9, one launch (start us, length us, event | category | flops | bytes accessed | tf_op | source)
XLA Modules:
  0.0 210.1 jit_solution(11305814958284856741)
XLA Ops:
  2.9 1.3 collective-permute-start
  4.3 1.1 collective-permute-start.1
  5.4 1.4 collective-permute-start.2
  10.1 4.1 %collective-permute-done.1.refs_1_ = bf16[48,1280]{1,0:T(8,128)(2,1)S(1)} collective-permute-done((bf16[48,1280]{1,0:T(8,128)(2,1)S(1)}, bf16[48,1280]{1,0:T(8,128)(2,1)S(1)}, u32[]{:S(2)}, u32[]{:S(2)}) %collective-permute-start.1) | collective-permute-done | bytes 122912 | tf_op jit(solution)/shard_map/ppermute | solution.py:457
  14.2 2.8 %collective-permute-done.2.refs_2_ = bf16[48,1280]{1,0:T(8,128)(2,1)S(1)} collective-permute-done((bf16[48,1280]{1,0:T(8,128)(2,1)S(1)}, bf16[48,1280]{1,0:T(8,128)(2,1)S(1)}, u32[]{:S(2)}, u32[]{:S(2)}) %collective-permute-start.2) | collective-permute-done | bytes 122912 | tf_op jit(solution)/shard_map/ppermute | solution.py:457
  18.2 1.2 collective-permute-start.3
  19.5 5.9 %collective-permute-done.4.refs_2_.refs_0_ = bf16[48,2176]{1,0:T(8,128)(2,1)S(1)} collective-permute-done((bf16[48,2176]{1,0:T(8,128)(2,1)S(1)}, bf16[48,2176]{1,0:T(8,128)(2,1)S(1)}, u32[]{:S(2)}, u32[]{:S(2)}) %collective-permute-start.4) | collective-permute-done | bytes 208928 | tf_op jit(solution)/shard_map/ppermute | solution.py:457
  26.1 2.3 %collective-permute-start.5 = (bf16[2,3,48,1152]{3,2,1,0:T(8,128)(2,1)S(1)}, bf16[2,3,48,1152]{3,2,1,0:T(8,128)(2,1)S(1)}, u32[]{:S(2)}, u32[]{:S(2)}) collective-permute-start(bf16[2,3,48,1152]{3,2,1,0:T(8,128)(2,1)S(1)} %join.6.refs_7_.refs_5_), channel_id=1, source_target_pairs={{0,16},{4,12},{8,24},{12,4},{16,0},{20,28},{24,8},{28,20},{1,17},{... | collective-permute-start | bytes 1990664 | tf_op jit(solution)/shard_map/ppermute | solution.py:454
  28.4 1.3 collective-permute-start.8
  29.7 7.0 %collective-permute-done.5.refs_3_.refs_8_.refs_6_ = bf16[2,3,48,1152]{3,2,1,0:T(8,128)(2,1)S(1)} collective-permute-done((bf16[2,3,48,1152]{3,2,1,0:T(8,128)(2,1)S(1)}, bf16[2,3,48,1152]{3,2,1,0:T(8,128)(2,1)S(1)}, u32[]{:S(2)}, u32[]{:S(2)}) %collective-permute-start.5) | collective-permute-done | bytes 663584 | tf_op jit(solution)/shard_map/ppermute | solution.py:454
  36.7 1.8 collective-permute-start.7
  38.5 4.9 %collective-permute-done.8.refs_1_ = bf16[48,2176]{1,0:T(8,128)(2,1)S(1)} collective-permute-done((bf16[48,2176]{1,0:T(8,128)(2,1)S(1)}, bf16[48,2176]{1,0:T(8,128)(2,1)S(1)}, u32[]{:S(2)}, u32[]{:S(2)}) %collective-permute-start.8) | collective-permute-done | bytes 208928 | tf_op jit(solution)/shard_map/ppermute | solution.py:457
  43.3 1.2 collective-permute-done.9.refs_2_
  51.4 8.3 %attn_forward.1 = (bf16[256,768]{1,0:T(8,128)(2,1)S(1)}, bf16[256,2304]{1,0:T(8,128)(2,1)S(1)}, bf16[256,768]{1,0:T(8,128)(2,1)S(1)}, f32[256,128]{1,0:T(8,128)S(1)}) custom-call(s32[4]{0:T(128)S(1)} %pad_add_fusion.place, f32[2,768]{1,0:T(2,128)S(1)} %pad_maximum_fusion.4.refs_0_.refs_2_, f32[256,128]{1,0:T(8,128)S(1)} %copy-done.6, ...), custom_call_target="tpu_custom_call" | custom-call | tf_op jit(solution)/shard_map/attn_forward/pallas_call | solution.py:39
  59.7 1.3 join.7.refs_8_
  61.1 1.3 collective-permute-start.11
  62.4 1.3 collective-permute-start.12
  63.7 13.6 %collective-permute-done.11.refs_9_ = bf16[2,3,48,2176]{3,2,1,0:T(8,128)(2,1)S(1)} collective-permute-done((bf16[2,3,48,2176]{3,2,1,0:T(8,128)(2,1)S(1)}, bf16[2,3,48,2176]{3,2,1,0:T(8,128)(2,1)S(1)}, u32[]{:S(2)}, u32[]{:S(2)}) %collective-permute-start.11) | collective-permute-done | bytes 1253408 | tf_op jit(solution)/shard_map/ppermute | solution.py:454
  77.3 1.9 collective-permute-start.13
  79.2 2.6 %collective-permute-done.13.refs_11_ = bf16[2,3,48,2176]{3,2,1,0:T(8,128)(2,1)S(1)} collective-permute-done((bf16[2,3,48,2176]{3,2,1,0:T(8,128)(2,1)S(1)}, bf16[2,3,48,2176]{3,2,1,0:T(8,128)(2,1)S(1)}, u32[]{:S(2)}, u32[]{:S(2)}) %collective-permute-start.13) | collective-permute-done | bytes 1253408 | tf_op jit(solution)/shard_map/ppermute | solution.py:454
  82.8 11.7 %feed_forward.1 = (bf16[256,768]{1,0:T(8,128)(2,1)}, f32[256,768]{1,0:T(8,128)S(1)}, bf16[256,768]{1,0:T(8,128)(2,1)S(1)}, bf16[256,768]{1,0:T(8,128)(2,1)S(1)},...) custom-call(s32[4]{0:T(128)S(1)} %pad_add_fusion.place, ...), custom_call_target="tpu_custom_call" | custom-call | tf_op jit(solution)/shard_map/feed_forward/pallas_call | solution.py:39
  95.8 6.4 %attn_backward.1 = (bf16[256,2304]{1,0:T(8,128)(2,1)S(1)}, bf16[256,1152]{1,0:T(8,128)(2,1)S(1)}) custom-call(s32[4]{0:T(128)S(1)} %pad_add_fusion.place, bf16[256,2304]{1,0:T(8,128)(2,1)S(1)} %get-tuple-element.53.refs_0_, f32[256,128]{1,0:T(8,128)S(1)} %get-tuple-element.54.refs_1_, bf16[256,768]{1,0:T(8,128)(2,1)S(1)} %get-tuple-element.55.refs_2_, ...), custom_call_target="tpu_custom_call" | custom-call | tf_op jit(solution)/shard_map/attn_backward/pallas_call | solution.py:39
  102.2 1.7 grad_for_self.3
  103.9 3.5 %grad_for_self.4 = (bf16[4,96,1536]{2,1,0:T(8,128)(2,1)S(1)}, bf16[4,96,1536]{2,1,0:T(8,128)(2,1)S(1)}) custom-call(s32[4]{0:T(128)S(1)} %pad_add_fusion.place, bf16[256,768]{1,0:T(8,128)(2,1)S(1)} %get-tuple-element.63.refs_0_, bf16[256,2304]{1,0:T(8,128)(2,1)S(1)} %get-tuple-element.64.refs_1_, bf16[256,768]{1,0:T(8,128)(2,1)S(1)} %get-tuple-element.50.refs_2_.refs_1_, ...), custom_call_target="tpu_custom_call" | custom-call | tf_op jit(solution)/shard_map/grad_for_self/pallas_call | solution.py:39
  107.4 1.3 collective-permute-start.16
  109.4 1.3 collective-permute-done.17.refs_3_
  110.7 2.6 %grad_for_self.5 = (bf16[4,96,1152]{2,1,0:T(8,128)(2,1)S(1)}, bf16[4,96,1152]{2,1,0:T(8,128)(2,1)S(1)}) custom-call(s32[4]{0:T(128)S(1)} %pad_add_fusion.place, bf16[256,768]{1,0:T(8,128)(2,1)S(1)} %get-tuple-element.51.refs_2_.refs_0_, bf16[256,2304]{1,0:T(8,128)(2,1)S(1)} %get-tuple-element.56.refs_1_.refs_0_, ...), custom_call_target="tpu_custom_call" | custom-call | tf_op jit(solution)/shard_map/grad_for_self/pallas_call | solution.py:39
  113.7 13.8 %collective-permute-done.15.refs_1_ = bf16[4,144,384]{2,1,0:T(8,128)(2,1)S(1)} collective-permute-done((bf16[4,144,384]{2,1,0:T(8,128)(2,1)S(1)}, bf16[4,144,384]{2,1,0:T(8,128)(2,1)S(1)}, u32[]{:S(2)}, u32[]{:S(2)}) %collective-permute-start.15) | collective-permute-done | bytes 442400 | tf_op jit(solution)/shard_map/ppermute | solution.py:454
  129.2 4.4 %attn_in_backward.1.refs_2_ = bf16[256,768]{1,0:T(8,128)(2,1)} custom-call(s32[4]{0:T(128)S(1)} %pad_add_fusion.place, bf16[256,2304]{1,0:T(8,128)(2,1)S(1)} %get-tuple-element.56.refs_1_.refs_0_, f32[256,768]{1,0:T(8,128)S(1)} %copy-done.17, f32[2,768]{1,0:T(2,128)S(1)} %pad_maximum_fusion.4.refs_0_.refs_2_, bf16[256,768]{1,0:T(8,128)(2,1)S(1)} %copy-done.4, ...), custom_call_target="tpu_custom_call" | custom-call | tf_op jit(solution)/shard_map/attn_in_backward/pallas_call | solution.py:39
  133.6 7.6 %collective-permute-done.18.refs_1_ = bf16[4,96,1152]{2,1,0:T(8,128)(2,1)S(1)} collective-permute-done((bf16[4,96,1152]{2,1,0:T(8,128)(2,1)S(1)}, bf16[4,96,1152]{2,1,0:T(8,128)(2,1)S(1)}, u32[]{:S(2)}, u32[]{:S(2)}) %collective-permute-start.18) | collective-permute-done | bytes 884768 | tf_op jit(solution)/shard_map/ppermute | solution.py:454
  143.7 2.6 %collective-permute-done.20.refs_1_ = bf16[4,48,2176]{2,1,0:T(8,128)(2,1)S(1)} collective-permute-done((bf16[4,48,2176]{2,1,0:T(8,128)(2,1)S(1)}, bf16[4,48,2176]{2,1,0:T(8,128)(2,1)S(1)}, u32[]{:S(2)}, u32[]{:S(2)}) %collective-permute-start.20) | collective-permute-done | bytes 835616 | tf_op jit(solution)/shard_map/ppermute | solution.py:454
  147.1 1.8 collective-permute-start.25
  148.9 1.4 collective-permute-start.26
  150.3 1.0 collective-permute-done.19.refs_1_
  152.4 11.5 %collective-permute-done.25.refs_2_ = bf16[48,2176]{1,0:T(8,128)(2,1)S(1)} collective-permute-done((bf16[48,2176]{1,0:T(8,128)(2,1)S(1)}, bf16[48,2176]{1,0:T(8,128)(2,1)S(1)}, u32[]{:S(2)}, u32[]{:S(2)}) %collective-permute-start.25) | collective-permute-done | bytes 208928 | tf_op jit(solution)/shard_map/ppermute | solution.py:457
  163.9 4.0 %collective-permute-done.26.refs_3_ = bf16[48,2176]{1,0:T(8,128)(2,1)S(1)} collective-permute-done((bf16[48,2176]{1,0:T(8,128)(2,1)S(1)}, bf16[48,2176]{1,0:T(8,128)(2,1)S(1)}, u32[]{:S(2)}, u32[]{:S(2)}) %collective-permute-start.26) | collective-permute-done | bytes 208928 | tf_op jit(solution)/shard_map/ppermute | solution.py:457
  169.1 4.4 %collective-permute-done.27.refs_1_ = bf16[48,2176]{1,0:T(8,128)(2,1)S(1)} collective-permute-done((bf16[48,2176]{1,0:T(8,128)(2,1)S(1)}, bf16[48,2176]{1,0:T(8,128)(2,1)S(1)}, u32[]{:S(2)}, u32[]{:S(2)}) %collective-permute-start.27) | collective-permute-done | bytes 208928 | tf_op jit(solution)/shard_map/ppermute | solution.py:454
  175.7 1.5 collective-permute-start.23
  177.1 1.3 collective-permute-done.21.refs_1_
  178.4 2.1 collective-permute-done.22.refs_2_
  180.5 6.1 %collective-permute-done.23.refs_3_ = bf16[48,1152]{1,0:T(8,128)(2,1)S(1)} collective-permute-done((bf16[48,1152]{1,0:T(8,128)(2,1)S(1)}, bf16[48,1152]{1,0:T(8,128)(2,1)S(1)}, u32[]{:S(2)}, u32[]{:S(2)}) %collective-permute-start.23) | collective-permute-done | bytes 110624 | tf_op jit(solution)/shard_map/ppermute | solution.py:457
  188.7 3.6 %collective-permute-done.28.refs_1_ = bf16[48,1152]{1,0:T(8,128)(2,1)S(1)} collective-permute-done((bf16[48,1152]{1,0:T(8,128)(2,1)S(1)}, bf16[48,1152]{1,0:T(8,128)(2,1)S(1)}, u32[]{:S(2)}, u32[]{:S(2)}) %collective-permute-start.28) | collective-permute-done | bytes 110624 | tf_op jit(solution)/shard_map/ppermute | solution.py:454
  193.8 4.2 %collective-permute-done.30.refs_1_ = bf16[2,48,1152]{2,1,0:T(8,128)(2,1)S(1)} collective-permute-done((bf16[2,48,1152]{2,1,0:T(8,128)(2,1)S(1)}, bf16[2,48,1152]{2,1,0:T(8,128)(2,1)S(1)}, u32[]{:S(2)}, u32[]{:S(2)}) %collective-permute-start.30) | collective-permute-done | bytes 221216 | tf_op jit(solution)/shard_map/ppermute | solution.py:454
  198.6 1.9 collective-permute-start.31
  200.8 3.2 %place_mlp.1 = (f32[192,2304]{1,0:T(8,128)}, f32[192,768]{1,0:T(8,128)}, f32[288,768]{1,0:T(8,128)}, f32[192,1]{1,0:T(8,128)S(1)}) custom-call(s32[4]{0:T(128)S(1)} %pad_add_fusion.place, f32[192,1]{1,0:T(8,128)S(1)} %copy.26.refs_0_, bf16[2,2,48,2176]{3,2,1,0:T(8,128)(2,1)S(1)} %join.9.refs_2_.refs_1_, ...), custom_call_target="tpu_custom_call" | custom-call | tf_op jit(solution)/shard_map/place_mlp/pallas_call | solution.py:39
  204.0 1.5 copy-done.11
  205.5 2.4 %place_qkv.1 = (f32[192,2304]{1,0:T(8,128)}, f32[192,1]{1,0:T(8,128)S(1)}) custom-call(s32[4]{0:T(128)S(1)} %pad_add_fusion.place, f32[192,1]{1,0:T(8,128)S(1)} %copy.27.refs_0_, bf16[2,2,48,1152]{3,2,1,0:T(8,128)(2,1)S(1)} %join.11.refs_1_, bf16[2,2,48,1152]{3,2,1,0:T(8,128)(2,1)} %collective-permute-done.31.refs_2_, bf16[192,2304]{1,0:T(8,128)(2,1)S(1)} %copy-done, ...), custom_call_target="tpu_custom_call" | custom-call | tf_op jit(solution)/shard_map/place_qkv/pallas_call | solution.py:39
  208.5 1.6 reduce.2
  (131 shorter events, 32.2 us)
Async XLA Ops:
  2.9 7.2 %collective-permute-start = (bf16[48,1280]{1,0:T(8,128)(2,1)S(1)}, bf16[48,1280]{1,0:T(8,128)(2,1)S(1)}, u32[]{:S(2)}, u32[]{:S(2)}) collective-permute-start(bf16[48,1280]{1,0:T(8,128)(2,1)S(1)} %pad_maximum_fusion.3), channel_id=1, source_target_pairs={{0,1},{1,2},{2,3},{3,0},{4,5},{5,6},{6,7},{7,4},{8,9},{9,10},{10,1... | collective-permute-start | bytes 368648 | tf_op jit(solution)/shard_map/ppermute | solution.py:457
  4.3 9.9 %collective-permute-start.1 = (bf16[48,1280]{1,0:T(8,128)(2,1)S(1)}, bf16[48,1280]{1,0:T(8,128)(2,1)S(1)}, u32[]{:S(2)}, u32[]{:S(2)}) collective-permute-start(bf16[48,1280]{1,0:T(8,128)(2,1)S(1)} %pad_maximum_fusion.3), channel_id=1, source_target_pairs={{0,2},{1,3},{2,0},{3,1},{4,6},{5,7},{6,4},{7,5},{8,10},{9,11},{10,... | collective-permute-start | bytes 368648 | tf_op jit(solution)/shard_map/ppermute | solution.py:457
  5.4 11.6 %collective-permute-start.2 = (bf16[48,1280]{1,0:T(8,128)(2,1)S(1)}, bf16[48,1280]{1,0:T(8,128)(2,1)S(1)}, u32[]{:S(2)}, u32[]{:S(2)}) collective-permute-start(bf16[48,1280]{1,0:T(8,128)(2,1)S(1)} %pad_maximum_fusion.3), channel_id=1, source_target_pairs={{0,3},{1,0},{2,1},{3,2},{4,7},{5,4},{6,5},{7,6},{8,11},{9,8},{10,9... | collective-permute-start | bytes 368648 | tf_op jit(solution)/shard_map/ppermute | solution.py:457
  10.1 15.4 %copy-start.5 = (f32[256,128]{1,0:T(8,128)}, f32[256,128]{1,0:T(8,128)S(1)}, u32[]{:S(2)}) copy-start(f32[256,128]{1,0:T(8,128)S(1)} %get-tuple-element.97.refs_3_.refs_1_) | copy-start | bytes 393220
  10.1 15.4 %copy-start.8 = (f32[256,128]{1,0:T(8,128)}, f32[256,128]{1,0:T(8,128)S(1)}, u32[]{:S(2)}) copy-start(f32[256,128]{1,0:T(8,128)S(1)} %get-tuple-element.98.refs_4_.refs_2_) | copy-start | bytes 393220
  18.2 7.3 %collective-permute-start.3 = (bf16[3,48,1152]{2,1,0:T(8,128)(2,1)S(1)}, bf16[3,48,1152]{2,1,0:T(8,128)(2,1)S(1)}, u32[]{:S(2)}, u32[]{:S(2)}) collective-permute-start(bf16[3,48,1152]{2,1,0:T(8,128)(2,1)S(1)} %get-tuple-element.49.refs_0_), channel_id=1, source_target_pairs={{0,8},{4,20},{8,0},{12,28},{16,24},{20,4},{24,16},{28,12},{1,9},{5... | collective-permute-start | bytes 995336 | tf_op jit(solution)/shard_map/ppermute | solution.py:454
  19.4 6.0 %collective-permute-start.4 = (bf16[48,2176]{1,0:T(8,128)(2,1)S(1)}, bf16[48,2176]{1,0:T(8,128)(2,1)S(1)}, u32[]{:S(2)}, u32[]{:S(2)}) collective-permute-start(bf16[48,2176]{1,0:T(8,128)(2,1)S(1)} %pad_maximum_fusion), channel_id=1, source_target_pairs={{0,1},{1,2},{2,3},{3,0},{4,5},{5,6},{6,7},{7,4},{8,9},{9,10},{10,1... | collective-permute-start | bytes 626696 | tf_op jit(solution)/shard_map/ppermute | solution.py:457
  26.1 20.0 %copy-start.23 = (s32[256]{0:T(256)S(1)}, s32[256]{0:T(256)}, u32[]{:S(2)}) copy-start(s32[256]{0:T(256)} %param.10) | copy-start | bytes 3076
  26.1 20.7 %copy-start.22 = (bf16[3,48,128]{2,1,0:T(8,128)(2,1)S(1)}, bf16[3,48,128]{2,1,0:T(8,128)(2,1)}, u32[]{:S(2)}) copy-start(bf16[3,48,128]{2,1,0:T(8,128)(2,1)} %copy-done.21) | copy-start | bytes 110596
  26.1 21.6 %copy-start = (bf16[192,2304]{1,0:T(8,128)(2,1)S(1)}, bf16[192,2304]{1,0:T(8,128)(2,1)}, u32[]{:S(2)}) copy-start(bf16[192,2304]{1,0:T(8,128)(2,1)} %refs_3_.7) | copy-start | bytes 2654212
  26.1 10.6 %collective-permute-start.5 = (bf16[2,3,48,1152]{3,2,1,0:T(8,128)(2,1)S(1)}, bf16[2,3,48,1152]{3,2,1,0:T(8,128)(2,1)S(1)}, u32[]{:S(2)}, u32[]{:S(2)}) collective-permute-start(bf16[2,3,48,1152]{3,2,1,0:T(8,128)(2,1)S(1)} %join.6.refs_7_.refs_5_), channel_id=1, source_target_pairs={{0,16},{4,12},{8,24},{12,4},{16,0},{20,28},{24,8},{28,20},{1,17},{... | collective-permute-start | bytes 1990664 | tf_op jit(solution)/shard_map/ppermute | solution.py:454
  28.4 16.2 %collective-permute-start.6 = (bf16[2,3,48,1152]{3,2,1,0:T(8,128)(2,1)S(1)}, bf16[2,3,48,1152]{3,2,1,0:T(8,128)(2,1)S(1)}, u32[]{:S(2)}, u32[]{:S(2)}) collective-permute-start(bf16[2,3,48,1152]{3,2,1,0:T(8,128)(2,1)S(1)} %join.6.refs_7_.refs_5_), channel_id=1, source_target_pairs={{0,4},{4,0},{8,12},{12,8},{16,20},{20,16},{24,28},{28,24},{1,5},{5... | collective-permute-start | bytes 1990664 | tf_op jit(solution)/shard_map/ppermute | solution.py:454
  28.4 15.0 %collective-permute-start.8 = (bf16[48,2176]{1,0:T(8,128)(2,1)S(1)}, bf16[48,2176]{1,0:T(8,128)(2,1)S(1)}, u32[]{:S(2)}, u32[]{:S(2)}) collective-permute-start(bf16[48,2176]{1,0:T(8,128)(2,1)S(1)} %pad_maximum_fusion), channel_id=1, source_target_pairs={{0,2},{1,3},{2,0},{3,1},{4,6},{5,7},{6,4},{7,5},{8,10},{9,11},{10,... | collective-permute-start | bytes 626696 | tf_op jit(solution)/shard_map/ppermute | solution.py:457
  29.6 14.9 %collective-permute-start.9 = (bf16[48,2176]{1,0:T(8,128)(2,1)S(1)}, bf16[48,2176]{1,0:T(8,128)(2,1)S(1)}, u32[]{:S(2)}, u32[]{:S(2)}) collective-permute-start(bf16[48,2176]{1,0:T(8,128)(2,1)S(1)} %pad_maximum_fusion), channel_id=1, source_target_pairs={{0,3},{1,0},{2,1},{3,2},{4,7},{5,4},{6,5},{7,6},{8,11},{9,8},{10,9... | collective-permute-start | bytes 626696 | tf_op jit(solution)/shard_map/ppermute | solution.py:457
  36.7 11.0 %collective-permute-start.7 = (bf16[2,3,48,1152]{3,2,1,0:T(8,128)(2,1)S(1)}, bf16[2,3,48,1152]{3,2,1,0:T(8,128)(2,1)}, u32[]{:S(2)}, u32[]{:S(2)}) collective-permute-start(bf16[2,3,48,1152]{3,2,1,0:T(8,128)(2,1)S(1)} %collective-permute-done.5.refs_3_.refs_8_.refs_6_), channel_id=1, source_target_pairs={{0,4},{4,0},{8,12},{12,8},{16,20},{20,16},{24,28},{28,24},{1,5},{5... | collective-permute-start | bytes 1990664 | tf_op jit(solution)/shard_map/ppermute | solution.py:454
  45.1 14.5 %collective-permute-start.10 = (bf16[3,48,2176]{2,1,0:T(8,128)(2,1)S(1)}, bf16[3,48,2176]{2,1,0:T(8,128)(2,1)}, u32[]{:S(2)}, u32[]{:S(2)}) collective-permute-start(bf16[3,48,2176]{2,1,0:T(8,128)(2,1)S(1)} %stack_pieces.3.refs_11_.refs_0_), channel_id=1, source_target_pairs={{0,8},{4,20},{8,0},{12,28},{16,24},{20,4},{24,16},{28,12},{1,9},{5... | collective-permute-start | bytes 1880072 | tf_op jit(solution)/shard_map/ppermute | solution.py:454
  59.7 23.1 %copy-start.1 = (bf16[192,2304]{1,0:T(8,128)(2,1)S(1)}, bf16[192,2304]{1,0:T(8,128)(2,1)}, u32[]{:S(2)}) copy-start(bf16[192,2304]{1,0:T(8,128)(2,1)} %refs_3_.6) | copy-start | bytes 2654212
  59.7 23.1 %copy-start.4 = (bf16[256,768]{1,0:T(8,128)(2,1)S(1)}, bf16[256,768]{1,0:T(8,128)(2,1)}, u32[]{:S(2)}) copy-start(bf16[256,768]{1,0:T(8,128)(2,1)} %refs_3_.5) | copy-start | bytes 1179652
  59.7 23.1 %copy-start.12 = (bf16[256,768]{1,0:T(8,128)(2,1)S(1)}, bf16[256,768]{1,0:T(8,128)(2,1)}, u32[]{:S(2)}) copy-start(bf16[256,768]{1,0:T(8,128)(2,1)} %refs_1_.1) | copy-start | bytes 1179652
  59.7 23.1 %copy-start.18 = (bf16[288,768]{1,0:T(8,128)(2,1)S(1)}, bf16[288,768]{1,0:T(8,128)(2,1)}, u32[]{:S(2)}) copy-start(bf16[288,768]{1,0:T(8,128)(2,1)} %refs_7_.1) | copy-start | bytes 1327108
  59.7 23.1 %copy-start.19 = (bf16[192,768]{1,0:T(8,128)(2,1)S(1)}, bf16[192,768]{1,0:T(8,128)(2,1)}, u32[]{:S(2)}) copy-start(bf16[192,768]{1,0:T(8,128)(2,1)} %refs_6_.3) | copy-start | bytes 884740
  61.1 16.2 %collective-permute-start.11 = (bf16[2,3,48,2176]{3,2,1,0:T(8,128)(2,1)S(1)}, bf16[2,3,48,2176]{3,2,1,0:T(8,128)(2,1)S(1)}, u32[]{:S(2)}, u32[]{:S(2)}) collective-permute-start(bf16[2,3,48,2176]{3,2,1,0:T(8,128)(2,1)S(1)} %join.7.refs_8_), channel_id=1, source_target_pairs={{0,16},{4,12},{8,24},{12,4},{16,0},{20,28},{24,8},{28,20},{1,17},{... | collective-permute-start | bytes 3760136 | tf_op jit(solution)/shard_map/ppermute | solution.py:454
  62.4 16.8 %collective-permute-start.12 = (bf16[2,3,48,2176]{3,2,1,0:T(8,128)(2,1)S(1)}, bf16[2,3,48,2176]{3,2,1,0:T(8,128)(2,1)S(1)}, u32[]{:S(2)}, u32[]{:S(2)}) collective-permute-start(bf16[2,3,48,2176]{3,2,1,0:T(8,128)(2,1)S(1)} %join.7.refs_8_), channel_id=1, source_target_pairs={{0,4},{4,0},{8,12},{12,8},{16,20},{20,16},{24,28},{28,24},{1,5},{5... | collective-permute-start | bytes 3760136 | tf_op jit(solution)/shard_map/ppermute | solution.py:454
  77.3 4.5 %collective-permute-start.13 = (bf16[2,3,48,2176]{3,2,1,0:T(8,128)(2,1)S(1)}, bf16[2,3,48,2176]{3,2,1,0:T(8,128)(2,1)S(1)}, u32[]{:S(2)}, u32[]{:S(2)}) collective-permute-start(bf16[2,3,48,2176]{3,2,1,0:T(8,128)(2,1)S(1)} %collective-permute-done.11.refs_9_), channel_id=1, source_target_pairs={{0,4},{4,0},{8,12},{12,8},{16,20},{20,16},{24,28},{28,24},{1,5},{5... | collective-permute-start | bytes 3760136 | tf_op jit(solution)/shard_map/ppermute | solution.py:454
  82.8 12.9 %copy-start.7 = (f32[256,128]{1,0:T(8,128)S(1)}, f32[256,128]{1,0:T(8,128)}, u32[]{:S(2)}) copy-start(f32[256,128]{1,0:T(8,128)} %copy-done.5) | copy-start | bytes 393220
  82.8 12.9 %copy-start.10 = (f32[256,128]{1,0:T(8,128)S(1)}, f32[256,128]{1,0:T(8,128)}, u32[]{:S(2)}) copy-start(f32[256,128]{1,0:T(8,128)} %copy-done.8) | copy-start | bytes 393220
  82.8 12.9 %copy-start.15 = (s32[256,1]{1,0:T(8,128)S(1)}, s32[256,1]{1,0:T(8,128)}, u32[]{:S(2)}) copy-start(s32[256,1]{1,0:T(8,128)} %copy.24.refs_3_.refs_5_) | copy-start | bytes 3076
  95.4 6.8 %collective-permute-start.14 = (bf16[256,5376]{1,0:T(8,128)(2,1)}, bf16[256,5376]{1,0:T(8,128)(2,1)S(1)}, u32[]{:S(2)}, u32[]{:S(2)}) collective-permute-start(bf16[256,5376]{1,0:T(8,128)(2,1)} %get-tuple-element.59), channel_id=1, source_target_pairs={{0,4},{4,0},{8,12},{12,8},{16,20},{20,16},{24,28},{28,24},{1,5},{5... | collective-permute-start | bytes 8257544 | tf_op jit(solution)/shard_map/ppermute | solution.py:454
  107.4 20.2 %collective-permute-start.16 = (bf16[4,96,1536]{2,1,0:T(8,128)(2,1)S(1)}, bf16[4,96,1536]{2,1,0:T(8,128)(2,1)S(1)}, u32[]{:S(2)}, u32[]{:S(2)}) collective-permute-start(bf16[4,96,1536]{2,1,0:T(8,128)(2,1)S(1)} %get-tuple-element.67), channel_id=1, source_target_pairs={{0,8},{4,20},{8,0},{12,28},{16,24},{20,4},{24,16},{28,12},{1,9},{5... | collective-permute-start | bytes 3538952 | tf_op jit(solution)/shard_map/ppermute | solution.py:454
  108.7 2.0 collective-permute-start.17
  108.7 18.8 %collective-permute-start.15 = (bf16[4,144,384]{2,1,0:T(8,128)(2,1)S(1)}, bf16[4,144,384]{2,1,0:T(8,128)(2,1)S(1)}, u32[]{:S(2)}, u32[]{:S(2)}) collective-permute-start(bf16[4,144,384]{2,1,0:T(8,128)(2,1)S(1)} %get-tuple-element.62), channel_id=1, source_target_pairs={{0,8},{4,20},{8,0},{12,28},{16,24},{20,4},{24,16},{28,12},{1,9},{5... | collective-permute-start | bytes 1327112 | tf_op jit(solution)/shard_map/ppermute | solution.py:454
  113.3 27.9 %collective-permute-start.18 = (bf16[4,96,1152]{2,1,0:T(8,128)(2,1)S(1)}, bf16[4,96,1152]{2,1,0:T(8,128)(2,1)S(1)}, u32[]{:S(2)}, u32[]{:S(2)}) collective-permute-start(bf16[4,96,1152]{2,1,0:T(8,128)(2,1)S(1)} %get-tuple-element.70), channel_id=1, source_target_pairs={{0,8},{4,20},{8,0},{12,28},{16,24},{20,4},{24,16},{28,12},{1,9},{5... | collective-permute-start | bytes 2654216 | tf_op jit(solution)/shard_map/ppermute | solution.py:454
  128.5 17.8 %collective-permute-start.20 = (bf16[4,48,2176]{2,1,0:T(8,128)(2,1)S(1)}, bf16[4,48,2176]{2,1,0:T(8,128)(2,1)S(1)}, u32[]{:S(2)}, u32[]{:S(2)}) collective-permute-start(bf16[4,48,2176]{2,1,0:T(8,128)(2,1)S(1)} %get-tuple-element.73), channel_id=1, source_target_pairs={{0,16},{4,12},{8,24},{12,4},{16,0},{20,28},{24,8},{28,20},{1,17},{... | collective-permute-start | bytes 2506760 | tf_op jit(solution)/shard_map/ppermute | solution.py:454
  143.0 8.3 %collective-permute-start.19 = (bf16[4,48,1152]{2,1,0:T(8,128)(2,1)S(1)}, bf16[4,48,1152]{2,1,0:T(8,128)(2,1)S(1)}, u32[]{:S(2)}, u32[]{:S(2)}) collective-permute-start(bf16[4,48,1152]{2,1,0:T(8,128)(2,1)S(1)} %get-tuple-element.72), channel_id=1, source_target_pairs={{0,16},{4,12},{8,24},{12,4},{16,0},{20,28},{24,8},{28,20},{1,17},{... | collective-permute-start | bytes 1327112 | tf_op jit(solution)/shard_map/ppermute | solution.py:454
  147.0 5.3 %collective-permute-start.24 = (bf16[48,2176]{1,0:T(8,128)(2,1)S(1)}, bf16[48,2176]{1,0:T(8,128)(2,1)S(1)}, u32[]{:S(2)}, u32[]{:S(2)}) collective-permute-start(bf16[48,2176]{1,0:T(8,128)(2,1)S(1)} %get-tuple-element.79), channel_id=1, source_target_pairs={{0,1},{1,2},{2,3},{3,0},{4,5},{5,6},{6,7},{7,4},{8,9},{9,10},{10,1... | collective-permute-start | bytes 626696 | tf_op jit(solution)/shard_map/ppermute | solution.py:457
  147.1 16.8 %collective-permute-start.25 = (bf16[48,2176]{1,0:T(8,128)(2,1)S(1)}, bf16[48,2176]{1,0:T(8,128)(2,1)S(1)}, u32[]{:S(2)}, u32[]{:S(2)}) collective-permute-start(bf16[48,2176]{1,0:T(8,128)(2,1)S(1)} %get-tuple-element.80), channel_id=1, source_target_pairs={{0,2},{1,3},{2,0},{3,1},{4,6},{5,7},{6,4},{7,5},{8,10},{9,11},{10,... | collective-permute-start | bytes 626696 | tf_op jit(solution)/shard_map/ppermute | solution.py:457
  148.9 19.0 %collective-permute-start.26 = (bf16[48,2176]{1,0:T(8,128)(2,1)S(1)}, bf16[48,2176]{1,0:T(8,128)(2,1)S(1)}, u32[]{:S(2)}, u32[]{:S(2)}) collective-permute-start(bf16[48,2176]{1,0:T(8,128)(2,1)S(1)} %get-tuple-element.81), channel_id=1, source_target_pairs={{0,3},{1,0},{2,1},{3,2},{4,7},{5,4},{6,5},{7,6},{8,11},{9,8},{10,9... | collective-permute-start | bytes 626696 | tf_op jit(solution)/shard_map/ppermute | solution.py:457
  168.6 5.0 %collective-permute-start.27 = (bf16[48,2176]{1,0:T(8,128)(2,1)S(1)}, bf16[48,2176]{1,0:T(8,128)(2,1)S(1)}, u32[]{:S(2)}, u32[]{:S(2)}) collective-permute-start(bf16[48,2176]{1,0:T(8,128)(2,1)S(1)} %sum_pieces.2.refs_0_), channel_id=1, source_target_pairs={{0,16},{4,12},{8,24},{12,4},{16,0},{20,28},{24,8},{28,20},{1,17},{... | collective-permute-start | bytes 626696 | tf_op jit(solution)/shard_map/ppermute | solution.py:454
  174.1 13.0 %collective-permute-start.29 = (bf16[2,48,2176]{2,1,0:T(8,128)(2,1)S(1)}, bf16[2,48,2176]{2,1,0:T(8,128)(2,1)S(1)}, u32[]{:S(2)}, u32[]{:S(2)}) collective-permute-start(bf16[2,48,2176]{2,1,0:T(8,128)(2,1)S(1)} %join.8.refs_4_.refs_0_), channel_id=1, source_target_pairs={{0,8},{4,20},{8,0},{12,28},{16,24},{20,4},{24,16},{28,12},{1,9},{5... | collective-permute-start | bytes 1253384 | tf_op jit(solution)/shard_map/ppermute | solution.py:454
  174.8 3.6 %collective-permute-start.21 = (bf16[48,1152]{1,0:T(8,128)(2,1)S(1)}, bf16[48,1152]{1,0:T(8,128)(2,1)S(1)}, u32[]{:S(2)}, u32[]{:S(2)}) collective-permute-start(bf16[48,1152]{1,0:T(8,128)(2,1)S(1)} %get-tuple-element.76), channel_id=1, source_target_pairs={{0,1},{1,2},{2,3},{3,0},{4,5},{5,6},{6,7},{7,4},{8,9},{9,10},{10,1... | collective-permute-start | bytes 331784 | tf_op jit(solution)/shard_map/ppermute | solution.py:457
  174.8 5.7 %collective-permute-start.22 = (bf16[48,1152]{1,0:T(8,128)(2,1)S(1)}, bf16[48,1152]{1,0:T(8,128)(2,1)S(1)}, u32[]{:S(2)}, u32[]{:S(2)}) collective-permute-start(bf16[48,1152]{1,0:T(8,128)(2,1)S(1)} %get-tuple-element.77), channel_id=1, source_target_pairs={{0,2},{1,3},{2,0},{3,1},{4,6},{5,7},{6,4},{7,5},{8,10},{9,11},{10,... | collective-permute-start | bytes 331784 | tf_op jit(solution)/shard_map/ppermute | solution.py:457
  175.7 10.9 %collective-permute-start.23 = (bf16[48,1152]{1,0:T(8,128)(2,1)S(1)}, bf16[48,1152]{1,0:T(8,128)(2,1)S(1)}, u32[]{:S(2)}, u32[]{:S(2)}) collective-permute-start(bf16[48,1152]{1,0:T(8,128)(2,1)S(1)} %get-tuple-element.78), channel_id=1, source_target_pairs={{0,3},{1,0},{2,1},{3,2},{4,7},{5,4},{6,5},{7,6},{8,11},{9,8},{10,9... | collective-permute-start | bytes 331784 | tf_op jit(solution)/shard_map/ppermute | solution.py:457
  187.8 12.7 %copy-start.26 = (bf16[192]{0:T(256)(128)(2,1)S(1)}, bf16[192]{0:T(256)(128)(2,1)}, u32[]{:S(2)}) copy-start(bf16[192]{0:T(256)(128)(2,1)} %param.14) | copy-start | bytes 1156
  187.8 12.9 %copy-start.2 = (bf16[192,2304]{1,0:T(8,128)(2,1)S(1)}, bf16[192,2304]{1,0:T(8,128)(2,1)}, u32[]{:S(2)}) copy-start(bf16[192,2304]{1,0:T(8,128)(2,1)} %refs_3_.6) | copy-start | bytes 2654212
  187.8 12.9 %collective-permute-start.32 = (bf16[2,2,48,2176]{3,2,1,0:T(8,128)(2,1)S(1)}, bf16[2,2,48,2176]{3,2,1,0:T(8,128)(2,1)}, u32[]{:S(2)}, u32[]{:S(2)}) collective-permute-start(bf16[2,2,48,2176]{3,2,1,0:T(8,128)(2,1)S(1)} %join.9.refs_2_.refs_1_), channel_id=1, source_target_pairs={{0,4},{4,0},{8,12},{12,8},{16,20},{20,16},{24,28},{28,24},{1,5},{5... | collective-permute-start | bytes 2506760 | tf_op jit(solution)/shard_map/ppermute | solution.py:454
  188.4 3.9 %collective-permute-start.28 = (bf16[48,1152]{1,0:T(8,128)(2,1)S(1)}, bf16[48,1152]{1,0:T(8,128)(2,1)S(1)}, u32[]{:S(2)}, u32[]{:S(2)}) collective-permute-start(bf16[48,1152]{1,0:T(8,128)(2,1)S(1)} %sum_pieces.3.refs_2_.refs_0_), channel_id=1, source_target_pairs={{0,16},{4,12},{8,24},{12,4},{16,0},{20,28},{24,8},{28,20},{1,17},{... | collective-permute-start | bytes 331784 | tf_op jit(solution)/shard_map/ppermute | solution.py:454
  192.9 5.1 %collective-permute-start.30 = (bf16[2,48,1152]{2,1,0:T(8,128)(2,1)S(1)}, bf16[2,48,1152]{2,1,0:T(8,128)(2,1)S(1)}, u32[]{:S(2)}, u32[]{:S(2)}) collective-permute-start(bf16[2,48,1152]{2,1,0:T(8,128)(2,1)S(1)} %join.10.refs_0_.refs_4_), channel_id=1, source_target_pairs={{0,8},{4,20},{8,0},{12,28},{16,24},{20,4},{24,16},{28,12},{1,9},{5... | collective-permute-start | bytes 663560 | tf_op jit(solution)/shard_map/ppermute | solution.py:454
  198.6 5.4 %collective-permute-start.31 = (bf16[2,2,48,1152]{3,2,1,0:T(8,128)(2,1)S(1)}, bf16[2,2,48,1152]{3,2,1,0:T(8,128)(2,1)}, u32[]{:S(2)}, u32[]{:S(2)}) collective-permute-start(bf16[2,2,48,1152]{3,2,1,0:T(8,128)(2,1)S(1)} %join.11.refs_1_), channel_id=1, source_target_pairs={{0,4},{4,0},{8,12},{12,8},{16,20},{20,16},{24,28},{28,24},{1,5},{5... | collective-permute-start | bytes 1327112 | tf_op jit(solution)/shard_map/ppermute | solution.py:454
  (15 other events, 51.4 us)

commit v3 on v2

--- a/solution.py
+++ b/solution.py
@@ -154,7 +154,7 @@
 
 
 def attn_forward(groups, place, gains, cosine, sine, seg_col, seg_row, tok, own, *rest):
-    parts, (attn_in, qkv, mixed, lse, w_full) = rest[:4], rest[4:]
+    parts, (attn_in, qkv, mixed, lse, for_other, w_full) = rest[:4], rest[4:]
     assemble(groups, place, parts, own, w_full, QKV, 0)
     normed, _ = norm_parts(tok[...].astype(f32))
     attn_in[...] = (normed * gains[0:1, :]).astype(bf16)
@@ -200,9 +200,11 @@
         return kept
 
     lse[...] = lax.fori_loop(0, HEADS // 2, pair, jnp.zeros((length, PAIR), f32), unroll=2)
-
-
-def feed_forward(groups, place, gains, mixed, attn_in, tok, grad_out, own_in, own_out, own_down, *rest):
+    for_other[:, :D] = attn_in[...]
+    for_other[:, D:] = mixed[...]
+
+
+def feed_forward(groups, place, gains, mixed, tok, grad_out, own_in, own_out, own_down, *rest):
     parts, rest = rest[:4], rest[4:]
     output, middle_grad, mixed_grad, branch_grad, hidden, mlp_in, gate_up_grad, for_other = rest[:8]
     w_in, w_out, w_down, middle, act, slope, total = rest[8:]
@@ -266,7 +268,7 @@
 
     lax.fori_loop(0, D // 256, back, 0)
     start = 0
-    for whole in (hidden, mlp_in, mixed, attn_in):
+    for whole in (hidden, mlp_in):
         for_other[:, start : start + whole.shape[1]] = whole[...]
         start += whole.shape[1]
     for whole in (grad_out, gate_up_grad, branch_grad):
@@ -275,8 +277,8 @@
         start += width
 
 
-HIDDEN, MLP_IN, MIXED, ATTN_IN, UPSTREAM, GATE_UP, BRANCH, SENT = (
-    0, FF, FF + D, FF + 2 * D, FF + 3 * D, FF + 3 * D + D // 2, 2 * FF + 3 * D + D // 2, 2 * FF + 4 * D
+HIDDEN, MLP_IN, UPSTREAM, GATE_UP, BRANCH, SENT = (
+    0, FF, FF + D, FF + D + D // 2, 2 * FF + D + D // 2, 2 * FF + 2 * D
 )
 
 
@@ -395,7 +397,12 @@
 
 
 def gain_grad(grad, weight, gain):
-    return jnp.sum(grad * weight.astype(f32), axis=1, keepdims=True) / gain
+    ones = jnp.ones((8, grad.shape[1]), f32)
+    summed = lax.dot_general(
+        ones, grad * weight.astype(f32), (((1,), (1,)), ((), ())),
+        precision=lax.Precision.HIGHEST, preferred_element_type=f32,
+    )
+    return summed[0:1, :] / gain
 
 
 def place_mlp(place, gain, here, other, weight, in_grad, out_grad, down_grad, gain_out):
@@ -438,6 +445,10 @@
             start += width
 
 
+def keep_copy(place, given, out):
+    out[...] = given[...]
+
+
 def join(place, near, got, out):
     out[0] = near[...]
     out[1] = got[...]
@@ -536,21 +547,24 @@
             axis=1,
         )
 
+        mlp_here = joined(mlp_stack, across(mlp_stack, swap_high), qkv_parts[3:])
         rope = [cosine, sine, seg_col, seg_row]
-        attn_in, qkv, mixed, lse = run(
+        attn_in, qkv, mixed, lse, attn_sent = run(
             functools.partial(attn_forward, groups), "attn_forward",
-            [shape((length, D)), shape((length, 3 * D)), shape((length, D)), shape((length, PAIR), f32)],
+            [shape((length, D)), shape((length, 3 * D)), shape((length, D)), shape((length, PAIR), f32), shape((length, 2 * D))],
             place, [gains] + rope + [tokens, w_qkv] + qkv_parts,
-            [pltpu.VMEM((D, 3 * D), bf16)], [mlp_stack],
-        )
-        mlp_parts = spread(mlp_stack, [mixed])
+            [pltpu.VMEM((D, 3 * D), bf16)], [mlp_here],
+        )
+        low = across(mlp_here, swap_low)
+        (low,) = run(keep_copy, "keep_copy", [shape(low.shape)], place, [low], (), [mixed])
+        mlp_parts = [mlp_here, low, across(mlp_here, swap_core), across(low, swap_core)]
         output, middle_grad, mixed_grad, branch_grad, hidden, mlp_in, gate_up_grad, for_other = run(
             functools.partial(feed_forward, groups), "feed_forward",
             [
                 shape((length, D)), shape((length, D), f32), shape((length, D)), shape((length, D)),
                 shape((length, FF)), shape((length, D)), shape((length, 2 * FF)), shape((length, SENT)),
             ],
-            place, [gains, mixed, attn_in, tokens, grad_out, w_in, w_out, w_down] + mlp_parts,
+            place, [gains, mixed, tokens, grad_out, w_in, w_out, w_down] + mlp_parts,
             [
                 pltpu.VMEM((D, 2 * FF), bf16), pltpu.VMEM((D, D), bf16), pltpu.VMEM((FF, D), bf16),
                 pltpu.VMEM((length, D), f32), pltpu.VMEM((length, FF), f32), pltpu.VMEM((length, FF), f32),
@@ -559,20 +573,21 @@
         )
         from_other = across(for_other, swap_core)
 
+        attn_other = across(attn_sent, swap_core)
+        down_keep, down_got = grad_self(
+            [hidden, grad_out, from_other], [(0, (2, HIDDEN), 1, (2, UPSTREAM))], 144
+        )
+        rest_keep, rest_got = grad_self(
+            [mlp_in, gate_up_grad, mixed, branch_grad, from_other, attn_other],
+            [(0, (4, MLP_IN), 1, (4, GATE_UP)), (2, (5, D), 3, (4, BRANCH))], 96, [down_keep],
+        )
         qkv_grad, qkv_send = run(
             attn_backward, "attn_backward", [shape((length, 3 * D)), shape((length, QKV))],
-            place, [qkv, lse, mixed_grad] + rope,
+            place, [qkv, lse, mixed_grad] + rope, (), [rest_keep],
         )
         qkv_other = across(qkv_send, swap_core)
-        down_keep, down_got = grad_self(
-            [hidden, grad_out, from_other], [(0, (2, HIDDEN), 1, (2, UPSTREAM))], 144, [qkv_send]
-        )
-        rest_keep, rest_got = grad_self(
-            [mlp_in, gate_up_grad, mixed, branch_grad, from_other],
-            [(0, (4, MLP_IN), 1, (4, GATE_UP)), (2, (4, MIXED), 3, (4, BRANCH))], 96, [down_keep],
-        )
         qkv_keep, qkv_got = grad_self(
-            [attn_in, qkv_grad, from_other, qkv_other], [(0, (2, ATTN_IN), 1, (3, 0))], 96, [rest_keep]
+            [attn_in, qkv_grad, attn_other, qkv_other], [(0, (2, 0), 1, (3, 0))], 96
         )
         mlp_keep, mlp_send = run(
             functools.partial(split_mlp, groups), "split_mlp", [shape((groups, ROWS, MLP))] * 2, place,
@@ -593,25 +608,26 @@
         mlp_mine, mlp_others = owners(mlp_keep, mlp_got, [qkv_keep])
         qkv_mine, qkv_others = owners(qkv_keep, qkv_got, [mlp_mine])
         mlp_sum = summed(mlp_mine, mlp_others, [qkv_mine])
-        mlp_pair = joined(mlp_sum, across(mlp_sum, swap_low))
-        qkv_sum = summed(qkv_mine, qkv_others, [mlp_pair])
-        mlp_quarters = joined(mlp_pair, across(mlp_pair, swap_high), [qkv_sum])
-        qkv_pair = joined(qkv_sum, across(qkv_sum, swap_low), [mlp_quarters])
-        qkv_quarters = joined(qkv_pair, across(qkv_pair, swap_high))
+        qkv_sum = summed(qkv_mine, qkv_others, [mlp_sum])
+        mlp_pair = joined(mlp_sum, across(mlp_sum, swap_low), [qkv_sum])
+        qkv_pair = joined(qkv_sum, across(qkv_sum, swap_low), [mlp_pair])
+        mlp_quarters = joined(mlp_pair, across(mlp_pair, swap_high), [qkv_pair])
+        qkv_got = across(qkv_pair, swap_high)
         shard = w_in.shape[0]
         in_grad, out_grad, down_grad, gain_two_grad = run(
             place_mlp, "place_mlp",
-            [shape((shard, 2 * FF), f32), shape((shard, D), f32), shape((w_down.shape[0], D), f32), shape((shard, 1), f32)],
-            place, [g_mlp.astype(f32)[:, None], mlp_quarters, across(mlp_quarters, swap_core), w_in],
+            [shape((shard, 2 * FF), f32), shape((shard, D), f32), shape((w_down.shape[0], D), f32), shape((1, shard), f32)],
+            place, [g_mlp.astype(f32)[None, :], mlp_quarters, across(mlp_quarters, swap_core), w_in],
             (), [qkv_pair],
         )
+        qkv_quarters = joined(qkv_pair, qkv_got, [in_grad])
         qkv_weight_grad, gain_one_grad = run(
-            place_qkv, "place_qkv", [shape((shard, 3 * D), f32), shape((shard, 1), f32)], place,
-            [g_attn.astype(f32)[:, None], qkv_quarters, across(qkv_quarters, swap_core), w_qkv],
+            place_qkv, "place_qkv", [shape((shard, 3 * D), f32), shape((1, shard), f32)], place,
+            [g_attn.astype(f32)[None, :], qkv_quarters, across(qkv_quarters, swap_core), w_qkv],
             (), [in_grad],
         )
         return (
-            output, tokens_grad, gain_one_grad[:, 0], qkv_weight_grad, out_grad, gain_two_grad[:, 0], in_grad, down_grad,
+            output, tokens_grad, gain_one_grad[0], qkv_weight_grad, out_grad, gain_two_grad[0], in_grad, down_grad,
         )
 
     return on_device

time: 211 us -> 198 us (0.938)
  waiting for transfers between devices: 106 us -> 95.1 us
  other arithmetic: 5.95 us -> 3.02 us
    ppermute x21 -> x22, waiting for transfers between devices: 61.8 us -> 50.9 us  [across(): return lax.ppermute(a, 'replica', perm)]
    pallas_call x2 -> x0, other arithmetic: 2.25 us -> none  [run(): pl.pallas_call(inner, out_shape=outs, in_specs=[SMEM] + [VMEM] * count +...]
    ppermute x21 -> x22, starting transfers between devices: 19.8 us -> 21.4 us  [across(): return lax.ppermute(a, 'replica', perm)]
    unnamed x57 -> x61, local copies, waits for them, and re-layouts: 8.85 us -> 9.97 us
    pallas_call x23 -> x24, Pallas kernels: 53.7 us -> 54.1 us  [run(): pl.pallas_call(inner, out_shape=outs, in_specs=[SMEM] + [VMEM] * count +...]
  transfers between devices with their start and end apart: 33 -> 34, of which waited for: 22 -> 24; matrix products, arithmetic and copies ran while one was open for 2% -> 2% of each run, Pallas kernels for 14% -> 17%
where the time goes in v3:
time: 198 us; the launch traced here: 197 us
  waiting for transfers between devices  95.1 us (48%)
  Pallas kernels  54.1 us (27%)
  starting transfers between devices  31.2 us (16%)
  local copies, waits for them, and re-layouts  12.9 us (7%)
  other arithmetic  3.02 us (2%)
    pallas_call x24, Pallas kernels, run(): pl.pallas_call(inner, out_shape=outs, in_specs=[SMEM] + [VMEM] * count +...  54.1 us
    ppermute x22, waiting for transfers between devices, across(): return lax.ppermute(a, 'replica', perm)  50.9 us
    ppermute x12, waiting for transfers between devices, shifted(): lax.ppermute(a, 'group', [(i, (i + k) % groups) for i in range(groups)])  44.2 us
    ppermute x22, starting transfers between devices, across(): return lax.ppermute(a, 'replica', perm)  21.4 us
    unnamed x61, local copies, waits for them, and re-layouts  9.97 us
    ppermute x12, starting transfers between devices, shifted(): lax.ppermute(a, 'group', [(i, (i + k) % groups) for i in range(groups)])  9.81 us
  transfers between devices with their start and end apart: 34, of which 24 were waited for; matrix products, arithmetic and copies ran while one was open for 2% of the time, Pallas kernels for 17%

profile of v3, /device:TPU:9, one launch (start us, length us, event | category | flops | bytes accessed | tf_op | source)
XLA Modules:
  0.0 197.5 jit_solution(5185406722469135223)
XLA Ops:
  2.3 1.3 collective-permute-start
  3.7 1.1 collective-permute-start.1
  4.8 1.4 collective-permute-start.2
  9.5 4.1 %collective-permute-done.1.refs_1_ = bf16[48,1280]{1,0:T(8,128)(2,1)S(1)} collective-permute-done((bf16[48,1280]{1,0:T(8,128)(2,1)S(1)}, bf16[48,1280]{1,0:T(8,128)(2,1)S(1)}, u32[]{:S(2)}, u32[]{:S(2)}) %collective-permute-start.1) | collective-permute-done | bytes 122912 | tf_op jit(solution)/shard_map/ppermute | solution.py:468
  13.6 2.8 %collective-permute-done.2.refs_2_ = bf16[48,1280]{1,0:T(8,128)(2,1)S(1)} collective-permute-done((bf16[48,1280]{1,0:T(8,128)(2,1)S(1)}, bf16[48,1280]{1,0:T(8,128)(2,1)S(1)}, u32[]{:S(2)}, u32[]{:S(2)}) %collective-permute-start.2) | collective-permute-done | bytes 122912 | tf_op jit(solution)/shard_map/ppermute | solution.py:468
  17.0 1.3 collective-permute-start.3
  18.4 5.9 %collective-permute-done.4.refs_2_.refs_0_ = bf16[48,2176]{1,0:T(8,128)(2,1)S(1)} collective-permute-done((bf16[48,2176]{1,0:T(8,128)(2,1)S(1)}, bf16[48,2176]{1,0:T(8,128)(2,1)S(1)}, u32[]{:S(2)}, u32[]{:S(2)}) %collective-permute-start.4) | collective-permute-done | bytes 208928 | tf_op jit(solution)/shard_map/ppermute | solution.py:468
  24.9 2.3 %collective-permute-start.5 = (bf16[2,3,48,1152]{3,2,1,0:T(8,128)(2,1)S(1)}, bf16[2,3,48,1152]{3,2,1,0:T(8,128)(2,1)S(1)}, u32[]{:S(2)}, u32[]{:S(2)}) collective-permute-start(bf16[2,3,48,1152]{3,2,1,0:T(8,128)(2,1)S(1)} %join.6.refs_7_.refs_5_), channel_id=1, source_target_pairs={{0,16},{4,12},{8,24},{12,4},{16,0},{20,28},{24,8},{28,20},{1,17},{... | collective-permute-start | bytes 1990664 | tf_op jit(solution)/shard_map/ppermute | solution.py:465
  27.2 1.3 collective-permute-start.8
  28.5 7.0 %collective-permute-done.5.refs_3_.refs_8_.refs_6_ = bf16[2,3,48,1152]{3,2,1,0:T(8,128)(2,1)S(1)} collective-permute-done((bf16[2,3,48,1152]{3,2,1,0:T(8,128)(2,1)S(1)}, bf16[2,3,48,1152]{3,2,1,0:T(8,128)(2,1)S(1)}, u32[]{:S(2)}, u32[]{:S(2)}) %collective-permute-start.5) | collective-permute-done | bytes 663584 | tf_op jit(solution)/shard_map/ppermute | solution.py:465
  35.5 1.8 collective-permute-start.7
  37.3 4.9 %collective-permute-done.8.refs_1_ = bf16[48,2176]{1,0:T(8,128)(2,1)S(1)} collective-permute-done((bf16[48,2176]{1,0:T(8,128)(2,1)S(1)}, bf16[48,2176]{1,0:T(8,128)(2,1)S(1)}, u32[]{:S(2)}, u32[]{:S(2)}) %collective-permute-start.8) | collective-permute-done | bytes 208928 | tf_op jit(solution)/shard_map/ppermute | solution.py:468
  42.2 1.2 collective-permute-done.9.refs_2_
  45.0 8.6 %collective-permute-done.10.refs_1_ = bf16[3,48,2176]{2,1,0:T(8,128)(2,1)S(1)} collective-permute-done((bf16[3,48,2176]{2,1,0:T(8,128)(2,1)S(1)}, bf16[3,48,2176]{2,1,0:T(8,128)(2,1)S(1)}, u32[]{:S(2)}, u32[]{:S(2)}) %collective-permute-start.10) | collective-permute-done | bytes 626720 | tf_op jit(solution)/shard_map/ppermute | solution.py:465
  56.3 2.0 collective-permute-start.12
  64.1 7.8 %attn_forward.1 = (bf16[256,768]{1,0:T(8,128)(2,1)S(1)}, bf16[256,2304]{1,0:T(8,128)(2,1)S(1)}, bf16[256,768]{1,0:T(8,128)(2,1)S(1)}, f32[256,128]{1,0:T(8,128)S(1)}, bf16[256,1536]{1,0:T(8,128)(2,1)S(1)}) custom-call(s32[4]{0:T(128)S(1)} %pad_add_fusion.place, f32[2,768]{1,0:T(2,128)S(1)} %pad_maximum_fusion.4.refs_0_.refs_2_, f32[256,128]{1,0:T(8,128)S(1)} %copy-done.12, ...), custom_call_target="tpu_custom_call" | custom-call | tf_op jit(solution)/shard_map/attn_forward/pallas_call | solution.py:39
  72.0 1.6 keep_copy.1.refs_8_
  73.5 1.3 collective-permute-start.13
  74.9 2.6 %collective-permute-done.13.refs_10_ = bf16[2,3,48,2176]{3,2,1,0:T(8,128)(2,1)S(1)} collective-permute-done((bf16[2,3,48,2176]{3,2,1,0:T(8,128)(2,1)S(1)}, bf16[2,3,48,2176]{3,2,1,0:T(8,128)(2,1)S(1)}, u32[]{:S(2)}, u32[]{:S(2)}) %collective-permute-start.13) | collective-permute-done | bytes 1253408 | tf_op jit(solution)/shard_map/ppermute | solution.py:465
  78.5 10.9 %feed_forward.1 = (bf16[256,768]{1,0:T(8,128)(2,1)}, f32[256,768]{1,0:T(8,128)S(1)}, bf16[256,768]{1,0:T(8,128)(2,1)S(1)}, bf16[256,768]{1,0:T(8,128)(2,1)S(1)},...) custom-call(s32[4]{0:T(128)S(1)} %pad_add_fusion.place, ...), custom_call_target="tpu_custom_call" | custom-call | tf_op jit(solution)/shard_map/feed_forward/pallas_call | solution.py:39
  89.9 4.8 %collective-permute-done.14.refs_2_.refs_4_ = bf16[256,3840]{1,0:T(8,128)(2,1)S(1)} collective-permute-done((bf16[256,3840]{1,0:T(8,128)(2,1)}, bf16[256,3840]{1,0:T(8,128)(2,1)S(1)}, u32[]{:S(2)}, u32[]{:S(2)}) %collective-permute-start.14) | collective-permute-done | bytes 1966112 | tf_op jit(solution)/shard_map/ppermute | solution.py:465
  94.7 1.7 grad_for_self.3
  96.4 3.5 %grad_for_self.4 = (bf16[4,96,1536]{2,1,0:T(8,128)(2,1)S(1)}, bf16[4,96,1536]{2,1,0:T(8,128)(2,1)S(1)}) custom-call(s32[4]{0:T(128)S(1)} %pad_add_fusion.place, bf16[256,768]{1,0:T(8,128)(2,1)S(1)} %get-tuple-element.56.refs_0_, bf16[256,2304]{1,0:T(8,128)(2,1)S(1)} %get-tuple-element.57.refs_1_, bf16[256,768]{1,0:T(8,128)(2,1)S(1)} %get-tuple-element.51.refs_1_.refs_2_, ...), custom_call_target="tpu_custom_call" | custom-call | tf_op jit(solution)/shard_map/grad_for_self/pallas_call | solution.py:39
  100.8 6.4 %attn_backward.1 = (bf16[256,2304]{1,0:T(8,128)(2,1)S(1)}, bf16[256,1152]{1,0:T(8,128)(2,1)S(1)}) custom-call(s32[4]{0:T(128)S(1)} %pad_add_fusion.place, bf16[256,2304]{1,0:T(8,128)(2,1)S(1)} %get-tuple-element.53.refs_0_, f32[256,128]{1,0:T(8,128)S(1)} %get-tuple-element.54.refs_1_, bf16[256,768]{1,0:T(8,128)(2,1)S(1)} %get-tuple-element.55.refs_2_, ...), custom_call_target="tpu_custom_call" | custom-call | tf_op jit(solution)/shard_map/attn_backward/pallas_call | solution.py:39
  108.0 1.2 collective-permute-start.16
  109.6 2.6 %grad_for_self.5 = (bf16[4,96,1152]{2,1,0:T(8,128)(2,1)S(1)}, bf16[4,96,1152]{2,1,0:T(8,128)(2,1)S(1)}) custom-call(s32[4]{0:T(128)S(1)} %pad_add_fusion.place, bf16[256,768]{1,0:T(8,128)(2,1)S(1)} %copy-done.24, bf16[256,2304]{1,0:T(8,128)(2,1)S(1)} %get-tuple-element.64.refs_1_.refs_0_, bf16[256,1536]{1,0:T(8,128)(2,1)S(1)} %collective-permute-done.15.refs_5_.refs_2_, ...), custom_call_target="tpu_custom_call" | custom-call | tf_op jit(solution)/shard_map/grad_for_self/pallas_call | solution.py:39
  112.2 1.3 collective-permute-start.19
  113.5 6.5 %collective-permute-done.16.refs_1_ = bf16[4,144,384]{2,1,0:T(8,128)(2,1)S(1)} collective-permute-done((bf16[4,144,384]{2,1,0:T(8,128)(2,1)S(1)}, bf16[4,144,384]{2,1,0:T(8,128)(2,1)S(1)}, u32[]{:S(2)}, u32[]{:S(2)}) %collective-permute-start.16) | collective-permute-done | bytes 442400 | tf_op jit(solution)/shard_map/ppermute | solution.py:465
  121.9 3.8 %attn_in_backward.1.refs_2_ = bf16[256,768]{1,0:T(8,128)(2,1)} custom-call(s32[4]{0:T(128)S(1)} %pad_add_fusion.place, bf16[256,2304]{1,0:T(8,128)(2,1)S(1)} %get-tuple-element.64.refs_1_.refs_0_, f32[256,768]{1,0:T(8,128)S(1)} %copy-done.21, f32[2,768]{1,0:T(2,128)S(1)} %pad_maximum_fusion.4.refs_0_.refs_2_, bf16[256,768]{1,0:T(8,128)(2,1)S(1)} %copy-done.10, ...), custom_call_target="tpu_custom_call" | custom-call | tf_op jit(solution)/shard_map/attn_in_backward/pallas_call | solution.py:39
  125.8 7.8 %collective-permute-done.19.refs_1_ = bf16[4,96,1152]{2,1,0:T(8,128)(2,1)S(1)} collective-permute-done((bf16[4,96,1152]{2,1,0:T(8,128)(2,1)S(1)}, bf16[4,96,1152]{2,1,0:T(8,128)(2,1)S(1)}, u32[]{:S(2)}, u32[]{:S(2)}) %collective-permute-start.19) | collective-permute-done | bytes 884768 | tf_op jit(solution)/shard_map/ppermute | solution.py:465
  136.1 2.9 %collective-permute-done.21.refs_1_ = bf16[4,48,2176]{2,1,0:T(8,128)(2,1)S(1)} collective-permute-done((bf16[4,48,2176]{2,1,0:T(8,128)(2,1)S(1)}, bf16[4,48,2176]{2,1,0:T(8,128)(2,1)S(1)}, u32[]{:S(2)}, u32[]{:S(2)}) %collective-permute-start.21) | collective-permute-done | bytes 835616 | tf_op jit(solution)/shard_map/ppermute | solution.py:465
  139.8 1.6 collective-permute-start.26
  141.5 1.4 collective-permute-start.27
  142.9 1.2 collective-permute-done.20.refs_1_
  145.4 11.5 %collective-permute-done.26.refs_2_ = bf16[48,2176]{1,0:T(8,128)(2,1)S(1)} collective-permute-done((bf16[48,2176]{1,0:T(8,128)(2,1)S(1)}, bf16[48,2176]{1,0:T(8,128)(2,1)S(1)}, u32[]{:S(2)}, u32[]{:S(2)}) %collective-permute-start.26) | collective-permute-done | bytes 208928 | tf_op jit(solution)/shard_map/ppermute | solution.py:468
  156.9 3.6 %collective-permute-done.27.refs_3_ = bf16[48,2176]{1,0:T(8,128)(2,1)S(1)} collective-permute-done((bf16[48,2176]{1,0:T(8,128)(2,1)S(1)}, bf16[48,2176]{1,0:T(8,128)(2,1)S(1)}, u32[]{:S(2)}, u32[]{:S(2)}) %collective-permute-start.27) | collective-permute-done | bytes 208928 | tf_op jit(solution)/shard_map/ppermute | solution.py:468
  162.2 1.5 collective-permute-start.24
  163.6 3.0 %collective-permute-done.22.refs_1_ = bf16[48,1152]{1,0:T(8,128)(2,1)S(1)} collective-permute-done((bf16[48,1152]{1,0:T(8,128)(2,1)S(1)}, bf16[48,1152]{1,0:T(8,128)(2,1)S(1)}, u32[]{:S(2)}, u32[]{:S(2)}) %collective-permute-start.22) | collective-permute-done | bytes 110624 | tf_op jit(solution)/shard_map/ppermute | solution.py:468
  166.6 5.2 %collective-permute-done.23.refs_2_ = bf16[48,1152]{1,0:T(8,128)(2,1)S(1)} collective-permute-done((bf16[48,1152]{1,0:T(8,128)(2,1)S(1)}, bf16[48,1152]{1,0:T(8,128)(2,1)S(1)}, u32[]{:S(2)}, u32[]{:S(2)}) %collective-permute-start.23) | collective-permute-done | bytes 110624 | tf_op jit(solution)/shard_map/ppermute | solution.py:468
  171.9 1.4 collective-permute-done.24.refs_3_
  175.9 4.3 %collective-permute-done.28.refs_1_ = bf16[48,1152]{1,0:T(8,128)(2,1)S(1)} collective-permute-done((bf16[48,1152]{1,0:T(8,128)(2,1)S(1)}, bf16[48,1152]{1,0:T(8,128)(2,1)S(1)}, u32[]{:S(2)}, u32[]{:S(2)}) %collective-permute-start.28) | collective-permute-done | bytes 110624 | tf_op jit(solution)/shard_map/ppermute | solution.py:465
  180.8 2.0 %collective-permute-done.31.refs_1_ = bf16[2,48,2176]{2,1,0:T(8,128)(2,1)S(1)} collective-permute-done((bf16[2,48,2176]{2,1,0:T(8,128)(2,1)S(1)}, bf16[2,48,2176]{2,1,0:T(8,128)(2,1)S(1)}, u32[]{:S(2)}, u32[]{:S(2)}) %collective-permute-start.31) | collective-permute-done | bytes 417824 | tf_op jit(solution)/shard_map/ppermute | solution.py:465
  183.5 1.3 collective-permute-start.32
  185.4 1.3 collective-permute-done.32.refs_2_
  186.7 3.9 %place_mlp.1 = (f32[192,2304]{1,0:T(8,128)}, f32[192,768]{1,0:T(8,128)}, f32[288,768]{1,0:T(8,128)}, f32[1,192]{1,0:T(1,128)}) custom-call(s32[4]{0:T(128)S(1)} %pad_add_fusion.place, f32[1,192]{1,0:T(1,128)S(1)} %bitcast.39, bf16[2,2,48,2176]{3,2,1,0:T(8,128)(2,1)S(1)} %join.10.refs_1_, bf16[2,2,48,2176]{3,2,1,0:T(8,128)(2,1)S(1)} %collective-permute-done.32.refs_2_, ...), custom_call_target="tpu_custom_call" | custom-call | tf_op jit(solution)/shard_map/place_mlp/pallas_call | solution.py:39
  190.6 1.5 copy-done.1
  193.1 1.4 collective-permute-done.33.refs_2_
  194.5 2.9 %place_qkv.1 = (f32[192,2304]{1,0:T(8,128)}, f32[1,192]{1,0:T(1,128)}) custom-call(s32[4]{0:T(128)S(1)} %pad_add_fusion.place, f32[1,192]{1,0:T(1,128)S(1)} %bitcast.40, bf16[2,2,48,1152]{3,2,1,0:T(8,128)(2,1)S(1)} %join.11.refs_1_, bf16[2,2,48,1152]{3,2,1,0:T(8,128)(2,1)S(1)} %collective-permute-done.33.refs_2_, bf16[192,2304]{1,0:T(8,128)(2,1)S(1)} %copy-done, ...), custom_call_target="tpu_custom_call" | custom-call | tf_op jit(solution)/shard_map/place_qkv/pallas_call | solution.py:39
  (134 shorter events, 33.8 us)
Async XLA Ops:
  2.3 7.2 %collective-permute-start = (bf16[48,1280]{1,0:T(8,128)(2,1)S(1)}, bf16[48,1280]{1,0:T(8,128)(2,1)S(1)}, u32[]{:S(2)}, u32[]{:S(2)}) collective-permute-start(bf16[48,1280]{1,0:T(8,128)(2,1)S(1)} %pad_maximum_fusion.3), channel_id=1, source_target_pairs={{0,1},{1,2},{2,3},{3,0},{4,5},{5,6},{6,7},{7,4},{8,9},{9,10},{10,1... | collective-permute-start | bytes 368648 | tf_op jit(solution)/shard_map/ppermute | solution.py:468
  3.7 9.9 %collective-permute-start.1 = (bf16[48,1280]{1,0:T(8,128)(2,1)S(1)}, bf16[48,1280]{1,0:T(8,128)(2,1)S(1)}, u32[]{:S(2)}, u32[]{:S(2)}) collective-permute-start(bf16[48,1280]{1,0:T(8,128)(2,1)S(1)} %pad_maximum_fusion.3), channel_id=1, source_target_pairs={{0,2},{1,3},{2,0},{3,1},{4,6},{5,7},{6,4},{7,5},{8,10},{9,11},{10,... | collective-permute-start | bytes 368648 | tf_op jit(solution)/shard_map/ppermute | solution.py:468
  4.8 11.6 %collective-permute-start.2 = (bf16[48,1280]{1,0:T(8,128)(2,1)S(1)}, bf16[48,1280]{1,0:T(8,128)(2,1)S(1)}, u32[]{:S(2)}, u32[]{:S(2)}) collective-permute-start(bf16[48,1280]{1,0:T(8,128)(2,1)S(1)} %pad_maximum_fusion.3), channel_id=1, source_target_pairs={{0,3},{1,0},{2,1},{3,2},{4,7},{5,4},{6,5},{7,6},{8,11},{9,8},{10,9... | collective-permute-start | bytes 368648 | tf_op jit(solution)/shard_map/ppermute | solution.py:468
  7.6 10.6 %dynamic-slice-start = ((bf16[192,2304]{1,0:T(8,128)(2,1)}, s32[]{:T(128)}, s32[]{:T(128)}), bf16[48,1152]{1,0:T(8,128)(2,1)S(1)}, s32[]{:S(2)}) async-start(bf16[192,2304]{1,0:T(8,128)(2,1)} %refs_3_.6, s32[]{:T(128)} %select_n.42, s32[]{:T(128)} %select_n.43), calls=%async_computation | async-start | bytes 221696 | tf_op jit(solution)/shard_map/dynamic_slice | solution.py:522
  8.3 10.0 %dynamic-slice-start.1 = ((bf16[192,768]{1,0:T(8,128)(2,1)}, s32[]{:T(128)}, s32[]{:T(128)}), bf16[48,384]{1,0:T(8,128)(2,1)S(1)}, s32[]{:S(2)}) async-start(bf16[192,768]{1,0:T(8,128)(2,1)} %refs_5_.3, s32[]{:T(128)} %select_n.42, s32[]{:T(128)} %select_n.49), calls=%async_computation.1 | async-start | bytes 74240 | tf_op jit(solution)/shard_map/dynamic_slice | solution.py:522
  9.5 14.8 %copy-start.11 = (f32[256,128]{1,0:T(8,128)}, f32[256,128]{1,0:T(8,128)S(1)}, u32[]{:S(2)}) copy-start(f32[256,128]{1,0:T(8,128)S(1)} %get-tuple-element.99.refs_3_.refs_1_) | copy-start | bytes 393220
  9.5 14.8 %copy-start.14 = (f32[256,128]{1,0:T(8,128)}, f32[256,128]{1,0:T(8,128)S(1)}, u32[]{:S(2)}) copy-start(f32[256,128]{1,0:T(8,128)S(1)} %get-tuple-element.100.refs_4_.refs_2_) | copy-start | bytes 393220
  17.0 7.3 %collective-permute-start.3 = (bf16[3,48,1152]{2,1,0:T(8,128)(2,1)S(1)}, bf16[3,48,1152]{2,1,0:T(8,128)(2,1)S(1)}, u32[]{:S(2)}, u32[]{:S(2)}) collective-permute-start(bf16[3,48,1152]{2,1,0:T(8,128)(2,1)S(1)} %get-tuple-element.50.refs_0_), channel_id=1, source_target_pairs={{0,8},{4,20},{8,0},{12,28},{16,24},{20,4},{24,16},{28,12},{1,9},{5... | collective-permute-start | bytes 995336 | tf_op jit(solution)/shard_map/ppermute | solution.py:465
  18.3 6.0 %collective-permute-start.4 = (bf16[48,2176]{1,0:T(8,128)(2,1)S(1)}, bf16[48,2176]{1,0:T(8,128)(2,1)S(1)}, u32[]{:S(2)}, u32[]{:S(2)}) collective-permute-start(bf16[48,2176]{1,0:T(8,128)(2,1)S(1)} %pad_maximum_fusion), channel_id=1, source_target_pairs={{0,1},{1,2},{2,3},{3,0},{4,5},{5,6},{6,7},{7,4},{8,9},{9,10},{10,1... | collective-permute-start | bytes 626696 | tf_op jit(solution)/shard_map/ppermute | solution.py:468
  24.9 10.6 %collective-permute-start.5 = (bf16[2,3,48,1152]{3,2,1,0:T(8,128)(2,1)S(1)}, bf16[2,3,48,1152]{3,2,1,0:T(8,128)(2,1)S(1)}, u32[]{:S(2)}, u32[]{:S(2)}) collective-permute-start(bf16[2,3,48,1152]{3,2,1,0:T(8,128)(2,1)S(1)} %join.6.refs_7_.refs_5_), channel_id=1, source_target_pairs={{0,16},{4,12},{8,24},{12,4},{16,0},{20,28},{24,8},{28,20},{1,17},{... | collective-permute-start | bytes 1990664 | tf_op jit(solution)/shard_map/ppermute | solution.py:465
  27.2 16.2 %collective-permute-start.6 = (bf16[2,3,48,1152]{3,2,1,0:T(8,128)(2,1)S(1)}, bf16[2,3,48,1152]{3,2,1,0:T(8,128)(2,1)S(1)}, u32[]{:S(2)}, u32[]{:S(2)}) collective-permute-start(bf16[2,3,48,1152]{3,2,1,0:T(8,128)(2,1)S(1)} %join.6.refs_7_.refs_5_), channel_id=1, source_target_pairs={{0,4},{4,0},{8,12},{12,8},{16,20},{20,16},{24,28},{28,24},{1,5},{5... | collective-permute-start | bytes 1990664 | tf_op jit(solution)/shard_map/ppermute | solution.py:465
  27.2 15.0 %collective-permute-start.8 = (bf16[48,2176]{1,0:T(8,128)(2,1)S(1)}, bf16[48,2176]{1,0:T(8,128)(2,1)S(1)}, u32[]{:S(2)}, u32[]{:S(2)}) collective-permute-start(bf16[48,2176]{1,0:T(8,128)(2,1)S(1)} %pad_maximum_fusion), channel_id=1, source_target_pairs={{0,2},{1,3},{2,0},{3,1},{4,6},{5,7},{6,4},{7,5},{8,10},{9,11},{10,... | collective-permute-start | bytes 626696 | tf_op jit(solution)/shard_map/ppermute | solution.py:468
  28.4 14.9 %collective-permute-start.9 = (bf16[48,2176]{1,0:T(8,128)(2,1)S(1)}, bf16[48,2176]{1,0:T(8,128)(2,1)S(1)}, u32[]{:S(2)}, u32[]{:S(2)}) collective-permute-start(bf16[48,2176]{1,0:T(8,128)(2,1)S(1)} %pad_maximum_fusion), channel_id=1, source_target_pairs={{0,3},{1,0},{2,1},{3,2},{4,7},{5,4},{6,5},{7,6},{8,11},{9,8},{10,9... | collective-permute-start | bytes 626696 | tf_op jit(solution)/shard_map/ppermute | solution.py:468
  35.5 18.1 %collective-permute-start.7 = (bf16[2,3,48,1152]{3,2,1,0:T(8,128)(2,1)S(1)}, bf16[2,3,48,1152]{3,2,1,0:T(8,128)(2,1)S(1)}, u32[]{:S(2)}, u32[]{:S(2)}) collective-permute-start(bf16[2,3,48,1152]{3,2,1,0:T(8,128)(2,1)S(1)} %collective-permute-done.5.refs_3_.refs_8_.refs_6_), channel_id=1, source_target_pairs={{0,4},{4,0},{8,12},{12,8},{16,20},{20,16},{24,28},{28,24},{1,5},{5... | collective-permute-start | bytes 1990664 | tf_op jit(solution)/shard_map/ppermute | solution.py:465
  44.2 11.1 %copy-start.26 = (s32[256]{0:T(256)S(1)}, s32[256]{0:T(256)}, u32[]{:S(2)}) copy-start(s32[256]{0:T(256)} %param.10) | copy-start | bytes 3076
  44.2 14.0 %copy-start = (bf16[192,2304]{1,0:T(8,128)(2,1)S(1)}, bf16[192,2304]{1,0:T(8,128)(2,1)}, u32[]{:S(2)}) copy-start(bf16[192,2304]{1,0:T(8,128)(2,1)} %refs_3_.7) | copy-start | bytes 2654212
  44.2 9.4 %collective-permute-start.10 = (bf16[3,48,2176]{2,1,0:T(8,128)(2,1)S(1)}, bf16[3,48,2176]{2,1,0:T(8,128)(2,1)S(1)}, u32[]{:S(2)}, u32[]{:S(2)}) collective-permute-start(bf16[3,48,2176]{2,1,0:T(8,128)(2,1)S(1)} %stack_pieces.3.refs_0_), channel_id=1, source_target_pairs={{0,8},{4,20},{8,0},{12,28},{16,24},{20,4},{24,16},{28,12},{1,9},{5... | collective-permute-start | bytes 1880072 | tf_op jit(solution)/shard_map/ppermute | solution.py:465
  54.5 17.4 %collective-permute-start.11 = (bf16[2,3,48,2176]{3,2,1,0:T(8,128)(2,1)S(1)}, bf16[2,3,48,2176]{3,2,1,0:T(8,128)(2,1)}, u32[]{:S(2)}, u32[]{:S(2)}) collective-permute-start(bf16[2,3,48,2176]{3,2,1,0:T(8,128)(2,1)S(1)} %join.7.refs_11_.refs_7_), channel_id=1, source_target_pairs={{0,16},{4,12},{8,24},{12,4},{16,0},{20,28},{24,8},{28,20},{1,17},{... | collective-permute-start | bytes 3760136 | tf_op jit(solution)/shard_map/ppermute | solution.py:465
  56.3 18.6 %collective-permute-start.12 = (bf16[2,3,48,2176]{3,2,1,0:T(8,128)(2,1)S(1)}, bf16[2,3,48,2176]{3,2,1,0:T(8,128)(2,1)S(1)}, u32[]{:S(2)}, u32[]{:S(2)}) collective-permute-start(bf16[2,3,48,2176]{3,2,1,0:T(8,128)(2,1)S(1)} %join.7.refs_11_.refs_7_), channel_id=1, source_target_pairs={{0,4},{4,0},{8,12},{12,8},{16,20},{20,16},{24,28},{28,24},{1,5},{5... | collective-permute-start | bytes 3760136 | tf_op jit(solution)/shard_map/ppermute | solution.py:465
  71.9 6.6 %copy-start.8 = (bf16[192,2304]{1,0:T(8,128)(2,1)S(1)}, bf16[192,2304]{1,0:T(8,128)(2,1)}, u32[]{:S(2)}) copy-start(bf16[192,2304]{1,0:T(8,128)(2,1)} %refs_3_.6) | copy-start | bytes 2654212
  71.9 6.6 %copy-start.10 = (bf16[256,768]{1,0:T(8,128)(2,1)S(1)}, bf16[256,768]{1,0:T(8,128)(2,1)}, u32[]{:S(2)}) copy-start(bf16[256,768]{1,0:T(8,128)(2,1)} %refs_3_.5) | copy-start | bytes 1179652
  71.9 6.6 %copy-start.17 = (bf16[256,768]{1,0:T(8,128)(2,1)S(1)}, bf16[256,768]{1,0:T(8,128)(2,1)}, u32[]{:S(2)}) copy-start(bf16[256,768]{1,0:T(8,128)(2,1)} %refs_1_.1) | copy-start | bytes 1179652
  71.9 6.6 %copy-start.22 = (bf16[288,768]{1,0:T(8,128)(2,1)S(1)}, bf16[288,768]{1,0:T(8,128)(2,1)}, u32[]{:S(2)}) copy-start(bf16[288,768]{1,0:T(8,128)(2,1)} %refs_6_.3) | copy-start | bytes 1327108
  71.9 6.6 %copy-start.25 = (bf16[192,768]{1,0:T(8,128)(2,1)S(1)}, bf16[192,768]{1,0:T(8,128)(2,1)}, u32[]{:S(2)}) copy-start(bf16[192,768]{1,0:T(8,128)(2,1)} %refs_5_.3) | copy-start | bytes 884740
  73.5 3.9 %collective-permute-start.13 = (bf16[2,3,48,2176]{3,2,1,0:T(8,128)(2,1)S(1)}, bf16[2,3,48,2176]{3,2,1,0:T(8,128)(2,1)S(1)}, u32[]{:S(2)}, u32[]{:S(2)}) collective-permute-start(bf16[2,3,48,2176]{3,2,1,0:T(8,128)(2,1)S(1)} %keep_copy.1.refs_8_), channel_id=1, source_target_pairs={{0,4},{4,0},{8,12},{12,8},{16,20},{20,16},{24,28},{28,24},{1,5},{5... | collective-permute-start | bytes 3760136 | tf_op jit(solution)/shard_map/ppermute | solution.py:465
  89.4 7.0 %copy-start.20 = (f32[256,768]{1,0:T(8,128)}, f32[256,768]{1,0:T(8,128)S(1)}, u32[]{:S(2)}) copy-start(f32[256,768]{1,0:T(8,128)S(1)} %get-tuple-element.65.refs_1_) | copy-start | bytes 2359300
  89.4 5.3 %collective-permute-start.14 = (bf16[256,3840]{1,0:T(8,128)(2,1)}, bf16[256,3840]{1,0:T(8,128)(2,1)S(1)}, u32[]{:S(2)}, u32[]{:S(2)}) collective-permute-start(bf16[256,3840]{1,0:T(8,128)(2,1)} %get-tuple-element.59), channel_id=1, source_target_pairs={{0,4},{4,0},{8,12},{12,8},{16,20},{20,16},{24,28},{28,24},{1,5},{5... | collective-permute-start | bytes 5898248 | tf_op jit(solution)/shard_map/ppermute | solution.py:465
  89.8 6.6 %collective-permute-start.15 = (bf16[256,1536]{1,0:T(8,128)(2,1)S(1)}, bf16[256,1536]{1,0:T(8,128)(2,1)S(1)}, u32[]{:S(2)}, u32[]{:S(2)}) collective-permute-start(bf16[256,1536]{1,0:T(8,128)(2,1)S(1)} %get-tuple-element.60), channel_id=1, source_target_pairs={{0,4},{4,0},{8,12},{12,8},{16,20},{20,16},{24,28},{28,24},{1,5},{5... | collective-permute-start | bytes 2359304 | tf_op jit(solution)/shard_map/ppermute | solution.py:465
  99.9 20.2 %collective-permute-start.17 = (bf16[4,96,1536]{2,1,0:T(8,128)(2,1)S(1)}, bf16[4,96,1536]{2,1,0:T(8,128)(2,1)S(1)}, u32[]{:S(2)}, u32[]{:S(2)}) collective-permute-start(bf16[4,96,1536]{2,1,0:T(8,128)(2,1)S(1)} %get-tuple-element.67), channel_id=1, source_target_pairs={{0,8},{4,20},{8,0},{12,28},{16,24},{20,4},{24,16},{28,12},{1,9},{5... | collective-permute-start | bytes 3538952 | tf_op jit(solution)/shard_map/ppermute | solution.py:465
  100.8 8.8 %copy-start.24 = (bf16[256,768]{1,0:T(8,128)(2,1)S(1)}, bf16[256,768]{1,0:T(8,128)(2,1)}, u32[]{:S(2)}) copy-start(bf16[256,768]{1,0:T(8,128)(2,1)} %copy-done.23) | copy-start | bytes 1179652
  107.3 2.3 %collective-permute-start.18 = (bf16[256,1152]{1,0:T(8,128)(2,1)S(1)}, bf16[256,1152]{1,0:T(8,128)(2,1)S(1)}, u32[]{:S(2)}, u32[]{:S(2)}) collective-permute-start(bf16[256,1152]{1,0:T(8,128)(2,1)S(1)} %get-tuple-element.69), channel_id=1, source_target_pairs={{0,4},{4,0},{8,12},{12,8},{16,20},{20,16},{24,28},{28,24},{1,5},{5... | collective-permute-start | bytes 1769480 | tf_op jit(solution)/shard_map/ppermute | solution.py:465
  108.0 12.1 %collective-permute-start.16 = (bf16[4,144,384]{2,1,0:T(8,128)(2,1)S(1)}, bf16[4,144,384]{2,1,0:T(8,128)(2,1)S(1)}, u32[]{:S(2)}, u32[]{:S(2)}) collective-permute-start(bf16[4,144,384]{2,1,0:T(8,128)(2,1)S(1)} %get-tuple-element.66), channel_id=1, source_target_pairs={{0,8},{4,20},{8,0},{12,28},{16,24},{20,4},{24,16},{28,12},{1,9},{5... | collective-permute-start | bytes 1327112 | tf_op jit(solution)/shard_map/ppermute | solution.py:465
  112.2 21.3 %collective-permute-start.19 = (bf16[4,96,1152]{2,1,0:T(8,128)(2,1)S(1)}, bf16[4,96,1152]{2,1,0:T(8,128)(2,1)S(1)}, u32[]{:S(2)}, u32[]{:S(2)}) collective-permute-start(bf16[4,96,1152]{2,1,0:T(8,128)(2,1)S(1)} %get-tuple-element.72), channel_id=1, source_target_pairs={{0,8},{4,20},{8,0},{12,28},{16,24},{20,4},{24,16},{28,12},{1,9},{5... | collective-permute-start | bytes 2654216 | tf_op jit(solution)/shard_map/ppermute | solution.py:465
  121.1 18.0 %collective-permute-start.21 = (bf16[4,48,2176]{2,1,0:T(8,128)(2,1)S(1)}, bf16[4,48,2176]{2,1,0:T(8,128)(2,1)S(1)}, u32[]{:S(2)}, u32[]{:S(2)}) collective-permute-start(bf16[4,48,2176]{2,1,0:T(8,128)(2,1)S(1)} %get-tuple-element.75), channel_id=1, source_target_pairs={{0,16},{4,12},{8,24},{12,4},{16,0},{20,28},{24,8},{28,20},{1,17},{... | collective-permute-start | bytes 2506760 | tf_op jit(solution)/shard_map/ppermute | solution.py:465
  135.3 8.8 %collective-permute-start.20 = (bf16[4,48,1152]{2,1,0:T(8,128)(2,1)S(1)}, bf16[4,48,1152]{2,1,0:T(8,128)(2,1)S(1)}, u32[]{:S(2)}, u32[]{:S(2)}) collective-permute-start(bf16[4,48,1152]{2,1,0:T(8,128)(2,1)S(1)} %get-tuple-element.74), channel_id=1, source_target_pairs={{0,16},{4,12},{8,24},{12,4},{16,0},{20,28},{24,8},{28,20},{1,17},{... | collective-permute-start | bytes 1327112 | tf_op jit(solution)/shard_map/ppermute | solution.py:465
  139.8 5.6 %collective-permute-start.25 = (bf16[48,2176]{1,0:T(8,128)(2,1)S(1)}, bf16[48,2176]{1,0:T(8,128)(2,1)S(1)}, u32[]{:S(2)}, u32[]{:S(2)}) collective-permute-start(bf16[48,2176]{1,0:T(8,128)(2,1)S(1)} %get-tuple-element.81), channel_id=1, source_target_pairs={{0,1},{1,2},{2,3},{3,0},{4,5},{5,6},{6,7},{7,4},{8,9},{9,10},{10,1... | collective-permute-start | bytes 626696 | tf_op jit(solution)/shard_map/ppermute | solution.py:468
  139.8 17.1 %collective-permute-start.26 = (bf16[48,2176]{1,0:T(8,128)(2,1)S(1)}, bf16[48,2176]{1,0:T(8,128)(2,1)S(1)}, u32[]{:S(2)}, u32[]{:S(2)}) collective-permute-start(bf16[48,2176]{1,0:T(8,128)(2,1)S(1)} %get-tuple-element.82), channel_id=1, source_target_pairs={{0,2},{1,3},{2,0},{3,1},{4,6},{5,7},{6,4},{7,5},{8,10},{9,11},{10,... | collective-permute-start | bytes 626696 | tf_op jit(solution)/shard_map/ppermute | solution.py:468
  141.5 19.0 %collective-permute-start.27 = (bf16[48,2176]{1,0:T(8,128)(2,1)S(1)}, bf16[48,2176]{1,0:T(8,128)(2,1)S(1)}, u32[]{:S(2)}, u32[]{:S(2)}) collective-permute-start(bf16[48,2176]{1,0:T(8,128)(2,1)S(1)} %get-tuple-element.83), channel_id=1, source_target_pairs={{0,3},{1,0},{2,1},{3,2},{4,7},{5,4},{6,5},{7,6},{8,11},{9,8},{10,9... | collective-permute-start | bytes 626696 | tf_op jit(solution)/shard_map/ppermute | solution.py:468
  161.1 12.7 %collective-permute-start.29 = (bf16[48,2176]{1,0:T(8,128)(2,1)S(1)}, bf16[48,2176]{1,0:T(8,128)(2,1)S(1)}, u32[]{:S(2)}, u32[]{:S(2)}) collective-permute-start(bf16[48,2176]{1,0:T(8,128)(2,1)S(1)} %sum_pieces.2.refs_4_.refs_0_), channel_id=1, source_target_pairs={{0,16},{4,12},{8,24},{12,4},{16,0},{20,28},{24,8},{28,20},{1,17},{... | collective-permute-start | bytes 626696 | tf_op jit(solution)/shard_map/ppermute | solution.py:465
  162.2 4.5 %collective-permute-start.22 = (bf16[48,1152]{1,0:T(8,128)(2,1)S(1)}, bf16[48,1152]{1,0:T(8,128)(2,1)S(1)}, u32[]{:S(2)}, u32[]{:S(2)}) collective-permute-start(bf16[48,1152]{1,0:T(8,128)(2,1)S(1)} %get-tuple-element.78), channel_id=1, source_target_pairs={{0,1},{1,2},{2,3},{3,0},{4,5},{5,6},{6,7},{7,4},{8,9},{9,10},{10,1... | collective-permute-start | bytes 331784 | tf_op jit(solution)/shard_map/ppermute | solution.py:468
  162.2 9.7 %collective-permute-start.23 = (bf16[48,1152]{1,0:T(8,128)(2,1)S(1)}, bf16[48,1152]{1,0:T(8,128)(2,1)S(1)}, u32[]{:S(2)}, u32[]{:S(2)}) collective-permute-start(bf16[48,1152]{1,0:T(8,128)(2,1)S(1)} %get-tuple-element.79), channel_id=1, source_target_pairs={{0,2},{1,3},{2,0},{3,1},{4,6},{5,7},{6,4},{7,5},{8,10},{9,11},{10,... | collective-permute-start | bytes 331784 | tf_op jit(solution)/shard_map/ppermute | solution.py:468
  162.2 11.1 %collective-permute-start.24 = (bf16[48,1152]{1,0:T(8,128)(2,1)S(1)}, bf16[48,1152]{1,0:T(8,128)(2,1)S(1)}, u32[]{:S(2)}, u32[]{:S(2)}) collective-permute-start(bf16[48,1152]{1,0:T(8,128)(2,1)S(1)} %get-tuple-element.80), channel_id=1, source_target_pairs={{0,3},{1,0},{2,1},{3,2},{4,7},{5,4},{6,5},{7,6},{8,11},{9,8},{10,9... | collective-permute-start | bytes 331784 | tf_op jit(solution)/shard_map/ppermute | solution.py:468
  174.4 11.0 %copy-start.28 = (bf16[192]{0:T(256)(128)(2,1)S(1)}, bf16[192]{0:T(256)(128)(2,1)}, u32[]{:S(2)}) copy-start(bf16[192]{0:T(256)(128)(2,1)} %param.14) | copy-start | bytes 1156
  174.4 8.4 %collective-permute-start.31 = (bf16[2,48,2176]{2,1,0:T(8,128)(2,1)S(1)}, bf16[2,48,2176]{2,1,0:T(8,128)(2,1)S(1)}, u32[]{:S(2)}, u32[]{:S(2)}) collective-permute-start(bf16[2,48,2176]{2,1,0:T(8,128)(2,1)S(1)} %join.8.refs_2_.refs_0_), channel_id=1, source_target_pairs={{0,8},{4,20},{8,0},{12,28},{16,24},{20,4},{24,16},{28,12},{1,9},{5... | collective-permute-start | bytes 1253384 | tf_op jit(solution)/shard_map/ppermute | solution.py:465
  175.3 5.0 %collective-permute-start.28 = (bf16[48,1152]{1,0:T(8,128)(2,1)S(1)}, bf16[48,1152]{1,0:T(8,128)(2,1)S(1)}, u32[]{:S(2)}, u32[]{:S(2)}) collective-permute-start(bf16[48,1152]{1,0:T(8,128)(2,1)S(1)} %sum_pieces.3.refs_2_.refs_0_), channel_id=1, source_target_pairs={{0,16},{4,12},{8,24},{12,4},{16,0},{20,28},{24,8},{28,20},{1,17},{... | collective-permute-start | bytes 331784 | tf_op jit(solution)/shard_map/ppermute | solution.py:465
  183.5 3.3 %collective-permute-start.32 = (bf16[2,2,48,2176]{3,2,1,0:T(8,128)(2,1)S(1)}, bf16[2,2,48,2176]{3,2,1,0:T(8,128)(2,1)S(1)}, u32[]{:S(2)}, u32[]{:S(2)}) collective-permute-start(bf16[2,2,48,2176]{3,2,1,0:T(8,128)(2,1)S(1)} %join.10.refs_1_), channel_id=1, source_target_pairs={{0,4},{4,0},{8,12},{12,8},{16,20},{20,16},{24,28},{28,24},{1,5},{5... | collective-permute-start | bytes 2506760 | tf_op jit(solution)/shard_map/ppermute | solution.py:465
  184.8 5.8 %collective-permute-start.30 = (bf16[2,48,1152]{2,1,0:T(8,128)(2,1)S(1)}, bf16[2,48,1152]{2,1,0:T(8,128)(2,1)S(1)}, u32[]{:S(2)}, u32[]{:S(2)}) collective-permute-start(bf16[2,48,1152]{2,1,0:T(8,128)(2,1)S(1)} %join.9.refs_2_.refs_4_.refs_0_), channel_id=1, source_target_pairs={{0,8},{4,20},{8,0},{12,28},{16,24},{20,4},{24,16},{28,12},{1,9},{5... | collective-permute-start | bytes 663560 | tf_op jit(solution)/shard_map/ppermute | solution.py:465
  192.7 1.9 collective-permute-start.33
  (18 other events, 28.1 us)

commit v4 on v3

--- a/solution.py
+++ b/solution.py
@@ -206,8 +206,8 @@
 
 def feed_forward(groups, place, gains, mixed, tok, grad_out, own_in, own_out, own_down, *rest):
     parts, rest = rest[:4], rest[4:]
-    output, middle_grad, mixed_grad, branch_grad, hidden, mlp_in, gate_up_grad, for_other = rest[:8]
-    w_in, w_out, w_down, middle, act, slope, total = rest[8:]
+    output, middle_grad, mixed_grad, branch_grad, hidden, mlp_in, gate_up_grad, for_other, for_other_next = rest[:9]
+    w_in, w_out, w_down, middle, act, slope, total = rest[9:]
     assemble(groups, place, parts, own_out, w_out, D // 2, FF)
     assemble(groups, place, parts, own_in, w_in, FF, 0)
     shard = own_down.shape[0]
@@ -267,19 +267,15 @@
         return 0
 
     lax.fori_loop(0, D // 256, back, 0)
-    start = 0
-    for whole in (hidden, mlp_in):
-        for_other[:, start : start + whole.shape[1]] = whole[...]
-        start += whole.shape[1]
-    for whole in (grad_out, gate_up_grad, branch_grad):
-        width = whole.shape[1] // 2
-        for_other[:, start : start + width] = whole[:, columns((1 - place[3]) * width, width)]
-        start += width
-
-
-HIDDEN, MLP_IN, UPSTREAM, GATE_UP, BRANCH, SENT = (
-    0, FF, FF + D, FF + D + D // 2, 2 * FF + D + D // 2, 2 * FF + 2 * D
-)
+    for_other[:, :D] = mlp_in[...]
+    copy_half(place, gate_up_grad, for_other.at[:, GATE_UP:BRANCH])
+    copy_half(place, branch_grad, for_other.at[:, BRANCH:])
+    for_other_next[:, :FF] = hidden[...]
+    copy_half(place, grad_out, for_other_next.at[:, UPSTREAM:])
+
+
+MLP_IN, GATE_UP, BRANCH, SENT_FIRST = 0, D, FF + D, FF + D + D // 2
+HIDDEN, UPSTREAM, SENT_NEXT = 0, FF, FF + D // 2
 
 
 def attn_backward(place, qkv, lse, mixed_grad, cosine, sine, seg_col, seg_row, qkv_grad, for_other):
@@ -558,11 +554,11 @@
         low = across(mlp_here, swap_low)
         (low,) = run(keep_copy, "keep_copy", [shape(low.shape)], place, [low], (), [mixed])
         mlp_parts = [mlp_here, low, across(mlp_here, swap_core), across(low, swap_core)]
-        output, middle_grad, mixed_grad, branch_grad, hidden, mlp_in, gate_up_grad, for_other = run(
+        output, middle_grad, mixed_grad, branch_grad, hidden, mlp_in, gate_up_grad, for_other, for_other_next = run(
             functools.partial(feed_forward, groups), "feed_forward",
             [
                 shape((length, D)), shape((length, D), f32), shape((length, D)), shape((length, D)),
-                shape((length, FF)), shape((length, D)), shape((length, 2 * FF)), shape((length, SENT)),
+                shape((length, FF)), shape((length, D)), shape((length, 2 * FF)), shape((length, SENT_FIRST)), shape((length, SENT_NEXT)),
             ],
             place, [gains, mixed, tokens, grad_out, w_in, w_out, w_down] + mlp_parts,
             [
@@ -571,19 +567,19 @@
                 pltpu.VMEM((length, D), f32),
             ],
         )
-        from_other = across(for_other, swap_core)
+        from_other, from_other_next = across(for_other, swap_core), across(for_other_next, swap_core)
 
         attn_other = across(attn_sent, swap_core)
-        down_keep, down_got = grad_self(
-            [hidden, grad_out, from_other], [(0, (2, HIDDEN), 1, (2, UPSTREAM))], 144
-        )
         rest_keep, rest_got = grad_self(
             [mlp_in, gate_up_grad, mixed, branch_grad, from_other, attn_other],
-            [(0, (4, MLP_IN), 1, (4, GATE_UP)), (2, (5, D), 3, (4, BRANCH))], 96, [down_keep],
+            [(0, (4, MLP_IN), 1, (4, GATE_UP)), (2, (5, D), 3, (4, BRANCH))], 96,
+        )
+        down_keep, down_got = grad_self(
+            [hidden, grad_out, from_other_next], [(0, (2, HIDDEN), 1, (2, UPSTREAM))], 144, [rest_keep]
         )
         qkv_grad, qkv_send = run(
             attn_backward, "attn_backward", [shape((length, 3 * D)), shape((length, QKV))],
-            place, [qkv, lse, mixed_grad] + rope, (), [rest_keep],
+            place, [qkv, lse, mixed_grad] + rope, (), [down_keep],
         )
         qkv_other = across(qkv_send, swap_core)
         qkv_keep, qkv_got = grad_self(

time: 198 us -> 195 us (0.985)
  waiting for transfers between devices: 95.1 us -> 91.7 us
    ppermute x22 -> x23, waiting for transfers between devices: 50.9 us -> 47.5 us  [across(): return lax.ppermute(a, 'replica', perm)]
    ppermute x22 -> x23, starting transfers between devices: 21.4 us -> 21.8 us  [across(): return lax.ppermute(a, 'replica', perm)]
    unnamed x61 -> x59, local copies, waits for them, and re-layouts: 9.97 us -> 9.99 us
  transfers between devices with their start and end apart: 34 -> 35, of which waited for: 24 -> 24; matrix products, arithmetic and copies ran while one was open for 2% -> 2% of each run, Pallas kernels for 17% -> 19%
where the time goes in v4:
time: 195 us; the launch traced here: 194 us
  waiting for transfers between devices  91.7 us (47%)
  Pallas kernels  53.9 us (28%)
  starting transfers between devices  31.6 us (16%)
  local copies, waits for them, and re-layouts  12.9 us (7%)
  other arithmetic  3.02 us (2%)
    pallas_call x24, Pallas kernels, run(): pl.pallas_call(inner, out_shape=outs, in_specs=[SMEM] + [VMEM] * count +...  53.9 us
    ppermute x23, waiting for transfers between devices, across(): return lax.ppermute(a, 'replica', perm)  47.5 us
    ppermute x12, waiting for transfers between devices, shifted(): lax.ppermute(a, 'group', [(i, (i + k) % groups) for i in range(groups)])  44.2 us
    ppermute x23, starting transfers between devices, across(): return lax.ppermute(a, 'replica', perm)  21.8 us
    unnamed x59, local copies, waits for them, and re-layouts  9.99 us
    ppermute x12, starting transfers between devices, shifted(): lax.ppermute(a, 'group', [(i, (i + k) % groups) for i in range(groups)])  9.8 us
  transfers between devices with their start and end apart: 35, of which 24 were waited for; matrix products, arithmetic and copies ran while one was open for 2% of the time, Pallas kernels for 19%

profile of v4, /device:TPU:9, one launch (start us, length us, event | category | flops | bytes accessed | tf_op | source)
XLA Modules:
  0.0 194.2 jit_solution(14421495348891955284)
XLA Ops:
  2.3 1.3 collective-permute-start
  3.7 1.1 collective-permute-start.1
  4.8 1.4 collective-permute-start.2
  9.5 4.0 %collective-permute-done.1.refs_1_ = bf16[48,1280]{1,0:T(8,128)(2,1)S(1)} collective-permute-done((bf16[48,1280]{1,0:T(8,128)(2,1)S(1)}, bf16[48,1280]{1,0:T(8,128)(2,1)S(1)}, u32[]{:S(2)}, u32[]{:S(2)}) %collective-permute-start.1) | collective-permute-done | bytes 122912 | tf_op jit(solution)/shard_map/ppermute | solution.py:464
  13.6 2.8 %collective-permute-done.2.refs_2_ = bf16[48,1280]{1,0:T(8,128)(2,1)S(1)} collective-permute-done((bf16[48,1280]{1,0:T(8,128)(2,1)S(1)}, bf16[48,1280]{1,0:T(8,128)(2,1)S(1)}, u32[]{:S(2)}, u32[]{:S(2)}) %collective-permute-start.2) | collective-permute-done | bytes 122912 | tf_op jit(solution)/shard_map/ppermute | solution.py:464
  17.0 1.3 collective-permute-start.3
  18.4 5.9 %collective-permute-done.4.refs_2_.refs_0_ = bf16[48,2176]{1,0:T(8,128)(2,1)S(1)} collective-permute-done((bf16[48,2176]{1,0:T(8,128)(2,1)S(1)}, bf16[48,2176]{1,0:T(8,128)(2,1)S(1)}, u32[]{:S(2)}, u32[]{:S(2)}) %collective-permute-start.4) | collective-permute-done | bytes 208928 | tf_op jit(solution)/shard_map/ppermute | solution.py:464
  24.9 2.3 %collective-permute-start.5 = (bf16[2,3,48,1152]{3,2,1,0:T(8,128)(2,1)S(1)}, bf16[2,3,48,1152]{3,2,1,0:T(8,128)(2,1)S(1)}, u32[]{:S(2)}, u32[]{:S(2)}) collective-permute-start(bf16[2,3,48,1152]{3,2,1,0:T(8,128)(2,1)S(1)} %join.6.refs_7_.refs_5_), channel_id=1, source_target_pairs={{0,16},{4,12},{8,24},{12,4},{16,0},{20,28},{24,8},{28,20},{1,17},{... | collective-permute-start | bytes 1990664 | tf_op jit(solution)/shard_map/ppermute | solution.py:461
  27.2 1.3 collective-permute-start.8
  28.5 7.0 %collective-permute-done.5.refs_3_.refs_8_.refs_6_ = bf16[2,3,48,1152]{3,2,1,0:T(8,128)(2,1)S(1)} collective-permute-done((bf16[2,3,48,1152]{3,2,1,0:T(8,128)(2,1)S(1)}, bf16[2,3,48,1152]{3,2,1,0:T(8,128)(2,1)S(1)}, u32[]{:S(2)}, u32[]{:S(2)}) %collective-permute-start.5) | collective-permute-done | bytes 663584 | tf_op jit(solution)/shard_map/ppermute | solution.py:461
  35.5 1.8 collective-permute-start.7
  37.3 4.9 %collective-permute-done.8.refs_1_ = bf16[48,2176]{1,0:T(8,128)(2,1)S(1)} collective-permute-done((bf16[48,2176]{1,0:T(8,128)(2,1)S(1)}, bf16[48,2176]{1,0:T(8,128)(2,1)S(1)}, u32[]{:S(2)}, u32[]{:S(2)}) %collective-permute-start.8) | collective-permute-done | bytes 208928 | tf_op jit(solution)/shard_map/ppermute | solution.py:464
  42.2 1.2 collective-permute-done.9.refs_2_
  45.0 8.6 %collective-permute-done.10.refs_1_ = bf16[3,48,2176]{2,1,0:T(8,128)(2,1)S(1)} collective-permute-done((bf16[3,48,2176]{2,1,0:T(8,128)(2,1)S(1)}, bf16[3,48,2176]{2,1,0:T(8,128)(2,1)S(1)}, u32[]{:S(2)}, u32[]{:S(2)}) %collective-permute-start.10) | collective-permute-done | bytes 626720 | tf_op jit(solution)/shard_map/ppermute | solution.py:461
  56.3 2.0 %collective-permute-start.12 = (bf16[2,3,48,2176]{3,2,1,0:T(8,128)(2,1)S(1)}, bf16[2,3,48,2176]{3,2,1,0:T(8,128)(2,1)S(1)}, u32[]{:S(2)}, u32[]{:S(2)}) collective-permute-start(bf16[2,3,48,2176]{3,2,1,0:T(8,128)(2,1)S(1)} %join.7.refs_11_.refs_7_), channel_id=1, source_target_pairs={{0,4},{4,0},{8,12},{12,8},{16,20},{20,16},{24,28},{28,24},{1,5},{5... | collective-permute-start | bytes 3760136 | tf_op jit(solution)/shard_map/ppermute | solution.py:461
  64.1 7.8 %attn_forward.1 = (bf16[256,768]{1,0:T(8,128)(2,1)S(1)}, bf16[256,2304]{1,0:T(8,128)(2,1)S(1)}, bf16[256,768]{1,0:T(8,128)(2,1)S(1)}, f32[256,128]{1,0:T(8,128)S(1)}, bf16[256,1536]{1,0:T(8,128)(2,1)S(1)}) custom-call(s32[4]{0:T(128)S(1)} %pad_add_fusion.place, f32[2,768]{1,0:T(2,128)S(1)} %pad_maximum_fusion.4.refs_0_.refs_2_, f32[256,128]{1,0:T(8,128)S(1)} %copy-done.13, ...), custom_call_target="tpu_custom_call" | custom-call | tf_op jit(solution)/shard_map/attn_forward/pallas_call | solution.py:39
  72.0 1.5 keep_copy.1.refs_8_
  73.5 1.4 collective-permute-start.13
  74.9 2.6 %collective-permute-done.13.refs_10_ = bf16[2,3,48,2176]{3,2,1,0:T(8,128)(2,1)S(1)} collective-permute-done((bf16[2,3,48,2176]{3,2,1,0:T(8,128)(2,1)S(1)}, bf16[2,3,48,2176]{3,2,1,0:T(8,128)(2,1)S(1)}, u32[]{:S(2)}, u32[]{:S(2)}) %collective-permute-start.13) | collective-permute-done | bytes 1253408 | tf_op jit(solution)/shard_map/ppermute | solution.py:461
  78.5 10.7 %feed_forward.1 = (bf16[256,768]{1,0:T(8,128)(2,1)}, f32[256,768]{1,0:T(8,128)S(1)}, bf16[256,768]{1,0:T(8,128)(2,1)S(1)}, bf16[256,768]{1,0:T(8,128)(2,1)S(1)},...) custom-call(s32[4]{0:T(128)S(1)} %pad_add_fusion.place, ...), custom_call_target="tpu_custom_call" | custom-call | tf_op jit(solution)/shard_map/feed_forward/pallas_call | solution.py:39
  90.1 3.1 %collective-permute-done.16.refs_5_.refs_2_ = bf16[256,1536]{1,0:T(8,128)(2,1)S(1)} collective-permute-done((bf16[256,1536]{1,0:T(8,128)(2,1)S(1)}, bf16[256,1536]{1,0:T(8,128)(2,1)S(1)}, u32[]{:S(2)}, u32[]{:S(2)}) %collective-permute-start.16) | collective-permute-done | bytes 786464 | tf_op jit(solution)/shard_map/ppermute | solution.py:461
  93.2 3.5 %grad_for_self.3 = (bf16[4,96,1536]{2,1,0:T(8,128)(2,1)S(1)}, bf16[4,96,1536]{2,1,0:T(8,128)(2,1)S(1)}) custom-call(s32[4]{0:T(128)S(1)} %pad_add_fusion.place, bf16[256,768]{1,0:T(8,128)(2,1)S(1)} %get-tuple-element.59.refs_0_, bf16[256,2304]{1,0:T(8,128)(2,1)S(1)} %get-tuple-element.60.refs_1_, bf16[256,768]{1,0:T(8,128)(2,1)S(1)} %get-tuple-element.52.refs_1_.refs_2_, ...), custom_call_target="tpu_custom_call" | custom-call | tf_op jit(solution)/shard_map/grad_for_self/pallas_call | solution.py:39
  97.6 1.7 grad_for_self.4
  99.3 6.5 %attn_backward.1 = (bf16[256,2304]{1,0:T(8,128)(2,1)S(1)}, bf16[256,1152]{1,0:T(8,128)(2,1)S(1)}) custom-call(s32[4]{0:T(128)S(1)} %pad_add_fusion.place, bf16[256,2304]{1,0:T(8,128)(2,1)S(1)} %get-tuple-element.54.refs_0_, f32[256,128]{1,0:T(8,128)S(1)} %get-tuple-element.55.refs_1_, bf16[256,768]{1,0:T(8,128)(2,1)S(1)} %get-tuple-element.56.refs_2_, ...), custom_call_target="tpu_custom_call" | custom-call | tf_op jit(solution)/shard_map/attn_backward/pallas_call | solution.py:39
  106.4 1.2 collective-permute-start.17
  108.1 2.6 %grad_for_self.5 = (bf16[4,96,1152]{2,1,0:T(8,128)(2,1)S(1)}, bf16[4,96,1152]{2,1,0:T(8,128)(2,1)S(1)}) custom-call(s32[4]{0:T(128)S(1)} %pad_add_fusion.place, bf16[256,768]{1,0:T(8,128)(2,1)S(1)} %get-tuple-element.70.refs_0_, bf16[256,2304]{1,0:T(8,128)(2,1)S(1)} %get-tuple-element.66.refs_1_.refs_0_, ...), custom_call_target="tpu_custom_call" | custom-call | tf_op jit(solution)/shard_map/grad_for_self/pallas_call | solution.py:39
  110.7 1.3 collective-permute-start.20
  112.0 4.8 %collective-permute-done.17.refs_1_ = bf16[4,144,384]{2,1,0:T(8,128)(2,1)S(1)} collective-permute-done((bf16[4,144,384]{2,1,0:T(8,128)(2,1)S(1)}, bf16[4,144,384]{2,1,0:T(8,128)(2,1)S(1)}, u32[]{:S(2)}, u32[]{:S(2)}) %collective-permute-start.17) | collective-permute-done | bytes 442400 | tf_op jit(solution)/shard_map/ppermute | solution.py:461
  118.7 3.8 %attn_in_backward.1.refs_2_ = bf16[256,768]{1,0:T(8,128)(2,1)} custom-call(s32[4]{0:T(128)S(1)} %pad_add_fusion.place, bf16[256,2304]{1,0:T(8,128)(2,1)S(1)} %get-tuple-element.66.refs_1_.refs_0_, f32[256,768]{1,0:T(8,128)S(1)} %get-tuple-element.67.refs_1_, f32[2,768]{1,0:T(2,128)S(1)} %pad_maximum_fusion.4.refs_0_.refs_2_, ...), custom_call_target="tpu_custom_call" | custom-call | tf_op jit(solution)/shard_map/attn_in_backward/pallas_call | solution.py:39
  122.5 7.8 %collective-permute-done.20.refs_1_ = bf16[4,96,1152]{2,1,0:T(8,128)(2,1)S(1)} collective-permute-done((bf16[4,96,1152]{2,1,0:T(8,128)(2,1)S(1)}, bf16[4,96,1152]{2,1,0:T(8,128)(2,1)S(1)}, u32[]{:S(2)}, u32[]{:S(2)}) %collective-permute-start.20) | collective-permute-done | bytes 884768 | tf_op jit(solution)/shard_map/ppermute | solution.py:461
  132.9 2.9 %collective-permute-done.22.refs_1_ = bf16[4,48,2176]{2,1,0:T(8,128)(2,1)S(1)} collective-permute-done((bf16[4,48,2176]{2,1,0:T(8,128)(2,1)S(1)}, bf16[4,48,2176]{2,1,0:T(8,128)(2,1)S(1)}, u32[]{:S(2)}, u32[]{:S(2)}) %collective-permute-start.22) | collective-permute-done | bytes 835616 | tf_op jit(solution)/shard_map/ppermute | solution.py:461
  136.6 1.6 collective-permute-start.27
  138.3 1.4 collective-permute-start.28
  139.6 1.2 collective-permute-done.21.refs_1_
  142.1 11.5 %collective-permute-done.27.refs_2_ = bf16[48,2176]{1,0:T(8,128)(2,1)S(1)} collective-permute-done((bf16[48,2176]{1,0:T(8,128)(2,1)S(1)}, bf16[48,2176]{1,0:T(8,128)(2,1)S(1)}, u32[]{:S(2)}, u32[]{:S(2)}) %collective-permute-start.27) | collective-permute-done | bytes 208928 | tf_op jit(solution)/shard_map/ppermute | solution.py:464
  153.7 3.6 %collective-permute-done.28.refs_3_ = bf16[48,2176]{1,0:T(8,128)(2,1)S(1)} collective-permute-done((bf16[48,2176]{1,0:T(8,128)(2,1)S(1)}, bf16[48,2176]{1,0:T(8,128)(2,1)S(1)}, u32[]{:S(2)}, u32[]{:S(2)}) %collective-permute-start.28) | collective-permute-done | bytes 208928 | tf_op jit(solution)/shard_map/ppermute | solution.py:464
  158.9 1.5 collective-permute-start.25
  160.4 3.0 %collective-permute-done.23.refs_1_ = bf16[48,1152]{1,0:T(8,128)(2,1)S(1)} collective-permute-done((bf16[48,1152]{1,0:T(8,128)(2,1)S(1)}, bf16[48,1152]{1,0:T(8,128)(2,1)S(1)}, u32[]{:S(2)}, u32[]{:S(2)}) %collective-permute-start.23) | collective-permute-done | bytes 110624 | tf_op jit(solution)/shard_map/ppermute | solution.py:464
  163.4 5.2 %collective-permute-done.24.refs_2_ = bf16[48,1152]{1,0:T(8,128)(2,1)S(1)} collective-permute-done((bf16[48,1152]{1,0:T(8,128)(2,1)S(1)}, bf16[48,1152]{1,0:T(8,128)(2,1)S(1)}, u32[]{:S(2)}, u32[]{:S(2)}) %collective-permute-start.24) | collective-permute-done | bytes 110624 | tf_op jit(solution)/shard_map/ppermute | solution.py:464
  168.6 1.4 collective-permute-done.25.refs_3_
  172.7 4.2 %collective-permute-done.29.refs_1_ = bf16[48,1152]{1,0:T(8,128)(2,1)S(1)} collective-permute-done((bf16[48,1152]{1,0:T(8,128)(2,1)S(1)}, bf16[48,1152]{1,0:T(8,128)(2,1)S(1)}, u32[]{:S(2)}, u32[]{:S(2)}) %collective-permute-start.29) | collective-permute-done | bytes 110624 | tf_op jit(solution)/shard_map/ppermute | solution.py:461
  177.5 2.1 %collective-permute-done.32.refs_1_ = bf16[2,48,2176]{2,1,0:T(8,128)(2,1)S(1)} collective-permute-done((bf16[2,48,2176]{2,1,0:T(8,128)(2,1)S(1)}, bf16[2,48,2176]{2,1,0:T(8,128)(2,1)S(1)}, u32[]{:S(2)}, u32[]{:S(2)}) %collective-permute-start.32) | collective-permute-done | bytes 417824 | tf_op jit(solution)/shard_map/ppermute | solution.py:461
  180.3 1.2 collective-permute-start.33
  182.2 1.3 collective-permute-done.33.refs_2_
  183.5 3.9 %place_mlp.1 = (f32[192,2304]{1,0:T(8,128)}, f32[192,768]{1,0:T(8,128)}, f32[288,768]{1,0:T(8,128)}, f32[1,192]{1,0:T(1,128)}) custom-call(s32[4]{0:T(128)S(1)} %pad_add_fusion.place, f32[1,192]{1,0:T(1,128)S(1)} %bitcast.39, bf16[2,2,48,2176]{3,2,1,0:T(8,128)(2,1)S(1)} %join.10.refs_1_, bf16[2,2,48,2176]{3,2,1,0:T(8,128)(2,1)S(1)} %collective-permute-done.33.refs_2_, ...), custom_call_target="tpu_custom_call" | custom-call | tf_op jit(solution)/shard_map/place_mlp/pallas_call | solution.py:39
  187.3 1.5 copy-done.1
  189.8 1.4 collective-permute-done.34.refs_2_
  191.3 2.9 %place_qkv.1 = (f32[192,2304]{1,0:T(8,128)}, f32[1,192]{1,0:T(1,128)}) custom-call(s32[4]{0:T(128)S(1)} %pad_add_fusion.place, f32[1,192]{1,0:T(1,128)S(1)} %bitcast.40, bf16[2,2,48,1152]{3,2,1,0:T(8,128)(2,1)S(1)} %join.11.refs_1_, bf16[2,2,48,1152]{3,2,1,0:T(8,128)(2,1)S(1)} %collective-permute-done.34.refs_2_, bf16[192,2304]{1,0:T(8,128)(2,1)S(1)} %copy-done, ...), custom_call_target="tpu_custom_call" | custom-call | tf_op jit(solution)/shard_map/place_qkv/pallas_call | solution.py:39
  (134 shorter events, 34.1 us)
Async XLA Ops:
  2.3 7.2 %collective-permute-start = (bf16[48,1280]{1,0:T(8,128)(2,1)S(1)}, bf16[48,1280]{1,0:T(8,128)(2,1)S(1)}, u32[]{:S(2)}, u32[]{:S(2)}) collective-permute-start(bf16[48,1280]{1,0:T(8,128)(2,1)S(1)} %pad_maximum_fusion.3), channel_id=1, source_target_pairs={{0,1},{1,2},{2,3},{3,0},{4,5},{5,6},{6,7},{7,4},{8,9},{9,10},{10,1... | collective-permute-start | bytes 368648 | tf_op jit(solution)/shard_map/ppermute | solution.py:464
  3.7 9.9 %collective-permute-start.1 = (bf16[48,1280]{1,0:T(8,128)(2,1)S(1)}, bf16[48,1280]{1,0:T(8,128)(2,1)S(1)}, u32[]{:S(2)}, u32[]{:S(2)}) collective-permute-start(bf16[48,1280]{1,0:T(8,128)(2,1)S(1)} %pad_maximum_fusion.3), channel_id=1, source_target_pairs={{0,2},{1,3},{2,0},{3,1},{4,6},{5,7},{6,4},{7,5},{8,10},{9,11},{10,... | collective-permute-start | bytes 368648 | tf_op jit(solution)/shard_map/ppermute | solution.py:464
  4.8 11.6 %collective-permute-start.2 = (bf16[48,1280]{1,0:T(8,128)(2,1)S(1)}, bf16[48,1280]{1,0:T(8,128)(2,1)S(1)}, u32[]{:S(2)}, u32[]{:S(2)}) collective-permute-start(bf16[48,1280]{1,0:T(8,128)(2,1)S(1)} %pad_maximum_fusion.3), channel_id=1, source_target_pairs={{0,3},{1,0},{2,1},{3,2},{4,7},{5,4},{6,5},{7,6},{8,11},{9,8},{10,9... | collective-permute-start | bytes 368648 | tf_op jit(solution)/shard_map/ppermute | solution.py:464
  8.2 10.1 %dynamic-slice-start = ((bf16[192,2304]{1,0:T(8,128)(2,1)}, s32[]{:T(128)}, s32[]{:T(128)}), bf16[48,1152]{1,0:T(8,128)(2,1)S(1)}, s32[]{:S(2)}) async-start(bf16[192,2304]{1,0:T(8,128)(2,1)} %refs_3_.6, s32[]{:T(128)} %select_n.42, s32[]{:T(128)} %select_n.43), calls=%async_computation | async-start | bytes 221696 | tf_op jit(solution)/shard_map/dynamic_slice | solution.py:518
  8.3 10.0 %dynamic-slice-start.1 = ((bf16[192,768]{1,0:T(8,128)(2,1)}, s32[]{:T(128)}, s32[]{:T(128)}), bf16[48,384]{1,0:T(8,128)(2,1)S(1)}, s32[]{:S(2)}) async-start(bf16[192,768]{1,0:T(8,128)(2,1)} %refs_5_.3, s32[]{:T(128)} %select_n.42, s32[]{:T(128)} %select_n.49), calls=%async_computation.1 | async-start | bytes 74240 | tf_op jit(solution)/shard_map/dynamic_slice | solution.py:518
  9.5 14.8 %copy-start.12 = (f32[256,128]{1,0:T(8,128)}, f32[256,128]{1,0:T(8,128)S(1)}, u32[]{:S(2)}) copy-start(f32[256,128]{1,0:T(8,128)S(1)} %get-tuple-element.101.refs_3_.refs_1_) | copy-start | bytes 393220
  9.5 14.8 %copy-start.15 = (f32[256,128]{1,0:T(8,128)}, f32[256,128]{1,0:T(8,128)S(1)}, u32[]{:S(2)}) copy-start(f32[256,128]{1,0:T(8,128)S(1)} %get-tuple-element.102.refs_4_.refs_2_) | copy-start | bytes 393220
  17.0 7.3 %collective-permute-start.3 = (bf16[3,48,1152]{2,1,0:T(8,128)(2,1)S(1)}, bf16[3,48,1152]{2,1,0:T(8,128)(2,1)S(1)}, u32[]{:S(2)}, u32[]{:S(2)}) collective-permute-start(bf16[3,48,1152]{2,1,0:T(8,128)(2,1)S(1)} %get-tuple-element.51.refs_0_), channel_id=1, source_target_pairs={{0,8},{4,20},{8,0},{12,28},{16,24},{20,4},{24,16},{28,12},{1,9},{5... | collective-permute-start | bytes 995336 | tf_op jit(solution)/shard_map/ppermute | solution.py:461
  18.3 6.0 %collective-permute-start.4 = (bf16[48,2176]{1,0:T(8,128)(2,1)S(1)}, bf16[48,2176]{1,0:T(8,128)(2,1)S(1)}, u32[]{:S(2)}, u32[]{:S(2)}) collective-permute-start(bf16[48,2176]{1,0:T(8,128)(2,1)S(1)} %pad_maximum_fusion), channel_id=1, source_target_pairs={{0,1},{1,2},{2,3},{3,0},{4,5},{5,6},{6,7},{7,4},{8,9},{9,10},{10,1... | collective-permute-start | bytes 626696 | tf_op jit(solution)/shard_map/ppermute | solution.py:464
  24.9 10.6 %collective-permute-start.5 = (bf16[2,3,48,1152]{3,2,1,0:T(8,128)(2,1)S(1)}, bf16[2,3,48,1152]{3,2,1,0:T(8,128)(2,1)S(1)}, u32[]{:S(2)}, u32[]{:S(2)}) collective-permute-start(bf16[2,3,48,1152]{3,2,1,0:T(8,128)(2,1)S(1)} %join.6.refs_7_.refs_5_), channel_id=1, source_target_pairs={{0,16},{4,12},{8,24},{12,4},{16,0},{20,28},{24,8},{28,20},{1,17},{... | collective-permute-start | bytes 1990664 | tf_op jit(solution)/shard_map/ppermute | solution.py:461
  27.2 16.2 %collective-permute-start.6 = (bf16[2,3,48,1152]{3,2,1,0:T(8,128)(2,1)S(1)}, bf16[2,3,48,1152]{3,2,1,0:T(8,128)(2,1)S(1)}, u32[]{:S(2)}, u32[]{:S(2)}) collective-permute-start(bf16[2,3,48,1152]{3,2,1,0:T(8,128)(2,1)S(1)} %join.6.refs_7_.refs_5_), channel_id=1, source_target_pairs={{0,4},{4,0},{8,12},{12,8},{16,20},{20,16},{24,28},{28,24},{1,5},{5... | collective-permute-start | bytes 1990664 | tf_op jit(solution)/shard_map/ppermute | solution.py:461
  27.2 15.0 %collective-permute-start.8 = (bf16[48,2176]{1,0:T(8,128)(2,1)S(1)}, bf16[48,2176]{1,0:T(8,128)(2,1)S(1)}, u32[]{:S(2)}, u32[]{:S(2)}) collective-permute-start(bf16[48,2176]{1,0:T(8,128)(2,1)S(1)} %pad_maximum_fusion), channel_id=1, source_target_pairs={{0,2},{1,3},{2,0},{3,1},{4,6},{5,7},{6,4},{7,5},{8,10},{9,11},{10,... | collective-permute-start | bytes 626696 | tf_op jit(solution)/shard_map/ppermute | solution.py:464
  28.4 14.9 %collective-permute-start.9 = (bf16[48,2176]{1,0:T(8,128)(2,1)S(1)}, bf16[48,2176]{1,0:T(8,128)(2,1)S(1)}, u32[]{:S(2)}, u32[]{:S(2)}) collective-permute-start(bf16[48,2176]{1,0:T(8,128)(2,1)S(1)} %pad_maximum_fusion), channel_id=1, source_target_pairs={{0,3},{1,0},{2,1},{3,2},{4,7},{5,4},{6,5},{7,6},{8,11},{9,8},{10,9... | collective-permute-start | bytes 626696 | tf_op jit(solution)/shard_map/ppermute | solution.py:464
  35.5 18.1 %collective-permute-start.7 = (bf16[2,3,48,1152]{3,2,1,0:T(8,128)(2,1)S(1)}, bf16[2,3,48,1152]{3,2,1,0:T(8,128)(2,1)S(1)}, u32[]{:S(2)}, u32[]{:S(2)}) collective-permute-start(bf16[2,3,48,1152]{3,2,1,0:T(8,128)(2,1)S(1)} %collective-permute-done.5.refs_3_.refs_8_.refs_6_), channel_id=1, source_target_pairs={{0,4},{4,0},{8,12},{12,8},{16,20},{20,16},{24,28},{28,24},{1,5},{5... | collective-permute-start | bytes 1990664 | tf_op jit(solution)/shard_map/ppermute | solution.py:461
  44.2 11.1 %copy-start.24 = (s32[256]{0:T(256)S(1)}, s32[256]{0:T(256)}, u32[]{:S(2)}) copy-start(s32[256]{0:T(256)} %param.10) | copy-start | bytes 3076
  44.2 14.0 %copy-start = (bf16[192,2304]{1,0:T(8,128)(2,1)S(1)}, bf16[192,2304]{1,0:T(8,128)(2,1)}, u32[]{:S(2)}) copy-start(bf16[192,2304]{1,0:T(8,128)(2,1)} %refs_3_.7) | copy-start | bytes 2654212
  44.2 9.4 %collective-permute-start.10 = (bf16[3,48,2176]{2,1,0:T(8,128)(2,1)S(1)}, bf16[3,48,2176]{2,1,0:T(8,128)(2,1)S(1)}, u32[]{:S(2)}, u32[]{:S(2)}) collective-permute-start(bf16[3,48,2176]{2,1,0:T(8,128)(2,1)S(1)} %stack_pieces.3.refs_0_), channel_id=1, source_target_pairs={{0,8},{4,20},{8,0},{12,28},{16,24},{20,4},{24,16},{28,12},{1,9},{5... | collective-permute-start | bytes 1880072 | tf_op jit(solution)/shard_map/ppermute | solution.py:461
  54.5 17.4 %collective-permute-start.11 = (bf16[2,3,48,2176]{3,2,1,0:T(8,128)(2,1)S(1)}, bf16[2,3,48,2176]{3,2,1,0:T(8,128)(2,1)}, u32[]{:S(2)}, u32[]{:S(2)}) collective-permute-start(bf16[2,3,48,2176]{3,2,1,0:T(8,128)(2,1)S(1)} %join.7.refs_11_.refs_7_), channel_id=1, source_target_pairs={{0,16},{4,12},{8,24},{12,4},{16,0},{20,28},{24,8},{28,20},{1,17},{... | collective-permute-start | bytes 3760136 | tf_op jit(solution)/shard_map/ppermute | solution.py:461
  56.3 18.6 %collective-permute-start.12 = (bf16[2,3,48,2176]{3,2,1,0:T(8,128)(2,1)S(1)}, bf16[2,3,48,2176]{3,2,1,0:T(8,128)(2,1)S(1)}, u32[]{:S(2)}, u32[]{:S(2)}) collective-permute-start(bf16[2,3,48,2176]{3,2,1,0:T(8,128)(2,1)S(1)} %join.7.refs_11_.refs_7_), channel_id=1, source_target_pairs={{0,4},{4,0},{8,12},{12,8},{16,20},{20,16},{24,28},{28,24},{1,5},{5... | collective-permute-start | bytes 3760136 | tf_op jit(solution)/shard_map/ppermute | solution.py:461
  71.9 6.6 %copy-start.9 = (bf16[192,2304]{1,0:T(8,128)(2,1)S(1)}, bf16[192,2304]{1,0:T(8,128)(2,1)}, u32[]{:S(2)}) copy-start(bf16[192,2304]{1,0:T(8,128)(2,1)} %refs_3_.6) | copy-start | bytes 2654212
  71.9 6.6 %copy-start.11 = (bf16[256,768]{1,0:T(8,128)(2,1)S(1)}, bf16[256,768]{1,0:T(8,128)(2,1)}, u32[]{:S(2)}) copy-start(bf16[256,768]{1,0:T(8,128)(2,1)} %refs_3_.5) | copy-start | bytes 1179652
  71.9 6.6 %copy-start.18 = (bf16[256,768]{1,0:T(8,128)(2,1)S(1)}, bf16[256,768]{1,0:T(8,128)(2,1)}, u32[]{:S(2)}) copy-start(bf16[256,768]{1,0:T(8,128)(2,1)} %refs_1_.1) | copy-start | bytes 1179652
  71.9 6.6 %copy-start.22 = (bf16[288,768]{1,0:T(8,128)(2,1)S(1)}, bf16[288,768]{1,0:T(8,128)(2,1)}, u32[]{:S(2)}) copy-start(bf16[288,768]{1,0:T(8,128)(2,1)} %refs_6_.3) | copy-start | bytes 1327108
  71.9 6.6 %copy-start.23 = (bf16[192,768]{1,0:T(8,128)(2,1)S(1)}, bf16[192,768]{1,0:T(8,128)(2,1)}, u32[]{:S(2)}) copy-start(bf16[192,768]{1,0:T(8,128)(2,1)} %refs_5_.3) | copy-start | bytes 884740
  73.5 4.0 %copy-start.8 = (bf16[2,3,48,2176]{3,2,1,0:T(8,128)(2,1)}, bf16[2,3,48,2176]{3,2,1,0:T(8,128)(2,1)S(1)}, u32[]{:S(2)}) copy-start(bf16[2,3,48,2176]{3,2,1,0:T(8,128)(2,1)S(1)} %keep_copy.1.refs_8_) | copy-start | bytes 3760132
  73.5 3.9 %collective-permute-start.13 = (bf16[2,3,48,2176]{3,2,1,0:T(8,128)(2,1)S(1)}, bf16[2,3,48,2176]{3,2,1,0:T(8,128)(2,1)S(1)}, u32[]{:S(2)}, u32[]{:S(2)}) collective-permute-start(bf16[2,3,48,2176]{3,2,1,0:T(8,128)(2,1)S(1)} %keep_copy.1.refs_8_), channel_id=1, source_target_pairs={{0,4},{4,0},{8,12},{12,8},{16,20},{20,16},{24,28},{28,24},{1,5},{5... | collective-permute-start | bytes 3760136 | tf_op jit(solution)/shard_map/ppermute | solution.py:461
  89.2 4.0 %collective-permute-start.15 = (bf16[256,2304]{1,0:T(8,128)(2,1)S(1)}, bf16[256,2304]{1,0:T(8,128)(2,1)S(1)}, u32[]{:S(2)}, u32[]{:S(2)}) collective-permute-start(bf16[256,2304]{1,0:T(8,128)(2,1)S(1)} %get-tuple-element.62), channel_id=1, source_target_pairs={{0,4},{4,0},{8,12},{12,8},{16,20},{20,16},{24,28},{28,24},{1,5},{5... | collective-permute-start | bytes 3538952 | tf_op jit(solution)/shard_map/ppermute | solution.py:461
  89.6 3.6 %collective-permute-start.16 = (bf16[256,1536]{1,0:T(8,128)(2,1)S(1)}, bf16[256,1536]{1,0:T(8,128)(2,1)S(1)}, u32[]{:S(2)}, u32[]{:S(2)}) collective-permute-start(bf16[256,1536]{1,0:T(8,128)(2,1)S(1)} %get-tuple-element.63), channel_id=1, source_target_pairs={{0,4},{4,0},{8,12},{12,8},{16,20},{20,16},{24,28},{28,24},{1,5},{5... | collective-permute-start | bytes 2359304 | tf_op jit(solution)/shard_map/ppermute | solution.py:461
  89.7 7.8 %collective-permute-start.14 = (bf16[256,1536]{1,0:T(8,128)(2,1)S(1)}, bf16[256,1536]{1,0:T(8,128)(2,1)S(1)}, u32[]{:S(2)}, u32[]{:S(2)}) collective-permute-start(bf16[256,1536]{1,0:T(8,128)(2,1)S(1)} %get-tuple-element.58), channel_id=1, source_target_pairs={{0,4},{4,0},{8,12},{12,8},{16,20},{20,16},{24,28},{28,24},{1,5},{5... | collective-permute-start | bytes 2359304 | tf_op jit(solution)/shard_map/ppermute | solution.py:461
  96.7 20.2 %collective-permute-start.18 = (bf16[4,96,1536]{2,1,0:T(8,128)(2,1)S(1)}, bf16[4,96,1536]{2,1,0:T(8,128)(2,1)S(1)}, u32[]{:S(2)}, u32[]{:S(2)}) collective-permute-start(bf16[4,96,1536]{2,1,0:T(8,128)(2,1)S(1)} %get-tuple-element.69), channel_id=1, source_target_pairs={{0,8},{4,20},{8,0},{12,28},{16,24},{20,4},{24,16},{28,12},{1,9},{5... | collective-permute-start | bytes 3538952 | tf_op jit(solution)/shard_map/ppermute | solution.py:461
  105.8 2.3 %collective-permute-start.19 = (bf16[256,1152]{1,0:T(8,128)(2,1)S(1)}, bf16[256,1152]{1,0:T(8,128)(2,1)S(1)}, u32[]{:S(2)}, u32[]{:S(2)}) collective-permute-start(bf16[256,1152]{1,0:T(8,128)(2,1)S(1)} %get-tuple-element.71), channel_id=1, source_target_pairs={{0,4},{4,0},{8,12},{12,8},{16,20},{20,16},{24,28},{28,24},{1,5},{5... | collective-permute-start | bytes 1769480 | tf_op jit(solution)/shard_map/ppermute | solution.py:461
  106.4 10.4 %collective-permute-start.17 = (bf16[4,144,384]{2,1,0:T(8,128)(2,1)S(1)}, bf16[4,144,384]{2,1,0:T(8,128)(2,1)S(1)}, u32[]{:S(2)}, u32[]{:S(2)}) collective-permute-start(bf16[4,144,384]{2,1,0:T(8,128)(2,1)S(1)} %get-tuple-element.68), channel_id=1, source_target_pairs={{0,8},{4,20},{8,0},{12,28},{16,24},{20,4},{24,16},{28,12},{1,9},{5... | collective-permute-start | bytes 1327112 | tf_op jit(solution)/shard_map/ppermute | solution.py:461
  110.7 19.6 %collective-permute-start.20 = (bf16[4,96,1152]{2,1,0:T(8,128)(2,1)S(1)}, bf16[4,96,1152]{2,1,0:T(8,128)(2,1)S(1)}, u32[]{:S(2)}, u32[]{:S(2)}) collective-permute-start(bf16[4,96,1152]{2,1,0:T(8,128)(2,1)S(1)} %get-tuple-element.74), channel_id=1, source_target_pairs={{0,8},{4,20},{8,0},{12,28},{16,24},{20,4},{24,16},{28,12},{1,9},{5... | collective-permute-start | bytes 2654216 | tf_op jit(solution)/shard_map/ppermute | solution.py:461
  117.8 18.0 %collective-permute-start.22 = (bf16[4,48,2176]{2,1,0:T(8,128)(2,1)S(1)}, bf16[4,48,2176]{2,1,0:T(8,128)(2,1)S(1)}, u32[]{:S(2)}, u32[]{:S(2)}) collective-permute-start(bf16[4,48,2176]{2,1,0:T(8,128)(2,1)S(1)} %get-tuple-element.77), channel_id=1, source_target_pairs={{0,16},{4,12},{8,24},{12,4},{16,0},{20,28},{24,8},{28,20},{1,17},{... | collective-permute-start | bytes 2506760 | tf_op jit(solution)/shard_map/ppermute | solution.py:461
  132.1 8.8 %collective-permute-start.21 = (bf16[4,48,1152]{2,1,0:T(8,128)(2,1)S(1)}, bf16[4,48,1152]{2,1,0:T(8,128)(2,1)S(1)}, u32[]{:S(2)}, u32[]{:S(2)}) collective-permute-start(bf16[4,48,1152]{2,1,0:T(8,128)(2,1)S(1)} %get-tuple-element.76), channel_id=1, source_target_pairs={{0,16},{4,12},{8,24},{12,4},{16,0},{20,28},{24,8},{28,20},{1,17},{... | collective-permute-start | bytes 1327112 | tf_op jit(solution)/shard_map/ppermute | solution.py:461
  136.6 5.6 %collective-permute-start.26 = (bf16[48,2176]{1,0:T(8,128)(2,1)S(1)}, bf16[48,2176]{1,0:T(8,128)(2,1)S(1)}, u32[]{:S(2)}, u32[]{:S(2)}) collective-permute-start(bf16[48,2176]{1,0:T(8,128)(2,1)S(1)} %get-tuple-element.83), channel_id=1, source_target_pairs={{0,1},{1,2},{2,3},{3,0},{4,5},{5,6},{6,7},{7,4},{8,9},{9,10},{10,1... | collective-permute-start | bytes 626696 | tf_op jit(solution)/shard_map/ppermute | solution.py:464
  136.6 17.0 %collective-permute-start.27 = (bf16[48,2176]{1,0:T(8,128)(2,1)S(1)}, bf16[48,2176]{1,0:T(8,128)(2,1)S(1)}, u32[]{:S(2)}, u32[]{:S(2)}) collective-permute-start(bf16[48,2176]{1,0:T(8,128)(2,1)S(1)} %get-tuple-element.84), channel_id=1, source_target_pairs={{0,2},{1,3},{2,0},{3,1},{4,6},{5,7},{6,4},{7,5},{8,10},{9,11},{10,... | collective-permute-start | bytes 626696 | tf_op jit(solution)/shard_map/ppermute | solution.py:464
  138.3 19.0 %collective-permute-start.28 = (bf16[48,2176]{1,0:T(8,128)(2,1)S(1)}, bf16[48,2176]{1,0:T(8,128)(2,1)S(1)}, u32[]{:S(2)}, u32[]{:S(2)}) collective-permute-start(bf16[48,2176]{1,0:T(8,128)(2,1)S(1)} %get-tuple-element.85), channel_id=1, source_target_pairs={{0,3},{1,0},{2,1},{3,2},{4,7},{5,4},{6,5},{7,6},{8,11},{9,8},{10,9... | collective-permute-start | bytes 626696 | tf_op jit(solution)/shard_map/ppermute | solution.py:464
  157.9 12.7 %collective-permute-start.30 = (bf16[48,2176]{1,0:T(8,128)(2,1)S(1)}, bf16[48,2176]{1,0:T(8,128)(2,1)S(1)}, u32[]{:S(2)}, u32[]{:S(2)}) collective-permute-start(bf16[48,2176]{1,0:T(8,128)(2,1)S(1)} %sum_pieces.2.refs_4_.refs_0_), channel_id=1, source_target_pairs={{0,16},{4,12},{8,24},{12,4},{16,0},{20,28},{24,8},{28,20},{1,17},{... | collective-permute-start | bytes 626696 | tf_op jit(solution)/shard_map/ppermute | solution.py:461
  158.9 4.5 %collective-permute-start.23 = (bf16[48,1152]{1,0:T(8,128)(2,1)S(1)}, bf16[48,1152]{1,0:T(8,128)(2,1)S(1)}, u32[]{:S(2)}, u32[]{:S(2)}) collective-permute-start(bf16[48,1152]{1,0:T(8,128)(2,1)S(1)} %get-tuple-element.80), channel_id=1, source_target_pairs={{0,1},{1,2},{2,3},{3,0},{4,5},{5,6},{6,7},{7,4},{8,9},{9,10},{10,1... | collective-permute-start | bytes 331784 | tf_op jit(solution)/shard_map/ppermute | solution.py:464
  158.9 9.7 %collective-permute-start.24 = (bf16[48,1152]{1,0:T(8,128)(2,1)S(1)}, bf16[48,1152]{1,0:T(8,128)(2,1)S(1)}, u32[]{:S(2)}, u32[]{:S(2)}) collective-permute-start(bf16[48,1152]{1,0:T(8,128)(2,1)S(1)} %get-tuple-element.81), channel_id=1, source_target_pairs={{0,2},{1,3},{2,0},{3,1},{4,6},{5,7},{6,4},{7,5},{8,10},{9,11},{10,... | collective-permute-start | bytes 331784 | tf_op jit(solution)/shard_map/ppermute | solution.py:464
  158.9 11.1 %collective-permute-start.25 = (bf16[48,1152]{1,0:T(8,128)(2,1)S(1)}, bf16[48,1152]{1,0:T(8,128)(2,1)S(1)}, u32[]{:S(2)}, u32[]{:S(2)}) collective-permute-start(bf16[48,1152]{1,0:T(8,128)(2,1)S(1)} %get-tuple-element.82), channel_id=1, source_target_pairs={{0,3},{1,0},{2,1},{3,2},{4,7},{5,4},{6,5},{7,6},{8,11},{9,8},{10,9... | collective-permute-start | bytes 331784 | tf_op jit(solution)/shard_map/ppermute | solution.py:464
  171.2 11.0 %copy-start.27 = (bf16[192]{0:T(256)(128)(2,1)S(1)}, bf16[192]{0:T(256)(128)(2,1)}, u32[]{:S(2)}) copy-start(bf16[192]{0:T(256)(128)(2,1)} %param.14) | copy-start | bytes 1156
  171.2 8.4 %collective-permute-start.32 = (bf16[2,48,2176]{2,1,0:T(8,128)(2,1)S(1)}, bf16[2,48,2176]{2,1,0:T(8,128)(2,1)S(1)}, u32[]{:S(2)}, u32[]{:S(2)}) collective-permute-start(bf16[2,48,2176]{2,1,0:T(8,128)(2,1)S(1)} %join.8.refs_2_.refs_0_), channel_id=1, source_target_pairs={{0,8},{4,20},{8,0},{12,28},{16,24},{20,4},{24,16},{28,12},{1,9},{5... | collective-permute-start | bytes 1253384 | tf_op jit(solution)/shard_map/ppermute | solution.py:461
  172.0 4.9 %collective-permute-start.29 = (bf16[48,1152]{1,0:T(8,128)(2,1)S(1)}, bf16[48,1152]{1,0:T(8,128)(2,1)S(1)}, u32[]{:S(2)}, u32[]{:S(2)}) collective-permute-start(bf16[48,1152]{1,0:T(8,128)(2,1)S(1)} %sum_pieces.3.refs_2_.refs_0_), channel_id=1, source_target_pairs={{0,16},{4,12},{8,24},{12,4},{16,0},{20,28},{24,8},{28,20},{1,17},{... | collective-permute-start | bytes 331784 | tf_op jit(solution)/shard_map/ppermute | solution.py:461
  180.3 3.2 %collective-permute-start.33 = (bf16[2,2,48,2176]{3,2,1,0:T(8,128)(2,1)S(1)}, bf16[2,2,48,2176]{3,2,1,0:T(8,128)(2,1)S(1)}, u32[]{:S(2)}, u32[]{:S(2)}) collective-permute-start(bf16[2,2,48,2176]{3,2,1,0:T(8,128)(2,1)S(1)} %join.10.refs_1_), channel_id=1, source_target_pairs={{0,4},{4,0},{8,12},{12,8},{16,20},{20,16},{24,28},{28,24},{1,5},{5... | collective-permute-start | bytes 2506760 | tf_op jit(solution)/shard_map/ppermute | solution.py:461
  181.5 5.8 %collective-permute-start.31 = (bf16[2,48,1152]{2,1,0:T(8,128)(2,1)S(1)}, bf16[2,48,1152]{2,1,0:T(8,128)(2,1)S(1)}, u32[]{:S(2)}, u32[]{:S(2)}) collective-permute-start(bf16[2,48,1152]{2,1,0:T(8,128)(2,1)S(1)} %join.9.refs_2_.refs_4_.refs_0_), channel_id=1, source_target_pairs={{0,8},{4,20},{8,0},{12,28},{16,24},{20,4},{24,16},{28,12},{1,9},{5... | collective-permute-start | bytes 663560 | tf_op jit(solution)/shard_map/ppermute | solution.py:461
  189.4 1.9 collective-permute-start.34
  (18 other events, 23.4 us)

commit v5 on v4

--- a/solution.py
+++ b/solution.py
@@ -235,7 +235,7 @@
         hidden[:, at] = (a * gate).astype(bf16)
         return 0
 
-    lax.fori_loop(0, FF // TILE, forward, 0)
+    lax.fori_loop(0, FF // TILE, forward, 0, unroll=True)
 
     def backward(j, _):
         at = columns(j * TILE, TILE)
@@ -244,7 +244,7 @@
         gate_up_grad[:, columns(FF + j * TILE, TILE)] = (hidden_grad * act[:, at]).astype(bf16)
         return 0
 
-    lax.fori_loop(0, FF // TILE, backward, 0)
+    lax.fori_loop(0, FF // TILE, backward, 0, unroll=True)
     for j in range(2):
         at = slice(j * TILE, (j + 1) * TILE)
         output[:, at] = (middle[:, at] + dot(hidden[...], w_down[:, at])).astype(bf16)
@@ -253,7 +253,7 @@
         total[:, columns(j * 256, 256)] = dot_bt(gate_up_grad[...], w_in[rows(j * 256, 256), :])
         return 0
 
-    lax.fori_loop(0, D // 256, step, 0)
+    lax.fori_loop(0, D // 256, step, 0, unroll=True)
     normed, inverse = norm_parts(middle[...])
     part = norm_back(total[...], normed, inverse, gains[1:2, :])
     whole = grad_out[...].astype(f32) + part
@@ -266,7 +266,7 @@
         ).astype(bf16)
         return 0
 
-    lax.fori_loop(0, D // 256, back, 0)
+    lax.fori_loop(0, D // 256, back, 0, unroll=True)
     for_other[:, :D] = mlp_in[...]
     copy_half(place, gate_up_grad, for_other.at[:, GATE_UP:BRANCH])
     copy_half(place, branch_grad, for_other.at[:, BRANCH:])
@@ -324,7 +324,7 @@
         total[:, columns(j * 256, 256)] = dot_bt(qkv_grad[...], w_full[rows(j * 256, 256), :])
         return 0
 
-    lax.fori_loop(0, D // 256, step, 0)
+    lax.fori_loop(0, D // 256, step, 0, unroll=True)
     normed, inverse = norm_parts(tok[...].astype(f32))
     part = norm_back(total[...], normed, inverse, gains[0:1, :])
     tokens_grad[...] = (middle_grad[...] + part).astype(bf16)
@@ -357,7 +357,7 @@
                     target[g, :, at] = made[side * cut + g * high : side * cut + (g + 1) * high, :].astype(bf16)
             return 0
 
-        lax.fori_loop(0, half // TILE, step, 0)
+        lax.fori_loop(0, half // TILE, step, 0, unroll=True)
         start += half
 
 
@@ -393,12 +393,8 @@
 
 
 def gain_grad(grad, weight, gain):
-    ones = jnp.ones((8, grad.shape[1]), f32)
-    summed = lax.dot_general(
-        ones, grad * weight.astype(f32), (((1,), (1,)), ((), ())),
-        precision=lax.Precision.HIGHEST, preferred_element_type=f32,
-    )
-    return summed[0:1, :] / gain
+    summed = jnp.sum(grad * weight.astype(f32), axis=1, keepdims=True)
+    return jnp.broadcast_to(summed, (grad.shape[0], PAIR)).T[0:1, :] / gain
 
 
 def place_mlp(place, gain, here, other, weight, in_grad, out_grad, down_grad, gain_out):

time: 195 us -> 191 us (0.979)
  Pallas kernels: 53.9 us -> 47.9 us
    pallas_call x24, Pallas kernels: 53.9 us -> 47.9 us  [run(): pl.pallas_call(inner, out_shape=outs, in_specs=[SMEM] + [VMEM] * count +...]
  transfers between devices with their start and end apart: 35 -> 35, of which waited for: 24 -> 25; matrix products, arithmetic and copies ran while one was open for 2% -> 2% of each run, Pallas kernels for 19% -> 17%
where the time goes in v5:
time: 191 us; the launch traced here: 190 us
  waiting for transfers between devices  93.2 us (49%)
  Pallas kernels  47.9 us (25%)
  starting transfers between devices  32.2 us (17%)
  local copies, waits for them, and re-layouts  12.9 us (7%)
  other arithmetic  3.02 us (2%)
    ppermute x23, waiting for transfers between devices, across(): return lax.ppermute(a, 'replica', perm)  49 us
    pallas_call x24, Pallas kernels, run(): pl.pallas_call(inner, out_shape=outs, in_specs=[SMEM] + [VMEM] * count +...  47.9 us
    ppermute x12, waiting for transfers between devices, shifted(): lax.ppermute(a, 'group', [(i, (i + k) % groups) for i in range(groups)])  44.2 us
    ppermute x23, starting transfers between devices, across(): return lax.ppermute(a, 'replica', perm)  22.4 us
    unnamed x59, local copies, waits for them, and re-layouts  9.99 us
    ppermute x12, starting transfers between devices, shifted(): lax.ppermute(a, 'group', [(i, (i + k) % groups) for i in range(groups)])  9.8 us
  transfers between devices with their start and end apart: 35, of which 25 were waited for; matrix products, arithmetic and copies ran while one was open for 2% of the time, Pallas kernels for 17%

profile of v5, /device:TPU:9, one launch (start us, length us, event | category | flops | bytes accessed | tf_op | source)
XLA Modules:
  0.0 190.3 jit_solution(13854945129005463869)
XLA Ops:
  2.3 1.3 collective-permute-start
  3.7 1.1 collective-permute-start.1
  4.8 1.4 collective-permute-start.2
  9.5 4.0 %collective-permute-done.1.refs_1_ = bf16[48,1280]{1,0:T(8,128)(2,1)S(1)} collective-permute-done((bf16[48,1280]{1,0:T(8,128)(2,1)S(1)}, bf16[48,1280]{1,0:T(8,128)(2,1)S(1)}, u32[]{:S(2)}, u32[]{:S(2)}) %collective-permute-start.1) | collective-permute-done | bytes 122912 | tf_op jit(solution)/shard_map/ppermute | solution.py:460
  13.6 2.8 %collective-permute-done.2.refs_2_ = bf16[48,1280]{1,0:T(8,128)(2,1)S(1)} collective-permute-done((bf16[48,1280]{1,0:T(8,128)(2,1)S(1)}, bf16[48,1280]{1,0:T(8,128)(2,1)S(1)}, u32[]{:S(2)}, u32[]{:S(2)}) %collective-permute-start.2) | collective-permute-done | bytes 122912 | tf_op jit(solution)/shard_map/ppermute | solution.py:460
  17.0 1.3 collective-permute-start.3
  18.4 5.9 %collective-permute-done.4.refs_2_.refs_0_ = bf16[48,2176]{1,0:T(8,128)(2,1)S(1)} collective-permute-done((bf16[48,2176]{1,0:T(8,128)(2,1)S(1)}, bf16[48,2176]{1,0:T(8,128)(2,1)S(1)}, u32[]{:S(2)}, u32[]{:S(2)}) %collective-permute-start.4) | collective-permute-done | bytes 208928 | tf_op jit(solution)/shard_map/ppermute | solution.py:460
  24.9 2.3 %collective-permute-start.5 = (bf16[2,3,48,1152]{3,2,1,0:T(8,128)(2,1)S(1)}, bf16[2,3,48,1152]{3,2,1,0:T(8,128)(2,1)S(1)}, u32[]{:S(2)}, u32[]{:S(2)}) collective-permute-start(bf16[2,3,48,1152]{3,2,1,0:T(8,128)(2,1)S(1)} %join.6.refs_7_.refs_5_), channel_id=1, source_target_pairs={{0,16},{4,12},{8,24},{12,4},{16,0},{20,28},{24,8},{28,20},{1,17},{... | collective-permute-start | bytes 1990664 | tf_op jit(solution)/shard_map/ppermute | solution.py:457
  27.2 1.3 collective-permute-start.8
  28.5 7.0 %collective-permute-done.5.refs_3_.refs_8_.refs_6_ = bf16[2,3,48,1152]{3,2,1,0:T(8,128)(2,1)S(1)} collective-permute-done((bf16[2,3,48,1152]{3,2,1,0:T(8,128)(2,1)S(1)}, bf16[2,3,48,1152]{3,2,1,0:T(8,128)(2,1)S(1)}, u32[]{:S(2)}, u32[]{:S(2)}) %collective-permute-start.5) | collective-permute-done | bytes 663584 | tf_op jit(solution)/shard_map/ppermute | solution.py:457
  35.5 1.8 collective-permute-start.7
  37.3 4.9 %collective-permute-done.8.refs_1_ = bf16[48,2176]{1,0:T(8,128)(2,1)S(1)} collective-permute-done((bf16[48,2176]{1,0:T(8,128)(2,1)S(1)}, bf16[48,2176]{1,0:T(8,128)(2,1)S(1)}, u32[]{:S(2)}, u32[]{:S(2)}) %collective-permute-start.8) | collective-permute-done | bytes 208928 | tf_op jit(solution)/shard_map/ppermute | solution.py:460
  42.2 1.2 collective-permute-done.9.refs_2_
  45.0 8.6 %collective-permute-done.10.refs_1_ = bf16[3,48,2176]{2,1,0:T(8,128)(2,1)S(1)} collective-permute-done((bf16[3,48,2176]{2,1,0:T(8,128)(2,1)S(1)}, bf16[3,48,2176]{2,1,0:T(8,128)(2,1)S(1)}, u32[]{:S(2)}, u32[]{:S(2)}) %collective-permute-start.10) | collective-permute-done | bytes 626720 | tf_op jit(solution)/shard_map/ppermute | solution.py:457
  56.3 2.0 %collective-permute-start.12 = (bf16[2,3,48,2176]{3,2,1,0:T(8,128)(2,1)S(1)}, bf16[2,3,48,2176]{3,2,1,0:T(8,128)(2,1)S(1)}, u32[]{:S(2)}, u32[]{:S(2)}) collective-permute-start(bf16[2,3,48,2176]{3,2,1,0:T(8,128)(2,1)S(1)} %join.7.refs_11_.refs_7_), channel_id=1, source_target_pairs={{0,4},{4,0},{8,12},{12,8},{16,20},{20,16},{24,28},{28,24},{1,5},{5... | collective-permute-start | bytes 3760136 | tf_op jit(solution)/shard_map/ppermute | solution.py:457
  64.1 7.8 %attn_forward.1 = (bf16[256,768]{1,0:T(8,128)(2,1)S(1)}, bf16[256,2304]{1,0:T(8,128)(2,1)S(1)}, bf16[256,768]{1,0:T(8,128)(2,1)S(1)}, f32[256,128]{1,0:T(8,128)S(1)}, bf16[256,1536]{1,0:T(8,128)(2,1)S(1)}) custom-call(s32[4]{0:T(128)S(1)} %pad_add_fusion.place, f32[2,768]{1,0:T(2,128)S(1)} %pad_maximum_fusion.4.refs_0_.refs_2_, f32[256,128]{1,0:T(8,128)S(1)} %copy-done.13, ...), custom_call_target="tpu_custom_call" | custom-call | tf_op jit(solution)/shard_map/attn_forward/pallas_call | solution.py:39
  72.0 1.5 keep_copy.1.refs_8_
  73.5 1.4 collective-permute-start.13
  74.9 2.6 %collective-permute-done.13.refs_10_ = bf16[2,3,48,2176]{3,2,1,0:T(8,128)(2,1)S(1)} collective-permute-done((bf16[2,3,48,2176]{3,2,1,0:T(8,128)(2,1)S(1)}, bf16[2,3,48,2176]{3,2,1,0:T(8,128)(2,1)S(1)}, u32[]{:S(2)}, u32[]{:S(2)}) %collective-permute-start.13) | collective-permute-done | bytes 1253408 | tf_op jit(solution)/shard_map/ppermute | solution.py:457
  78.5 8.7 %feed_forward.1 = (bf16[256,768]{1,0:T(8,128)(2,1)}, f32[256,768]{1,0:T(8,128)S(1)}, bf16[256,768]{1,0:T(8,128)(2,1)S(1)}, bf16[256,768]{1,0:T(8,128)(2,1)S(1)},...) custom-call(s32[4]{0:T(128)S(1)} %pad_add_fusion.place, ...), custom_call_target="tpu_custom_call" | custom-call | tf_op jit(solution)/shard_map/feed_forward/pallas_call | solution.py:39
  88.1 3.1 %collective-permute-done.16.refs_5_.refs_2_ = bf16[256,1536]{1,0:T(8,128)(2,1)S(1)} collective-permute-done((bf16[256,1536]{1,0:T(8,128)(2,1)S(1)}, bf16[256,1536]{1,0:T(8,128)(2,1)S(1)}, u32[]{:S(2)}, u32[]{:S(2)}) %collective-permute-start.16) | collective-permute-done | bytes 786464 | tf_op jit(solution)/shard_map/ppermute | solution.py:457
  91.2 2.7 %grad_for_self.3 = (bf16[4,96,1536]{2,1,0:T(8,128)(2,1)S(1)}, bf16[4,96,1536]{2,1,0:T(8,128)(2,1)S(1)}) custom-call(s32[4]{0:T(128)S(1)} %pad_add_fusion.place, bf16[256,768]{1,0:T(8,128)(2,1)S(1)} %get-tuple-element.59.refs_0_, bf16[256,2304]{1,0:T(8,128)(2,1)S(1)} %get-tuple-element.60.refs_1_, bf16[256,768]{1,0:T(8,128)(2,1)S(1)} %get-tuple-element.52.refs_1_.refs_2_, ...), custom_call_target="tpu_custom_call" | custom-call | tf_op jit(solution)/shard_map/grad_for_self/pallas_call | solution.py:39
  94.8 1.7 grad_for_self.4
  96.5 6.7 %attn_backward.1 = (bf16[256,2304]{1,0:T(8,128)(2,1)S(1)}, bf16[256,1152]{1,0:T(8,128)(2,1)S(1)}) custom-call(s32[4]{0:T(128)S(1)} %pad_add_fusion.place, bf16[256,2304]{1,0:T(8,128)(2,1)S(1)} %get-tuple-element.54.refs_0_, f32[256,128]{1,0:T(8,128)S(1)} %get-tuple-element.55.refs_1_, bf16[256,768]{1,0:T(8,128)(2,1)S(1)} %get-tuple-element.56.refs_2_, ...), custom_call_target="tpu_custom_call" | custom-call | tf_op jit(solution)/shard_map/attn_backward/pallas_call | solution.py:39
  103.8 1.3 collective-permute-start.17
  105.5 2.2 %grad_for_self.5 = (bf16[4,96,1152]{2,1,0:T(8,128)(2,1)S(1)}, bf16[4,96,1152]{2,1,0:T(8,128)(2,1)S(1)}) custom-call(s32[4]{0:T(128)S(1)} %pad_add_fusion.place, bf16[256,768]{1,0:T(8,128)(2,1)S(1)} %get-tuple-element.70.refs_0_, bf16[256,2304]{1,0:T(8,128)(2,1)S(1)} %get-tuple-element.66.refs_1_.refs_0_, ...), custom_call_target="tpu_custom_call" | custom-call | tf_op jit(solution)/shard_map/grad_for_self/pallas_call | solution.py:39
  107.7 1.3 collective-permute-start.20
  109.0 5.0 %collective-permute-done.17.refs_1_ = bf16[4,144,384]{2,1,0:T(8,128)(2,1)S(1)} collective-permute-done((bf16[4,144,384]{2,1,0:T(8,128)(2,1)S(1)}, bf16[4,144,384]{2,1,0:T(8,128)(2,1)S(1)}, u32[]{:S(2)}, u32[]{:S(2)}) %collective-permute-start.17) | collective-permute-done | bytes 442400 | tf_op jit(solution)/shard_map/ppermute | solution.py:457
  115.8 2.9 %attn_in_backward.1.refs_2_ = bf16[256,768]{1,0:T(8,128)(2,1)} custom-call(s32[4]{0:T(128)S(1)} %pad_add_fusion.place, bf16[256,2304]{1,0:T(8,128)(2,1)S(1)} %get-tuple-element.66.refs_1_.refs_0_, f32[256,768]{1,0:T(8,128)S(1)} %get-tuple-element.67.refs_1_, f32[2,768]{1,0:T(2,128)S(1)} %pad_maximum_fusion.4.refs_0_.refs_2_, ...), custom_call_target="tpu_custom_call" | custom-call | tf_op jit(solution)/shard_map/attn_in_backward/pallas_call | solution.py:39
  118.8 8.7 %collective-permute-done.20.refs_1_ = bf16[4,96,1152]{2,1,0:T(8,128)(2,1)S(1)} collective-permute-done((bf16[4,96,1152]{2,1,0:T(8,128)(2,1)S(1)}, bf16[4,96,1152]{2,1,0:T(8,128)(2,1)S(1)}, u32[]{:S(2)}, u32[]{:S(2)}) %collective-permute-start.20) | collective-permute-done | bytes 884768 | tf_op jit(solution)/shard_map/ppermute | solution.py:457
  130.1 2.9 %collective-permute-done.22.refs_1_ = bf16[4,48,2176]{2,1,0:T(8,128)(2,1)S(1)} collective-permute-done((bf16[4,48,2176]{2,1,0:T(8,128)(2,1)S(1)}, bf16[4,48,2176]{2,1,0:T(8,128)(2,1)S(1)}, u32[]{:S(2)}, u32[]{:S(2)}) %collective-permute-start.22) | collective-permute-done | bytes 835616 | tf_op jit(solution)/shard_map/ppermute | solution.py:457
  133.8 1.6 collective-permute-start.27
  135.4 1.4 collective-permute-start.28
  136.8 1.2 collective-permute-done.21.refs_1_
  139.3 11.5 %collective-permute-done.27.refs_2_ = bf16[48,2176]{1,0:T(8,128)(2,1)S(1)} collective-permute-done((bf16[48,2176]{1,0:T(8,128)(2,1)S(1)}, bf16[48,2176]{1,0:T(8,128)(2,1)S(1)}, u32[]{:S(2)}, u32[]{:S(2)}) %collective-permute-start.27) | collective-permute-done | bytes 208928 | tf_op jit(solution)/shard_map/ppermute | solution.py:460
  150.8 3.6 %collective-permute-done.28.refs_3_ = bf16[48,2176]{1,0:T(8,128)(2,1)S(1)} collective-permute-done((bf16[48,2176]{1,0:T(8,128)(2,1)S(1)}, bf16[48,2176]{1,0:T(8,128)(2,1)S(1)}, u32[]{:S(2)}, u32[]{:S(2)}) %collective-permute-start.28) | collective-permute-done | bytes 208928 | tf_op jit(solution)/shard_map/ppermute | solution.py:460
  156.1 1.5 collective-permute-start.25
  157.6 3.0 %collective-permute-done.23.refs_1_ = bf16[48,1152]{1,0:T(8,128)(2,1)S(1)} collective-permute-done((bf16[48,1152]{1,0:T(8,128)(2,1)S(1)}, bf16[48,1152]{1,0:T(8,128)(2,1)S(1)}, u32[]{:S(2)}, u32[]{:S(2)}) %collective-permute-start.23) | collective-permute-done | bytes 110624 | tf_op jit(solution)/shard_map/ppermute | solution.py:460
  160.6 5.1 %collective-permute-done.24.refs_2_ = bf16[48,1152]{1,0:T(8,128)(2,1)S(1)} collective-permute-done((bf16[48,1152]{1,0:T(8,128)(2,1)S(1)}, bf16[48,1152]{1,0:T(8,128)(2,1)S(1)}, u32[]{:S(2)}, u32[]{:S(2)}) %collective-permute-start.24) | collective-permute-done | bytes 110624 | tf_op jit(solution)/shard_map/ppermute | solution.py:460
  165.7 1.5 collective-permute-done.25.refs_3_
  169.9 4.2 %collective-permute-done.29.refs_1_ = bf16[48,1152]{1,0:T(8,128)(2,1)S(1)} collective-permute-done((bf16[48,1152]{1,0:T(8,128)(2,1)S(1)}, bf16[48,1152]{1,0:T(8,128)(2,1)S(1)}, u32[]{:S(2)}, u32[]{:S(2)}) %collective-permute-start.29) | collective-permute-done | bytes 110624 | tf_op jit(solution)/shard_map/ppermute | solution.py:457
  174.7 2.1 %collective-permute-done.32.refs_1_ = bf16[2,48,2176]{2,1,0:T(8,128)(2,1)S(1)} collective-permute-done((bf16[2,48,2176]{2,1,0:T(8,128)(2,1)S(1)}, bf16[2,48,2176]{2,1,0:T(8,128)(2,1)S(1)}, u32[]{:S(2)}, u32[]{:S(2)}) %collective-permute-start.32) | collective-permute-done | bytes 417824 | tf_op jit(solution)/shard_map/ppermute | solution.py:457
  177.4 1.2 collective-permute-start.33
  179.4 1.3 collective-permute-done.33.refs_2_
  180.6 2.6 %place_mlp.1 = (f32[192,2304]{1,0:T(8,128)}, f32[192,768]{1,0:T(8,128)}, f32[288,768]{1,0:T(8,128)}, f32[1,192]{1,0:T(1,128)}) custom-call(s32[4]{0:T(128)S(1)} %pad_add_fusion.place, f32[1,192]{1,0:T(1,128)S(1)} %bitcast.39, bf16[2,2,48,2176]{3,2,1,0:T(8,128)(2,1)S(1)} %join.10.refs_1_, bf16[2,2,48,2176]{3,2,1,0:T(8,128)(2,1)S(1)} %collective-permute-done.33.refs_2_, ...), custom_call_target="tpu_custom_call" | custom-call | tf_op jit(solution)/shard_map/place_mlp/pallas_call | solution.py:39
  183.7 1.5 copy-done.1
  186.8 1.4 collective-permute-done.34.refs_2_
  188.2 2.1 %place_qkv.1 = (f32[192,2304]{1,0:T(8,128)}, f32[1,192]{1,0:T(1,128)}) custom-call(s32[4]{0:T(128)S(1)} %pad_add_fusion.place, f32[1,192]{1,0:T(1,128)S(1)} %bitcast.40, bf16[2,2,48,1152]{3,2,1,0:T(8,128)(2,1)S(1)} %join.11.refs_1_, bf16[2,2,48,1152]{3,2,1,0:T(8,128)(2,1)S(1)} %collective-permute-done.34.refs_2_, bf16[192,2304]{1,0:T(8,128)(2,1)S(1)} %copy-done, ...), custom_call_target="tpu_custom_call" | custom-call | tf_op jit(solution)/shard_map/place_qkv/pallas_call | solution.py:39
  (134 shorter events, 35.1 us)
Async XLA Ops:
  2.3 7.2 %collective-permute-start = (bf16[48,1280]{1,0:T(8,128)(2,1)S(1)}, bf16[48,1280]{1,0:T(8,128)(2,1)S(1)}, u32[]{:S(2)}, u32[]{:S(2)}) collective-permute-start(bf16[48,1280]{1,0:T(8,128)(2,1)S(1)} %pad_maximum_fusion.3), channel_id=1, source_target_pairs={{0,1},{1,2},{2,3},{3,0},{4,5},{5,6},{6,7},{7,4},{8,9},{9,10},{10,1... | collective-permute-start | bytes 368648 | tf_op jit(solution)/shard_map/ppermute | solution.py:460
  3.7 9.9 %collective-permute-start.1 = (bf16[48,1280]{1,0:T(8,128)(2,1)S(1)}, bf16[48,1280]{1,0:T(8,128)(2,1)S(1)}, u32[]{:S(2)}, u32[]{:S(2)}) collective-permute-start(bf16[48,1280]{1,0:T(8,128)(2,1)S(1)} %pad_maximum_fusion.3), channel_id=1, source_target_pairs={{0,2},{1,3},{2,0},{3,1},{4,6},{5,7},{6,4},{7,5},{8,10},{9,11},{10,... | collective-permute-start | bytes 368648 | tf_op jit(solution)/shard_map/ppermute | solution.py:460
  4.8 11.6 %collective-permute-start.2 = (bf16[48,1280]{1,0:T(8,128)(2,1)S(1)}, bf16[48,1280]{1,0:T(8,128)(2,1)S(1)}, u32[]{:S(2)}, u32[]{:S(2)}) collective-permute-start(bf16[48,1280]{1,0:T(8,128)(2,1)S(1)} %pad_maximum_fusion.3), channel_id=1, source_target_pairs={{0,3},{1,0},{2,1},{3,2},{4,7},{5,4},{6,5},{7,6},{8,11},{9,8},{10,9... | collective-permute-start | bytes 368648 | tf_op jit(solution)/shard_map/ppermute | solution.py:460
  8.2 10.1 %dynamic-slice-start = ((bf16[192,2304]{1,0:T(8,128)(2,1)}, s32[]{:T(128)}, s32[]{:T(128)}), bf16[48,1152]{1,0:T(8,128)(2,1)S(1)}, s32[]{:S(2)}) async-start(bf16[192,2304]{1,0:T(8,128)(2,1)} %refs_3_.6, s32[]{:T(128)} %select_n.42, s32[]{:T(128)} %select_n.43), calls=%async_computation | async-start | bytes 221696 | tf_op jit(solution)/shard_map/dynamic_slice | solution.py:514
  8.3 10.0 %dynamic-slice-start.1 = ((bf16[192,768]{1,0:T(8,128)(2,1)}, s32[]{:T(128)}, s32[]{:T(128)}), bf16[48,384]{1,0:T(8,128)(2,1)S(1)}, s32[]{:S(2)}) async-start(bf16[192,768]{1,0:T(8,128)(2,1)} %refs_5_.3, s32[]{:T(128)} %select_n.42, s32[]{:T(128)} %select_n.49), calls=%async_computation.1 | async-start | bytes 74240 | tf_op jit(solution)/shard_map/dynamic_slice | solution.py:514
  9.5 14.8 %copy-start.12 = (f32[256,128]{1,0:T(8,128)}, f32[256,128]{1,0:T(8,128)S(1)}, u32[]{:S(2)}) copy-start(f32[256,128]{1,0:T(8,128)S(1)} %get-tuple-element.101.refs_3_.refs_1_) | copy-start | bytes 393220
  9.5 14.8 %copy-start.15 = (f32[256,128]{1,0:T(8,128)}, f32[256,128]{1,0:T(8,128)S(1)}, u32[]{:S(2)}) copy-start(f32[256,128]{1,0:T(8,128)S(1)} %get-tuple-element.102.refs_4_.refs_2_) | copy-start | bytes 393220
  17.0 7.3 %collective-permute-start.3 = (bf16[3,48,1152]{2,1,0:T(8,128)(2,1)S(1)}, bf16[3,48,1152]{2,1,0:T(8,128)(2,1)S(1)}, u32[]{:S(2)}, u32[]{:S(2)}) collective-permute-start(bf16[3,48,1152]{2,1,0:T(8,128)(2,1)S(1)} %get-tuple-element.51.refs_0_), channel_id=1, source_target_pairs={{0,8},{4,20},{8,0},{12,28},{16,24},{20,4},{24,16},{28,12},{1,9},{5... | collective-permute-start | bytes 995336 | tf_op jit(solution)/shard_map/ppermute | solution.py:457
  18.3 6.0 %collective-permute-start.4 = (bf16[48,2176]{1,0:T(8,128)(2,1)S(1)}, bf16[48,2176]{1,0:T(8,128)(2,1)S(1)}, u32[]{:S(2)}, u32[]{:S(2)}) collective-permute-start(bf16[48,2176]{1,0:T(8,128)(2,1)S(1)} %pad_maximum_fusion), channel_id=1, source_target_pairs={{0,1},{1,2},{2,3},{3,0},{4,5},{5,6},{6,7},{7,4},{8,9},{9,10},{10,1... | collective-permute-start | bytes 626696 | tf_op jit(solution)/shard_map/ppermute | solution.py:460
  24.9 10.6 %collective-permute-start.5 = (bf16[2,3,48,1152]{3,2,1,0:T(8,128)(2,1)S(1)}, bf16[2,3,48,1152]{3,2,1,0:T(8,128)(2,1)S(1)}, u32[]{:S(2)}, u32[]{:S(2)}) collective-permute-start(bf16[2,3,48,1152]{3,2,1,0:T(8,128)(2,1)S(1)} %join.6.refs_7_.refs_5_), channel_id=1, source_target_pairs={{0,16},{4,12},{8,24},{12,4},{16,0},{20,28},{24,8},{28,20},{1,17},{... | collective-permute-start | bytes 1990664 | tf_op jit(solution)/shard_map/ppermute | solution.py:457
  27.2 16.2 %collective-permute-start.6 = (bf16[2,3,48,1152]{3,2,1,0:T(8,128)(2,1)S(1)}, bf16[2,3,48,1152]{3,2,1,0:T(8,128)(2,1)S(1)}, u32[]{:S(2)}, u32[]{:S(2)}) collective-permute-start(bf16[2,3,48,1152]{3,2,1,0:T(8,128)(2,1)S(1)} %join.6.refs_7_.refs_5_), channel_id=1, source_target_pairs={{0,4},{4,0},{8,12},{12,8},{16,20},{20,16},{24,28},{28,24},{1,5},{5... | collective-permute-start | bytes 1990664 | tf_op jit(solution)/shard_map/ppermute | solution.py:457
  27.2 15.0 %collective-permute-start.8 = (bf16[48,2176]{1,0:T(8,128)(2,1)S(1)}, bf16[48,2176]{1,0:T(8,128)(2,1)S(1)}, u32[]{:S(2)}, u32[]{:S(2)}) collective-permute-start(bf16[48,2176]{1,0:T(8,128)(2,1)S(1)} %pad_maximum_fusion), channel_id=1, source_target_pairs={{0,2},{1,3},{2,0},{3,1},{4,6},{5,7},{6,4},{7,5},{8,10},{9,11},{10,... | collective-permute-start | bytes 626696 | tf_op jit(solution)/shard_map/ppermute | solution.py:460
  28.4 14.9 %collective-permute-start.9 = (bf16[48,2176]{1,0:T(8,128)(2,1)S(1)}, bf16[48,2176]{1,0:T(8,128)(2,1)S(1)}, u32[]{:S(2)}, u32[]{:S(2)}) collective-permute-start(bf16[48,2176]{1,0:T(8,128)(2,1)S(1)} %pad_maximum_fusion), channel_id=1, source_target_pairs={{0,3},{1,0},{2,1},{3,2},{4,7},{5,4},{6,5},{7,6},{8,11},{9,8},{10,9... | collective-permute-start | bytes 626696 | tf_op jit(solution)/shard_map/ppermute | solution.py:460
  35.5 18.1 %collective-permute-start.7 = (bf16[2,3,48,1152]{3,2,1,0:T(8,128)(2,1)S(1)}, bf16[2,3,48,1152]{3,2,1,0:T(8,128)(2,1)S(1)}, u32[]{:S(2)}, u32[]{:S(2)}) collective-permute-start(bf16[2,3,48,1152]{3,2,1,0:T(8,128)(2,1)S(1)} %collective-permute-done.5.refs_3_.refs_8_.refs_6_), channel_id=1, source_target_pairs={{0,4},{4,0},{8,12},{12,8},{16,20},{20,16},{24,28},{28,24},{1,5},{5... | collective-permute-start | bytes 1990664 | tf_op jit(solution)/shard_map/ppermute | solution.py:457
  44.2 11.1 %copy-start.24 = (s32[256]{0:T(256)S(1)}, s32[256]{0:T(256)}, u32[]{:S(2)}) copy-start(s32[256]{0:T(256)} %param.10) | copy-start | bytes 3076
  44.2 14.0 %copy-start = (bf16[192,2304]{1,0:T(8,128)(2,1)S(1)}, bf16[192,2304]{1,0:T(8,128)(2,1)}, u32[]{:S(2)}) copy-start(bf16[192,2304]{1,0:T(8,128)(2,1)} %refs_3_.7) | copy-start | bytes 2654212
  44.2 9.4 %collective-permute-start.10 = (bf16[3,48,2176]{2,1,0:T(8,128)(2,1)S(1)}, bf16[3,48,2176]{2,1,0:T(8,128)(2,1)S(1)}, u32[]{:S(2)}, u32[]{:S(2)}) collective-permute-start(bf16[3,48,2176]{2,1,0:T(8,128)(2,1)S(1)} %stack_pieces.3.refs_0_), channel_id=1, source_target_pairs={{0,8},{4,20},{8,0},{12,28},{16,24},{20,4},{24,16},{28,12},{1,9},{5... | collective-permute-start | bytes 1880072 | tf_op jit(solution)/shard_map/ppermute | solution.py:457
  54.5 17.4 %collective-permute-start.11 = (bf16[2,3,48,2176]{3,2,1,0:T(8,128)(2,1)S(1)}, bf16[2,3,48,2176]{3,2,1,0:T(8,128)(2,1)}, u32[]{:S(2)}, u32[]{:S(2)}) collective-permute-start(bf16[2,3,48,2176]{3,2,1,0:T(8,128)(2,1)S(1)} %join.7.refs_11_.refs_7_), channel_id=1, source_target_pairs={{0,16},{4,12},{8,24},{12,4},{16,0},{20,28},{24,8},{28,20},{1,17},{... | collective-permute-start | bytes 3760136 | tf_op jit(solution)/shard_map/ppermute | solution.py:457
  56.3 18.6 %collective-permute-start.12 = (bf16[2,3,48,2176]{3,2,1,0:T(8,128)(2,1)S(1)}, bf16[2,3,48,2176]{3,2,1,0:T(8,128)(2,1)S(1)}, u32[]{:S(2)}, u32[]{:S(2)}) collective-permute-start(bf16[2,3,48,2176]{3,2,1,0:T(8,128)(2,1)S(1)} %join.7.refs_11_.refs_7_), channel_id=1, source_target_pairs={{0,4},{4,0},{8,12},{12,8},{16,20},{20,16},{24,28},{28,24},{1,5},{5... | collective-permute-start | bytes 3760136 | tf_op jit(solution)/shard_map/ppermute | solution.py:457
  71.9 6.6 %copy-start.9 = (bf16[192,2304]{1,0:T(8,128)(2,1)S(1)}, bf16[192,2304]{1,0:T(8,128)(2,1)}, u32[]{:S(2)}) copy-start(bf16[192,2304]{1,0:T(8,128)(2,1)} %refs_3_.6) | copy-start | bytes 2654212
  71.9 6.6 %copy-start.11 = (bf16[256,768]{1,0:T(8,128)(2,1)S(1)}, bf16[256,768]{1,0:T(8,128)(2,1)}, u32[]{:S(2)}) copy-start(bf16[256,768]{1,0:T(8,128)(2,1)} %refs_3_.5) | copy-start | bytes 1179652
  71.9 6.6 %copy-start.18 = (bf16[256,768]{1,0:T(8,128)(2,1)S(1)}, bf16[256,768]{1,0:T(8,128)(2,1)}, u32[]{:S(2)}) copy-start(bf16[256,768]{1,0:T(8,128)(2,1)} %refs_1_.1) | copy-start | bytes 1179652
  71.9 6.6 %copy-start.22 = (bf16[288,768]{1,0:T(8,128)(2,1)S(1)}, bf16[288,768]{1,0:T(8,128)(2,1)}, u32[]{:S(2)}) copy-start(bf16[288,768]{1,0:T(8,128)(2,1)} %refs_6_.3) | copy-start | bytes 1327108
  71.9 6.6 %copy-start.23 = (bf16[192,768]{1,0:T(8,128)(2,1)S(1)}, bf16[192,768]{1,0:T(8,128)(2,1)}, u32[]{:S(2)}) copy-start(bf16[192,768]{1,0:T(8,128)(2,1)} %refs_5_.3) | copy-start | bytes 884740
  73.5 4.0 %copy-start.8 = (bf16[2,3,48,2176]{3,2,1,0:T(8,128)(2,1)}, bf16[2,3,48,2176]{3,2,1,0:T(8,128)(2,1)S(1)}, u32[]{:S(2)}) copy-start(bf16[2,3,48,2176]{3,2,1,0:T(8,128)(2,1)S(1)} %keep_copy.1.refs_8_) | copy-start | bytes 3760132
  73.5 3.9 %collective-permute-start.13 = (bf16[2,3,48,2176]{3,2,1,0:T(8,128)(2,1)S(1)}, bf16[2,3,48,2176]{3,2,1,0:T(8,128)(2,1)S(1)}, u32[]{:S(2)}, u32[]{:S(2)}) collective-permute-start(bf16[2,3,48,2176]{3,2,1,0:T(8,128)(2,1)S(1)} %keep_copy.1.refs_8_), channel_id=1, source_target_pairs={{0,4},{4,0},{8,12},{12,8},{16,20},{20,16},{24,28},{28,24},{1,5},{5... | collective-permute-start | bytes 3760136 | tf_op jit(solution)/shard_map/ppermute | solution.py:457
  87.2 4.0 %collective-permute-start.15 = (bf16[256,2304]{1,0:T(8,128)(2,1)S(1)}, bf16[256,2304]{1,0:T(8,128)(2,1)S(1)}, u32[]{:S(2)}, u32[]{:S(2)}) collective-permute-start(bf16[256,2304]{1,0:T(8,128)(2,1)S(1)} %get-tuple-element.62), channel_id=1, source_target_pairs={{0,4},{4,0},{8,12},{12,8},{16,20},{20,16},{24,28},{28,24},{1,5},{5... | collective-permute-start | bytes 3538952 | tf_op jit(solution)/shard_map/ppermute | solution.py:457
  87.6 3.6 %collective-permute-start.16 = (bf16[256,1536]{1,0:T(8,128)(2,1)S(1)}, bf16[256,1536]{1,0:T(8,128)(2,1)S(1)}, u32[]{:S(2)}, u32[]{:S(2)}) collective-permute-start(bf16[256,1536]{1,0:T(8,128)(2,1)S(1)} %get-tuple-element.63), channel_id=1, source_target_pairs={{0,4},{4,0},{8,12},{12,8},{16,20},{20,16},{24,28},{28,24},{1,5},{5... | collective-permute-start | bytes 2359304 | tf_op jit(solution)/shard_map/ppermute | solution.py:457
  87.7 7.0 %collective-permute-start.14 = (bf16[256,1536]{1,0:T(8,128)(2,1)S(1)}, bf16[256,1536]{1,0:T(8,128)(2,1)S(1)}, u32[]{:S(2)}, u32[]{:S(2)}) collective-permute-start(bf16[256,1536]{1,0:T(8,128)(2,1)S(1)} %get-tuple-element.58), channel_id=1, source_target_pairs={{0,4},{4,0},{8,12},{12,8},{16,20},{20,16},{24,28},{28,24},{1,5},{5... | collective-permute-start | bytes 2359304 | tf_op jit(solution)/shard_map/ppermute | solution.py:457
  93.9 20.2 %collective-permute-start.18 = (bf16[4,96,1536]{2,1,0:T(8,128)(2,1)S(1)}, bf16[4,96,1536]{2,1,0:T(8,128)(2,1)S(1)}, u32[]{:S(2)}, u32[]{:S(2)}) collective-permute-start(bf16[4,96,1536]{2,1,0:T(8,128)(2,1)S(1)} %get-tuple-element.69), channel_id=1, source_target_pairs={{0,8},{4,20},{8,0},{12,28},{16,24},{20,4},{24,16},{28,12},{1,9},{5... | collective-permute-start | bytes 3538952 | tf_op jit(solution)/shard_map/ppermute | solution.py:457
  103.2 2.3 %collective-permute-start.19 = (bf16[256,1152]{1,0:T(8,128)(2,1)S(1)}, bf16[256,1152]{1,0:T(8,128)(2,1)S(1)}, u32[]{:S(2)}, u32[]{:S(2)}) collective-permute-start(bf16[256,1152]{1,0:T(8,128)(2,1)S(1)} %get-tuple-element.71), channel_id=1, source_target_pairs={{0,4},{4,0},{8,12},{12,8},{16,20},{20,16},{24,28},{28,24},{1,5},{5... | collective-permute-start | bytes 1769480 | tf_op jit(solution)/shard_map/ppermute | solution.py:457
  103.8 10.2 %collective-permute-start.17 = (bf16[4,144,384]{2,1,0:T(8,128)(2,1)S(1)}, bf16[4,144,384]{2,1,0:T(8,128)(2,1)S(1)}, u32[]{:S(2)}, u32[]{:S(2)}) collective-permute-start(bf16[4,144,384]{2,1,0:T(8,128)(2,1)S(1)} %get-tuple-element.68), channel_id=1, source_target_pairs={{0,8},{4,20},{8,0},{12,28},{16,24},{20,4},{24,16},{28,12},{1,9},{5... | collective-permute-start | bytes 1327112 | tf_op jit(solution)/shard_map/ppermute | solution.py:457
  107.7 19.8 %collective-permute-start.20 = (bf16[4,96,1152]{2,1,0:T(8,128)(2,1)S(1)}, bf16[4,96,1152]{2,1,0:T(8,128)(2,1)S(1)}, u32[]{:S(2)}, u32[]{:S(2)}) collective-permute-start(bf16[4,96,1152]{2,1,0:T(8,128)(2,1)S(1)} %get-tuple-element.74), channel_id=1, source_target_pairs={{0,8},{4,20},{8,0},{12,28},{16,24},{20,4},{24,16},{28,12},{1,9},{5... | collective-permute-start | bytes 2654216 | tf_op jit(solution)/shard_map/ppermute | solution.py:457
  115.0 18.0 %collective-permute-start.22 = (bf16[4,48,2176]{2,1,0:T(8,128)(2,1)S(1)}, bf16[4,48,2176]{2,1,0:T(8,128)(2,1)S(1)}, u32[]{:S(2)}, u32[]{:S(2)}) collective-permute-start(bf16[4,48,2176]{2,1,0:T(8,128)(2,1)S(1)} %get-tuple-element.77), channel_id=1, source_target_pairs={{0,16},{4,12},{8,24},{12,4},{16,0},{20,28},{24,8},{28,20},{1,17},{... | collective-permute-start | bytes 2506760 | tf_op jit(solution)/shard_map/ppermute | solution.py:457
  129.3 8.8 %collective-permute-start.21 = (bf16[4,48,1152]{2,1,0:T(8,128)(2,1)S(1)}, bf16[4,48,1152]{2,1,0:T(8,128)(2,1)S(1)}, u32[]{:S(2)}, u32[]{:S(2)}) collective-permute-start(bf16[4,48,1152]{2,1,0:T(8,128)(2,1)S(1)} %get-tuple-element.76), channel_id=1, source_target_pairs={{0,16},{4,12},{8,24},{12,4},{16,0},{20,28},{24,8},{28,20},{1,17},{... | collective-permute-start | bytes 1327112 | tf_op jit(solution)/shard_map/ppermute | solution.py:457
  133.7 5.5 %collective-permute-start.26 = (bf16[48,2176]{1,0:T(8,128)(2,1)S(1)}, bf16[48,2176]{1,0:T(8,128)(2,1)S(1)}, u32[]{:S(2)}, u32[]{:S(2)}) collective-permute-start(bf16[48,2176]{1,0:T(8,128)(2,1)S(1)} %get-tuple-element.83), channel_id=1, source_target_pairs={{0,1},{1,2},{2,3},{3,0},{4,5},{5,6},{6,7},{7,4},{8,9},{9,10},{10,1... | collective-permute-start | bytes 626696 | tf_op jit(solution)/shard_map/ppermute | solution.py:460
  133.8 17.0 %collective-permute-start.27 = (bf16[48,2176]{1,0:T(8,128)(2,1)S(1)}, bf16[48,2176]{1,0:T(8,128)(2,1)S(1)}, u32[]{:S(2)}, u32[]{:S(2)}) collective-permute-start(bf16[48,2176]{1,0:T(8,128)(2,1)S(1)} %get-tuple-element.84), channel_id=1, source_target_pairs={{0,2},{1,3},{2,0},{3,1},{4,6},{5,7},{6,4},{7,5},{8,10},{9,11},{10,... | collective-permute-start | bytes 626696 | tf_op jit(solution)/shard_map/ppermute | solution.py:460
  135.4 19.0 %collective-permute-start.28 = (bf16[48,2176]{1,0:T(8,128)(2,1)S(1)}, bf16[48,2176]{1,0:T(8,128)(2,1)S(1)}, u32[]{:S(2)}, u32[]{:S(2)}) collective-permute-start(bf16[48,2176]{1,0:T(8,128)(2,1)S(1)} %get-tuple-element.85), channel_id=1, source_target_pairs={{0,3},{1,0},{2,1},{3,2},{4,7},{5,4},{6,5},{7,6},{8,11},{9,8},{10,9... | collective-permute-start | bytes 626696 | tf_op jit(solution)/shard_map/ppermute | solution.py:460
  155.1 12.7 %collective-permute-start.30 = (bf16[48,2176]{1,0:T(8,128)(2,1)S(1)}, bf16[48,2176]{1,0:T(8,128)(2,1)S(1)}, u32[]{:S(2)}, u32[]{:S(2)}) collective-permute-start(bf16[48,2176]{1,0:T(8,128)(2,1)S(1)} %sum_pieces.2.refs_4_.refs_0_), channel_id=1, source_target_pairs={{0,16},{4,12},{8,24},{12,4},{16,0},{20,28},{24,8},{28,20},{1,17},{... | collective-permute-start | bytes 626696 | tf_op jit(solution)/shard_map/ppermute | solution.py:457
  156.1 4.5 %collective-permute-start.23 = (bf16[48,1152]{1,0:T(8,128)(2,1)S(1)}, bf16[48,1152]{1,0:T(8,128)(2,1)S(1)}, u32[]{:S(2)}, u32[]{:S(2)}) collective-permute-start(bf16[48,1152]{1,0:T(8,128)(2,1)S(1)} %get-tuple-element.80), channel_id=1, source_target_pairs={{0,1},{1,2},{2,3},{3,0},{4,5},{5,6},{6,7},{7,4},{8,9},{9,10},{10,1... | collective-permute-start | bytes 331784 | tf_op jit(solution)/shard_map/ppermute | solution.py:460
  156.1 9.5 %collective-permute-start.24 = (bf16[48,1152]{1,0:T(8,128)(2,1)S(1)}, bf16[48,1152]{1,0:T(8,128)(2,1)S(1)}, u32[]{:S(2)}, u32[]{:S(2)}) collective-permute-start(bf16[48,1152]{1,0:T(8,128)(2,1)S(1)} %get-tuple-element.81), channel_id=1, source_target_pairs={{0,2},{1,3},{2,0},{3,1},{4,6},{5,7},{6,4},{7,5},{8,10},{9,11},{10,... | collective-permute-start | bytes 331784 | tf_op jit(solution)/shard_map/ppermute | solution.py:460
  156.1 11.1 %collective-permute-start.25 = (bf16[48,1152]{1,0:T(8,128)(2,1)S(1)}, bf16[48,1152]{1,0:T(8,128)(2,1)S(1)}, u32[]{:S(2)}, u32[]{:S(2)}) collective-permute-start(bf16[48,1152]{1,0:T(8,128)(2,1)S(1)} %get-tuple-element.82), channel_id=1, source_target_pairs={{0,3},{1,0},{2,1},{3,2},{4,7},{5,4},{6,5},{7,6},{8,11},{9,8},{10,9... | collective-permute-start | bytes 331784 | tf_op jit(solution)/shard_map/ppermute | solution.py:460
  168.4 11.0 %copy-start.27 = (bf16[192]{0:T(256)(128)(2,1)S(1)}, bf16[192]{0:T(256)(128)(2,1)}, u32[]{:S(2)}) copy-start(bf16[192]{0:T(256)(128)(2,1)} %param.14) | copy-start | bytes 1156
  168.4 8.4 %collective-permute-start.32 = (bf16[2,48,2176]{2,1,0:T(8,128)(2,1)S(1)}, bf16[2,48,2176]{2,1,0:T(8,128)(2,1)S(1)}, u32[]{:S(2)}, u32[]{:S(2)}) collective-permute-start(bf16[2,48,2176]{2,1,0:T(8,128)(2,1)S(1)} %join.8.refs_2_.refs_0_), channel_id=1, source_target_pairs={{0,8},{4,20},{8,0},{12,28},{16,24},{20,4},{24,16},{28,12},{1,9},{5... | collective-permute-start | bytes 1253384 | tf_op jit(solution)/shard_map/ppermute | solution.py:457
  169.2 4.9 %collective-permute-start.29 = (bf16[48,1152]{1,0:T(8,128)(2,1)S(1)}, bf16[48,1152]{1,0:T(8,128)(2,1)S(1)}, u32[]{:S(2)}, u32[]{:S(2)}) collective-permute-start(bf16[48,1152]{1,0:T(8,128)(2,1)S(1)} %sum_pieces.3.refs_2_.refs_0_), channel_id=1, source_target_pairs={{0,16},{4,12},{8,24},{12,4},{16,0},{20,28},{24,8},{28,20},{1,17},{... | collective-permute-start | bytes 331784 | tf_op jit(solution)/shard_map/ppermute | solution.py:457
  177.4 3.2 %collective-permute-start.33 = (bf16[2,2,48,2176]{3,2,1,0:T(8,128)(2,1)S(1)}, bf16[2,2,48,2176]{3,2,1,0:T(8,128)(2,1)S(1)}, u32[]{:S(2)}, u32[]{:S(2)}) collective-permute-start(bf16[2,2,48,2176]{3,2,1,0:T(8,128)(2,1)S(1)} %join.10.refs_1_), channel_id=1, source_target_pairs={{0,4},{4,0},{8,12},{12,8},{16,20},{20,16},{24,28},{28,24},{1,5},{5... | collective-permute-start | bytes 2506760 | tf_op jit(solution)/shard_map/ppermute | solution.py:457
  178.7 5.1 %collective-permute-start.31 = (bf16[2,48,1152]{2,1,0:T(8,128)(2,1)S(1)}, bf16[2,48,1152]{2,1,0:T(8,128)(2,1)S(1)}, u32[]{:S(2)}, u32[]{:S(2)}) collective-permute-start(bf16[2,48,1152]{2,1,0:T(8,128)(2,1)S(1)} %join.9.refs_2_.refs_4_.refs_0_), channel_id=1, source_target_pairs={{0,8},{4,20},{8,0},{12,28},{16,24},{20,4},{24,16},{28,12},{1,9},{5... | collective-permute-start | bytes 663560 | tf_op jit(solution)/shard_map/ppermute | solution.py:457
  185.8 2.4 %collective-permute-start.34 = (bf16[2,2,48,1152]{3,2,1,0:T(8,128)(2,1)S(1)}, bf16[2,2,48,1152]{3,2,1,0:T(8,128)(2,1)S(1)}, u32[]{:S(2)}, u32[]{:S(2)}) collective-permute-start(bf16[2,2,48,1152]{3,2,1,0:T(8,128)(2,1)S(1)} %join.11.refs_1_), channel_id=1, source_target_pairs={{0,4},{4,0},{8,12},{12,8},{16,20},{20,16},{24,28},{28,24},{1,5},{5... | collective-permute-start | bytes 1327112 | tf_op jit(solution)/shard_map/ppermute | solution.py:457
  (18 other events, 24.0 us)

commit v6 on v5

--- a/solution.py
+++ b/solution.py
@@ -397,7 +397,7 @@
     return jnp.broadcast_to(summed, (grad.shape[0], PAIR)).T[0:1, :] / gain
 
 
-def place_mlp(place, gain, here, other, weight, in_grad, out_grad, down_grad, gain_out):
+def place_mlp(place, gain, here, other, weight, _, in_grad, out_grad, down_grad, gain_out):
     for core, part in enumerate((here, other)):
         for flip_high in range(2):
             hi, lo = piece_rows(place, flip_high, 0, core)
@@ -609,7 +609,7 @@
         in_grad, out_grad, down_grad, gain_two_grad = run(
             place_mlp, "place_mlp",
             [shape((shard, 2 * FF), f32), shape((shard, D), f32), shape((w_down.shape[0], D), f32), shape((1, shard), f32)],
-            place, [g_mlp.astype(f32)[None, :], mlp_quarters, across(mlp_quarters, swap_core), w_in],
+            place, [g_mlp.astype(f32)[None, :], mlp_quarters, across(mlp_quarters, swap_core), w_in, w_qkv],
             (), [qkv_pair],
         )
         qkv_quarters = joined(qkv_pair, qkv_got, [in_grad])

time: 191 us -> 191 us (level)
  no operation moved by 1% of the time
where the time goes in v6:
time: 191 us; the launch traced here: 190 us
  waiting for transfers between devices  93.2 us (49%)
  Pallas kernels  47.9 us (25%)
  starting transfers between devices  32.2 us (17%)
  local copies, waits for them, and re-layouts  12.9 us (7%)
  other arithmetic  3.02 us (2%)
    ppermute x23, waiting for transfers between devices, across(): return lax.ppermute(a, 'replica', perm)  49 us
    pallas_call x24, Pallas kernels, run(): pl.pallas_call(inner, out_shape=outs, in_specs=[SMEM] + [VMEM] * count +...  47.9 us
    ppermute x12, waiting for transfers between devices, shifted(): lax.ppermute(a, 'group', [(i, (i + k) % groups) for i in range(groups)])  44.2 us
    ppermute x23, starting transfers between devices, across(): return lax.ppermute(a, 'replica', perm)  22.4 us
    unnamed x59, local copies, waits for them, and re-layouts  9.99 us
    ppermute x12, starting transfers between devices, shifted(): lax.ppermute(a, 'group', [(i, (i + k) % groups) for i in range(groups)])  9.8 us
  transfers between devices with their start and end apart: 35, of which 25 were waited for; matrix products, arithmetic and copies ran while one was open for 2% of the time, Pallas kernels for 17%

profile of v6, /device:TPU:9, one launch (start us, length us, event | category | flops | bytes accessed | tf_op | source)
XLA Modules:
  0.0 190.3 jit_solution(895912398719167733)
XLA Ops:
  2.3 1.3 collective-permute-start
  3.7 1.1 collective-permute-start.1
  4.8 1.4 collective-permute-start.2
  9.5 4.0 %collective-permute-done.1.refs_1_ = bf16[48,1280]{1,0:T(8,128)(2,1)S(1)} collective-permute-done((bf16[48,1280]{1,0:T(8,128)(2,1)S(1)}, bf16[48,1280]{1,0:T(8,128)(2,1)S(1)}, u32[]{:S(2)}, u32[]{:S(2)}) %collective-permute-start.1) | collective-permute-done | bytes 122912 | tf_op jit(solution)/shard_map/ppermute | solution.py:460
  13.6 2.8 %collective-permute-done.2.refs_2_ = bf16[48,1280]{1,0:T(8,128)(2,1)S(1)} collective-permute-done((bf16[48,1280]{1,0:T(8,128)(2,1)S(1)}, bf16[48,1280]{1,0:T(8,128)(2,1)S(1)}, u32[]{:S(2)}, u32[]{:S(2)}) %collective-permute-start.2) | collective-permute-done | bytes 122912 | tf_op jit(solution)/shard_map/ppermute | solution.py:460
  17.0 1.3 collective-permute-start.3
  18.4 5.9 %collective-permute-done.4.refs_2_.refs_0_ = bf16[48,2176]{1,0:T(8,128)(2,1)S(1)} collective-permute-done((bf16[48,2176]{1,0:T(8,128)(2,1)S(1)}, bf16[48,2176]{1,0:T(8,128)(2,1)S(1)}, u32[]{:S(2)}, u32[]{:S(2)}) %collective-permute-start.4) | collective-permute-done | bytes 208928 | tf_op jit(solution)/shard_map/ppermute | solution.py:460
  24.9 2.3 %collective-permute-start.5 = (bf16[2,3,48,1152]{3,2,1,0:T(8,128)(2,1)S(1)}, bf16[2,3,48,1152]{3,2,1,0:T(8,128)(2,1)S(1)}, u32[]{:S(2)}, u32[]{:S(2)}) collective-permute-start(bf16[2,3,48,1152]{3,2,1,0:T(8,128)(2,1)S(1)} %join.6.refs_7_.refs_5_), channel_id=1, source_target_pairs={{0,16},{4,12},{8,24},{12,4},{16,0},{20,28},{24,8},{28,20},{1,17},{... | collective-permute-start | bytes 1990664 | tf_op jit(solution)/shard_map/ppermute | solution.py:457
  27.2 1.3 collective-permute-start.8
  28.5 7.0 %collective-permute-done.5.refs_3_.refs_8_.refs_6_ = bf16[2,3,48,1152]{3,2,1,0:T(8,128)(2,1)S(1)} collective-permute-done((bf16[2,3,48,1152]{3,2,1,0:T(8,128)(2,1)S(1)}, bf16[2,3,48,1152]{3,2,1,0:T(8,128)(2,1)S(1)}, u32[]{:S(2)}, u32[]{:S(2)}) %collective-permute-start.5) | collective-permute-done | bytes 663584 | tf_op jit(solution)/shard_map/ppermute | solution.py:457
  35.5 1.8 collective-permute-start.7
  37.3 4.9 %collective-permute-done.8.refs_1_ = bf16[48,2176]{1,0:T(8,128)(2,1)S(1)} collective-permute-done((bf16[48,2176]{1,0:T(8,128)(2,1)S(1)}, bf16[48,2176]{1,0:T(8,128)(2,1)S(1)}, u32[]{:S(2)}, u32[]{:S(2)}) %collective-permute-start.8) | collective-permute-done | bytes 208928 | tf_op jit(solution)/shard_map/ppermute | solution.py:460
  42.2 1.2 collective-permute-done.9.refs_2_
  45.0 8.6 %collective-permute-done.10.refs_1_ = bf16[3,48,2176]{2,1,0:T(8,128)(2,1)S(1)} collective-permute-done((bf16[3,48,2176]{2,1,0:T(8,128)(2,1)S(1)}, bf16[3,48,2176]{2,1,0:T(8,128)(2,1)S(1)}, u32[]{:S(2)}, u32[]{:S(2)}) %collective-permute-start.10) | collective-permute-done | bytes 626720 | tf_op jit(solution)/shard_map/ppermute | solution.py:457
  56.3 2.0 %collective-permute-start.12 = (bf16[2,3,48,2176]{3,2,1,0:T(8,128)(2,1)S(1)}, bf16[2,3,48,2176]{3,2,1,0:T(8,128)(2,1)S(1)}, u32[]{:S(2)}, u32[]{:S(2)}) collective-permute-start(bf16[2,3,48,2176]{3,2,1,0:T(8,128)(2,1)S(1)} %join.7.refs_11_.refs_7_), channel_id=1, source_target_pairs={{0,4},{4,0},{8,12},{12,8},{16,20},{20,16},{24,28},{28,24},{1,5},{5... | collective-permute-start | bytes 3760136 | tf_op jit(solution)/shard_map/ppermute | solution.py:457
  64.1 7.8 %attn_forward.1 = (bf16[256,768]{1,0:T(8,128)(2,1)S(1)}, bf16[256,2304]{1,0:T(8,128)(2,1)S(1)}, bf16[256,768]{1,0:T(8,128)(2,1)S(1)}, f32[256,128]{1,0:T(8,128)S(1)}, bf16[256,1536]{1,0:T(8,128)(2,1)S(1)}) custom-call(s32[4]{0:T(128)S(1)} %pad_add_fusion.place, f32[2,768]{1,0:T(2,128)S(1)} %pad_maximum_fusion.4.refs_0_.refs_2_, f32[256,128]{1,0:T(8,128)S(1)} %copy-done.13, ...), custom_call_target="tpu_custom_call" | custom-call | tf_op jit(solution)/shard_map/attn_forward/pallas_call | solution.py:39
  72.0 1.5 keep_copy.1.refs_8_
  73.5 1.4 collective-permute-start.13
  74.9 2.6 %collective-permute-done.13.refs_10_ = bf16[2,3,48,2176]{3,2,1,0:T(8,128)(2,1)S(1)} collective-permute-done((bf16[2,3,48,2176]{3,2,1,0:T(8,128)(2,1)S(1)}, bf16[2,3,48,2176]{3,2,1,0:T(8,128)(2,1)S(1)}, u32[]{:S(2)}, u32[]{:S(2)}) %collective-permute-start.13) | collective-permute-done | bytes 1253408 | tf_op jit(solution)/shard_map/ppermute | solution.py:457
  78.5 8.7 %feed_forward.1 = (bf16[256,768]{1,0:T(8,128)(2,1)}, f32[256,768]{1,0:T(8,128)S(1)}, bf16[256,768]{1,0:T(8,128)(2,1)S(1)}, bf16[256,768]{1,0:T(8,128)(2,1)S(1)},...) custom-call(s32[4]{0:T(128)S(1)} %pad_add_fusion.place, ...), custom_call_target="tpu_custom_call" | custom-call | tf_op jit(solution)/shard_map/feed_forward/pallas_call | solution.py:39
  88.1 3.1 %collective-permute-done.16.refs_5_.refs_2_ = bf16[256,1536]{1,0:T(8,128)(2,1)S(1)} collective-permute-done((bf16[256,1536]{1,0:T(8,128)(2,1)S(1)}, bf16[256,1536]{1,0:T(8,128)(2,1)S(1)}, u32[]{:S(2)}, u32[]{:S(2)}) %collective-permute-start.16) | collective-permute-done | bytes 786464 | tf_op jit(solution)/shard_map/ppermute | solution.py:457
  91.2 2.7 %grad_for_self.3 = (bf16[4,96,1536]{2,1,0:T(8,128)(2,1)S(1)}, bf16[4,96,1536]{2,1,0:T(8,128)(2,1)S(1)}) custom-call(s32[4]{0:T(128)S(1)} %pad_add_fusion.place, bf16[256,768]{1,0:T(8,128)(2,1)S(1)} %get-tuple-element.59.refs_0_, bf16[256,2304]{1,0:T(8,128)(2,1)S(1)} %get-tuple-element.60.refs_1_, bf16[256,768]{1,0:T(8,128)(2,1)S(1)} %get-tuple-element.52.refs_1_.refs_2_, ...), custom_call_target="tpu_custom_call" | custom-call | tf_op jit(solution)/shard_map/grad_for_self/pallas_call | solution.py:39
  94.8 1.7 grad_for_self.4
  96.5 6.7 %attn_backward.1 = (bf16[256,2304]{1,0:T(8,128)(2,1)S(1)}, bf16[256,1152]{1,0:T(8,128)(2,1)S(1)}) custom-call(s32[4]{0:T(128)S(1)} %pad_add_fusion.place, bf16[256,2304]{1,0:T(8,128)(2,1)S(1)} %get-tuple-element.54.refs_0_, f32[256,128]{1,0:T(8,128)S(1)} %get-tuple-element.55.refs_1_, bf16[256,768]{1,0:T(8,128)(2,1)S(1)} %get-tuple-element.56.refs_2_, ...), custom_call_target="tpu_custom_call" | custom-call | tf_op jit(solution)/shard_map/attn_backward/pallas_call | solution.py:39
  103.9 1.2 collective-permute-start.17
  105.5 2.2 %grad_for_self.5 = (bf16[4,96,1152]{2,1,0:T(8,128)(2,1)S(1)}, bf16[4,96,1152]{2,1,0:T(8,128)(2,1)S(1)}) custom-call(s32[4]{0:T(128)S(1)} %pad_add_fusion.place, bf16[256,768]{1,0:T(8,128)(2,1)S(1)} %get-tuple-element.70.refs_0_, bf16[256,2304]{1,0:T(8,128)(2,1)S(1)} %get-tuple-element.66.refs_1_.refs_0_, ...), custom_call_target="tpu_custom_call" | custom-call | tf_op jit(solution)/shard_map/grad_for_self/pallas_call | solution.py:39
  107.7 1.3 collective-permute-start.20
  109.0 5.0 %collective-permute-done.17.refs_1_ = bf16[4,144,384]{2,1,0:T(8,128)(2,1)S(1)} collective-permute-done((bf16[4,144,384]{2,1,0:T(8,128)(2,1)S(1)}, bf16[4,144,384]{2,1,0:T(8,128)(2,1)S(1)}, u32[]{:S(2)}, u32[]{:S(2)}) %collective-permute-start.17) | collective-permute-done | bytes 442400 | tf_op jit(solution)/shard_map/ppermute | solution.py:457
  115.8 3.0 %attn_in_backward.1.refs_2_ = bf16[256,768]{1,0:T(8,128)(2,1)} custom-call(s32[4]{0:T(128)S(1)} %pad_add_fusion.place, bf16[256,2304]{1,0:T(8,128)(2,1)S(1)} %get-tuple-element.66.refs_1_.refs_0_, f32[256,768]{1,0:T(8,128)S(1)} %get-tuple-element.67.refs_1_, f32[2,768]{1,0:T(2,128)S(1)} %pad_maximum_fusion.4.refs_0_.refs_2_, ...), custom_call_target="tpu_custom_call" | custom-call | tf_op jit(solution)/shard_map/attn_in_backward/pallas_call | solution.py:39
  118.8 8.7 %collective-permute-done.20.refs_1_ = bf16[4,96,1152]{2,1,0:T(8,128)(2,1)S(1)} collective-permute-done((bf16[4,96,1152]{2,1,0:T(8,128)(2,1)S(1)}, bf16[4,96,1152]{2,1,0:T(8,128)(2,1)S(1)}, u32[]{:S(2)}, u32[]{:S(2)}) %collective-permute-start.20) | collective-permute-done | bytes 884768 | tf_op jit(solution)/shard_map/ppermute | solution.py:457
  130.1 2.9 %collective-permute-done.22.refs_1_ = bf16[4,48,2176]{2,1,0:T(8,128)(2,1)S(1)} collective-permute-done((bf16[4,48,2176]{2,1,0:T(8,128)(2,1)S(1)}, bf16[4,48,2176]{2,1,0:T(8,128)(2,1)S(1)}, u32[]{:S(2)}, u32[]{:S(2)}) %collective-permute-start.22) | collective-permute-done | bytes 835616 | tf_op jit(solution)/shard_map/ppermute | solution.py:457
  133.8 1.6 collective-permute-start.27
  135.4 1.4 collective-permute-start.28
  136.8 1.2 collective-permute-done.21.refs_1_
  139.3 11.5 %collective-permute-done.27.refs_2_ = bf16[48,2176]{1,0:T(8,128)(2,1)S(1)} collective-permute-done((bf16[48,2176]{1,0:T(8,128)(2,1)S(1)}, bf16[48,2176]{1,0:T(8,128)(2,1)S(1)}, u32[]{:S(2)}, u32[]{:S(2)}) %collective-permute-start.27) | collective-permute-done | bytes 208928 | tf_op jit(solution)/shard_map/ppermute | solution.py:460
  150.8 3.6 %collective-permute-done.28.refs_3_ = bf16[48,2176]{1,0:T(8,128)(2,1)S(1)} collective-permute-done((bf16[48,2176]{1,0:T(8,128)(2,1)S(1)}, bf16[48,2176]{1,0:T(8,128)(2,1)S(1)}, u32[]{:S(2)}, u32[]{:S(2)}) %collective-permute-start.28) | collective-permute-done | bytes 208928 | tf_op jit(solution)/shard_map/ppermute | solution.py:460
  156.1 1.5 collective-permute-start.25
  157.6 3.0 %collective-permute-done.23.refs_1_ = bf16[48,1152]{1,0:T(8,128)(2,1)S(1)} collective-permute-done((bf16[48,1152]{1,0:T(8,128)(2,1)S(1)}, bf16[48,1152]{1,0:T(8,128)(2,1)S(1)}, u32[]{:S(2)}, u32[]{:S(2)}) %collective-permute-start.23) | collective-permute-done | bytes 110624 | tf_op jit(solution)/shard_map/ppermute | solution.py:460
  160.6 5.1 %collective-permute-done.24.refs_2_ = bf16[48,1152]{1,0:T(8,128)(2,1)S(1)} collective-permute-done((bf16[48,1152]{1,0:T(8,128)(2,1)S(1)}, bf16[48,1152]{1,0:T(8,128)(2,1)S(1)}, u32[]{:S(2)}, u32[]{:S(2)}) %collective-permute-start.24) | collective-permute-done | bytes 110624 | tf_op jit(solution)/shard_map/ppermute | solution.py:460
  165.7 1.5 collective-permute-done.25.refs_3_
  169.9 4.2 %collective-permute-done.29.refs_1_ = bf16[48,1152]{1,0:T(8,128)(2,1)S(1)} collective-permute-done((bf16[48,1152]{1,0:T(8,128)(2,1)S(1)}, bf16[48,1152]{1,0:T(8,128)(2,1)S(1)}, u32[]{:S(2)}, u32[]{:S(2)}) %collective-permute-start.29) | collective-permute-done | bytes 110624 | tf_op jit(solution)/shard_map/ppermute | solution.py:457
  174.7 2.1 %collective-permute-done.32.refs_1_ = bf16[2,48,2176]{2,1,0:T(8,128)(2,1)S(1)} collective-permute-done((bf16[2,48,2176]{2,1,0:T(8,128)(2,1)S(1)}, bf16[2,48,2176]{2,1,0:T(8,128)(2,1)S(1)}, u32[]{:S(2)}, u32[]{:S(2)}) %collective-permute-start.32) | collective-permute-done | bytes 417824 | tf_op jit(solution)/shard_map/ppermute | solution.py:457
  177.4 1.2 collective-permute-start.33
  179.4 1.3 collective-permute-done.33.refs_2_
  180.6 2.6 %place_mlp.1 = (f32[192,2304]{1,0:T(8,128)}, f32[192,768]{1,0:T(8,128)}, f32[288,768]{1,0:T(8,128)}, f32[1,192]{1,0:T(1,128)}) custom-call(s32[4]{0:T(128)S(1)} %pad_add_fusion.place, f32[1,192]{1,0:T(1,128)S(1)} %bitcast.39, bf16[2,2,48,2176]{3,2,1,0:T(8,128)(2,1)S(1)} %join.10.refs_1_, bf16[2,2,48,2176]{3,2,1,0:T(8,128)(2,1)S(1)} %collective-permute-done.33.refs_2_, ...), custom_call_target="tpu_custom_call" | custom-call | tf_op jit(solution)/shard_map/place_mlp/pallas_call | solution.py:39
  183.7 1.5 copy-done.1
  186.8 1.4 collective-permute-done.34.refs_2_
  188.2 2.0 %place_qkv.1 = (f32[192,2304]{1,0:T(8,128)}, f32[1,192]{1,0:T(1,128)}) custom-call(s32[4]{0:T(128)S(1)} %pad_add_fusion.place, f32[1,192]{1,0:T(1,128)S(1)} %bitcast.40, bf16[2,2,48,1152]{3,2,1,0:T(8,128)(2,1)S(1)} %join.11.refs_1_, bf16[2,2,48,1152]{3,2,1,0:T(8,128)(2,1)S(1)} %collective-permute-done.34.refs_2_, bf16[192,2304]{1,0:T(8,128)(2,1)S(1)} %copy-done, ...), custom_call_target="tpu_custom_call" | custom-call | tf_op jit(solution)/shard_map/place_qkv/pallas_call | solution.py:39
  (134 shorter events, 35.1 us)
Async XLA Ops:
  2.3 7.2 %collective-permute-start = (bf16[48,1280]{1,0:T(8,128)(2,1)S(1)}, bf16[48,1280]{1,0:T(8,128)(2,1)S(1)}, u32[]{:S(2)}, u32[]{:S(2)}) collective-permute-start(bf16[48,1280]{1,0:T(8,128)(2,1)S(1)} %pad_maximum_fusion.3), channel_id=1, source_target_pairs={{0,1},{1,2},{2,3},{3,0},{4,5},{5,6},{6,7},{7,4},{8,9},{9,10},{10,1... | collective-permute-start | bytes 368648 | tf_op jit(solution)/shard_map/ppermute | solution.py:460
  3.7 9.9 %collective-permute-start.1 = (bf16[48,1280]{1,0:T(8,128)(2,1)S(1)}, bf16[48,1280]{1,0:T(8,128)(2,1)S(1)}, u32[]{:S(2)}, u32[]{:S(2)}) collective-permute-start(bf16[48,1280]{1,0:T(8,128)(2,1)S(1)} %pad_maximum_fusion.3), channel_id=1, source_target_pairs={{0,2},{1,3},{2,0},{3,1},{4,6},{5,7},{6,4},{7,5},{8,10},{9,11},{10,... | collective-permute-start | bytes 368648 | tf_op jit(solution)/shard_map/ppermute | solution.py:460
  4.8 11.6 %collective-permute-start.2 = (bf16[48,1280]{1,0:T(8,128)(2,1)S(1)}, bf16[48,1280]{1,0:T(8,128)(2,1)S(1)}, u32[]{:S(2)}, u32[]{:S(2)}) collective-permute-start(bf16[48,1280]{1,0:T(8,128)(2,1)S(1)} %pad_maximum_fusion.3), channel_id=1, source_target_pairs={{0,3},{1,0},{2,1},{3,2},{4,7},{5,4},{6,5},{7,6},{8,11},{9,8},{10,9... | collective-permute-start | bytes 368648 | tf_op jit(solution)/shard_map/ppermute | solution.py:460
  8.2 10.1 %dynamic-slice-start = ((bf16[192,2304]{1,0:T(8,128)(2,1)}, s32[]{:T(128)}, s32[]{:T(128)}), bf16[48,1152]{1,0:T(8,128)(2,1)S(1)}, s32[]{:S(2)}) async-start(bf16[192,2304]{1,0:T(8,128)(2,1)} %refs_3_.6, s32[]{:T(128)} %select_n.42, s32[]{:T(128)} %select_n.43), calls=%async_computation | async-start | bytes 221696 | tf_op jit(solution)/shard_map/dynamic_slice | solution.py:514
  8.3 10.0 %dynamic-slice-start.1 = ((bf16[192,768]{1,0:T(8,128)(2,1)}, s32[]{:T(128)}, s32[]{:T(128)}), bf16[48,384]{1,0:T(8,128)(2,1)S(1)}, s32[]{:S(2)}) async-start(bf16[192,768]{1,0:T(8,128)(2,1)} %refs_5_.3, s32[]{:T(128)} %select_n.42, s32[]{:T(128)} %select_n.49), calls=%async_computation.1 | async-start | bytes 74240 | tf_op jit(solution)/shard_map/dynamic_slice | solution.py:514
  9.5 14.8 %copy-start.12 = (f32[256,128]{1,0:T(8,128)}, f32[256,128]{1,0:T(8,128)S(1)}, u32[]{:S(2)}) copy-start(f32[256,128]{1,0:T(8,128)S(1)} %get-tuple-element.101.refs_3_.refs_1_) | copy-start | bytes 393220
  9.5 14.8 %copy-start.15 = (f32[256,128]{1,0:T(8,128)}, f32[256,128]{1,0:T(8,128)S(1)}, u32[]{:S(2)}) copy-start(f32[256,128]{1,0:T(8,128)S(1)} %get-tuple-element.102.refs_4_.refs_2_) | copy-start | bytes 393220
  17.0 7.3 %collective-permute-start.3 = (bf16[3,48,1152]{2,1,0:T(8,128)(2,1)S(1)}, bf16[3,48,1152]{2,1,0:T(8,128)(2,1)S(1)}, u32[]{:S(2)}, u32[]{:S(2)}) collective-permute-start(bf16[3,48,1152]{2,1,0:T(8,128)(2,1)S(1)} %get-tuple-element.51.refs_0_), channel_id=1, source_target_pairs={{0,8},{4,20},{8,0},{12,28},{16,24},{20,4},{24,16},{28,12},{1,9},{5... | collective-permute-start | bytes 995336 | tf_op jit(solution)/shard_map/ppermute | solution.py:457
  18.3 6.0 %collective-permute-start.4 = (bf16[48,2176]{1,0:T(8,128)(2,1)S(1)}, bf16[48,2176]{1,0:T(8,128)(2,1)S(1)}, u32[]{:S(2)}, u32[]{:S(2)}) collective-permute-start(bf16[48,2176]{1,0:T(8,128)(2,1)S(1)} %pad_maximum_fusion), channel_id=1, source_target_pairs={{0,1},{1,2},{2,3},{3,0},{4,5},{5,6},{6,7},{7,4},{8,9},{9,10},{10,1... | collective-permute-start | bytes 626696 | tf_op jit(solution)/shard_map/ppermute | solution.py:460
  24.9 10.6 %collective-permute-start.5 = (bf16[2,3,48,1152]{3,2,1,0:T(8,128)(2,1)S(1)}, bf16[2,3,48,1152]{3,2,1,0:T(8,128)(2,1)S(1)}, u32[]{:S(2)}, u32[]{:S(2)}) collective-permute-start(bf16[2,3,48,1152]{3,2,1,0:T(8,128)(2,1)S(1)} %join.6.refs_7_.refs_5_), channel_id=1, source_target_pairs={{0,16},{4,12},{8,24},{12,4},{16,0},{20,28},{24,8},{28,20},{1,17},{... | collective-permute-start | bytes 1990664 | tf_op jit(solution)/shard_map/ppermute | solution.py:457
  27.2 16.2 %collective-permute-start.6 = (bf16[2,3,48,1152]{3,2,1,0:T(8,128)(2,1)S(1)}, bf16[2,3,48,1152]{3,2,1,0:T(8,128)(2,1)S(1)}, u32[]{:S(2)}, u32[]{:S(2)}) collective-permute-start(bf16[2,3,48,1152]{3,2,1,0:T(8,128)(2,1)S(1)} %join.6.refs_7_.refs_5_), channel_id=1, source_target_pairs={{0,4},{4,0},{8,12},{12,8},{16,20},{20,16},{24,28},{28,24},{1,5},{5... | collective-permute-start | bytes 1990664 | tf_op jit(solution)/shard_map/ppermute | solution.py:457
  27.2 15.0 %collective-permute-start.8 = (bf16[48,2176]{1,0:T(8,128)(2,1)S(1)}, bf16[48,2176]{1,0:T(8,128)(2,1)S(1)}, u32[]{:S(2)}, u32[]{:S(2)}) collective-permute-start(bf16[48,2176]{1,0:T(8,128)(2,1)S(1)} %pad_maximum_fusion), channel_id=1, source_target_pairs={{0,2},{1,3},{2,0},{3,1},{4,6},{5,7},{6,4},{7,5},{8,10},{9,11},{10,... | collective-permute-start | bytes 626696 | tf_op jit(solution)/shard_map/ppermute | solution.py:460
  28.4 14.9 %collective-permute-start.9 = (bf16[48,2176]{1,0:T(8,128)(2,1)S(1)}, bf16[48,2176]{1,0:T(8,128)(2,1)S(1)}, u32[]{:S(2)}, u32[]{:S(2)}) collective-permute-start(bf16[48,2176]{1,0:T(8,128)(2,1)S(1)} %pad_maximum_fusion), channel_id=1, source_target_pairs={{0,3},{1,0},{2,1},{3,2},{4,7},{5,4},{6,5},{7,6},{8,11},{9,8},{10,9... | collective-permute-start | bytes 626696 | tf_op jit(solution)/shard_map/ppermute | solution.py:460
  35.5 18.1 %collective-permute-start.7 = (bf16[2,3,48,1152]{3,2,1,0:T(8,128)(2,1)S(1)}, bf16[2,3,48,1152]{3,2,1,0:T(8,128)(2,1)S(1)}, u32[]{:S(2)}, u32[]{:S(2)}) collective-permute-start(bf16[2,3,48,1152]{3,2,1,0:T(8,128)(2,1)S(1)} %collective-permute-done.5.refs_3_.refs_8_.refs_6_), channel_id=1, source_target_pairs={{0,4},{4,0},{8,12},{12,8},{16,20},{20,16},{24,28},{28,24},{1,5},{5... | collective-permute-start | bytes 1990664 | tf_op jit(solution)/shard_map/ppermute | solution.py:457
  44.2 11.1 %copy-start.24 = (s32[256]{0:T(256)S(1)}, s32[256]{0:T(256)}, u32[]{:S(2)}) copy-start(s32[256]{0:T(256)} %param.10) | copy-start | bytes 3076
  44.2 14.0 %copy-start = (bf16[192,2304]{1,0:T(8,128)(2,1)S(1)}, bf16[192,2304]{1,0:T(8,128)(2,1)}, u32[]{:S(2)}) copy-start(bf16[192,2304]{1,0:T(8,128)(2,1)} %refs_3_.7) | copy-start | bytes 2654212
  44.2 9.4 %collective-permute-start.10 = (bf16[3,48,2176]{2,1,0:T(8,128)(2,1)S(1)}, bf16[3,48,2176]{2,1,0:T(8,128)(2,1)S(1)}, u32[]{:S(2)}, u32[]{:S(2)}) collective-permute-start(bf16[3,48,2176]{2,1,0:T(8,128)(2,1)S(1)} %stack_pieces.3.refs_0_), channel_id=1, source_target_pairs={{0,8},{4,20},{8,0},{12,28},{16,24},{20,4},{24,16},{28,12},{1,9},{5... | collective-permute-start | bytes 1880072 | tf_op jit(solution)/shard_map/ppermute | solution.py:457
  54.5 17.4 %collective-permute-start.11 = (bf16[2,3,48,2176]{3,2,1,0:T(8,128)(2,1)S(1)}, bf16[2,3,48,2176]{3,2,1,0:T(8,128)(2,1)}, u32[]{:S(2)}, u32[]{:S(2)}) collective-permute-start(bf16[2,3,48,2176]{3,2,1,0:T(8,128)(2,1)S(1)} %join.7.refs_11_.refs_7_), channel_id=1, source_target_pairs={{0,16},{4,12},{8,24},{12,4},{16,0},{20,28},{24,8},{28,20},{1,17},{... | collective-permute-start | bytes 3760136 | tf_op jit(solution)/shard_map/ppermute | solution.py:457
  56.3 18.6 %collective-permute-start.12 = (bf16[2,3,48,2176]{3,2,1,0:T(8,128)(2,1)S(1)}, bf16[2,3,48,2176]{3,2,1,0:T(8,128)(2,1)S(1)}, u32[]{:S(2)}, u32[]{:S(2)}) collective-permute-start(bf16[2,3,48,2176]{3,2,1,0:T(8,128)(2,1)S(1)} %join.7.refs_11_.refs_7_), channel_id=1, source_target_pairs={{0,4},{4,0},{8,12},{12,8},{16,20},{20,16},{24,28},{28,24},{1,5},{5... | collective-permute-start | bytes 3760136 | tf_op jit(solution)/shard_map/ppermute | solution.py:457
  71.9 6.6 %copy-start.9 = (bf16[192,2304]{1,0:T(8,128)(2,1)S(1)}, bf16[192,2304]{1,0:T(8,128)(2,1)}, u32[]{:S(2)}) copy-start(bf16[192,2304]{1,0:T(8,128)(2,1)} %refs_3_.6) | copy-start | bytes 2654212
  71.9 6.6 %copy-start.11 = (bf16[256,768]{1,0:T(8,128)(2,1)S(1)}, bf16[256,768]{1,0:T(8,128)(2,1)}, u32[]{:S(2)}) copy-start(bf16[256,768]{1,0:T(8,128)(2,1)} %refs_3_.5) | copy-start | bytes 1179652
  71.9 6.6 %copy-start.18 = (bf16[256,768]{1,0:T(8,128)(2,1)S(1)}, bf16[256,768]{1,0:T(8,128)(2,1)}, u32[]{:S(2)}) copy-start(bf16[256,768]{1,0:T(8,128)(2,1)} %refs_1_.1) | copy-start | bytes 1179652
  71.9 6.6 %copy-start.22 = (bf16[288,768]{1,0:T(8,128)(2,1)S(1)}, bf16[288,768]{1,0:T(8,128)(2,1)}, u32[]{:S(2)}) copy-start(bf16[288,768]{1,0:T(8,128)(2,1)} %refs_6_.3) | copy-start | bytes 1327108
  71.9 6.6 %copy-start.23 = (bf16[192,768]{1,0:T(8,128)(2,1)S(1)}, bf16[192,768]{1,0:T(8,128)(2,1)}, u32[]{:S(2)}) copy-start(bf16[192,768]{1,0:T(8,128)(2,1)} %refs_5_.3) | copy-start | bytes 884740
  73.5 4.0 %copy-start.8 = (bf16[2,3,48,2176]{3,2,1,0:T(8,128)(2,1)}, bf16[2,3,48,2176]{3,2,1,0:T(8,128)(2,1)S(1)}, u32[]{:S(2)}) copy-start(bf16[2,3,48,2176]{3,2,1,0:T(8,128)(2,1)S(1)} %keep_copy.1.refs_8_) | copy-start | bytes 3760132
  73.5 3.9 %collective-permute-start.13 = (bf16[2,3,48,2176]{3,2,1,0:T(8,128)(2,1)S(1)}, bf16[2,3,48,2176]{3,2,1,0:T(8,128)(2,1)S(1)}, u32[]{:S(2)}, u32[]{:S(2)}) collective-permute-start(bf16[2,3,48,2176]{3,2,1,0:T(8,128)(2,1)S(1)} %keep_copy.1.refs_8_), channel_id=1, source_target_pairs={{0,4},{4,0},{8,12},{12,8},{16,20},{20,16},{24,28},{28,24},{1,5},{5... | collective-permute-start | bytes 3760136 | tf_op jit(solution)/shard_map/ppermute | solution.py:457
  87.2 4.0 %collective-permute-start.15 = (bf16[256,2304]{1,0:T(8,128)(2,1)S(1)}, bf16[256,2304]{1,0:T(8,128)(2,1)S(1)}, u32[]{:S(2)}, u32[]{:S(2)}) collective-permute-start(bf16[256,2304]{1,0:T(8,128)(2,1)S(1)} %get-tuple-element.62), channel_id=1, source_target_pairs={{0,4},{4,0},{8,12},{12,8},{16,20},{20,16},{24,28},{28,24},{1,5},{5... | collective-permute-start | bytes 3538952 | tf_op jit(solution)/shard_map/ppermute | solution.py:457
  87.6 3.6 %collective-permute-start.16 = (bf16[256,1536]{1,0:T(8,128)(2,1)S(1)}, bf16[256,1536]{1,0:T(8,128)(2,1)S(1)}, u32[]{:S(2)}, u32[]{:S(2)}) collective-permute-start(bf16[256,1536]{1,0:T(8,128)(2,1)S(1)} %get-tuple-element.63), channel_id=1, source_target_pairs={{0,4},{4,0},{8,12},{12,8},{16,20},{20,16},{24,28},{28,24},{1,5},{5... | collective-permute-start | bytes 2359304 | tf_op jit(solution)/shard_map/ppermute | solution.py:457
  87.7 7.0 %collective-permute-start.14 = (bf16[256,1536]{1,0:T(8,128)(2,1)S(1)}, bf16[256,1536]{1,0:T(8,128)(2,1)S(1)}, u32[]{:S(2)}, u32[]{:S(2)}) collective-permute-start(bf16[256,1536]{1,0:T(8,128)(2,1)S(1)} %get-tuple-element.58), channel_id=1, source_target_pairs={{0,4},{4,0},{8,12},{12,8},{16,20},{20,16},{24,28},{28,24},{1,5},{5... | collective-permute-start | bytes 2359304 | tf_op jit(solution)/shard_map/ppermute | solution.py:457
  93.9 20.2 %collective-permute-start.18 = (bf16[4,96,1536]{2,1,0:T(8,128)(2,1)S(1)}, bf16[4,96,1536]{2,1,0:T(8,128)(2,1)S(1)}, u32[]{:S(2)}, u32[]{:S(2)}) collective-permute-start(bf16[4,96,1536]{2,1,0:T(8,128)(2,1)S(1)} %get-tuple-element.69), channel_id=1, source_target_pairs={{0,8},{4,20},{8,0},{12,28},{16,24},{20,4},{24,16},{28,12},{1,9},{5... | collective-permute-start | bytes 3538952 | tf_op jit(solution)/shard_map/ppermute | solution.py:457
  103.2 2.3 %collective-permute-start.19 = (bf16[256,1152]{1,0:T(8,128)(2,1)S(1)}, bf16[256,1152]{1,0:T(8,128)(2,1)S(1)}, u32[]{:S(2)}, u32[]{:S(2)}) collective-permute-start(bf16[256,1152]{1,0:T(8,128)(2,1)S(1)} %get-tuple-element.71), channel_id=1, source_target_pairs={{0,4},{4,0},{8,12},{12,8},{16,20},{20,16},{24,28},{28,24},{1,5},{5... | collective-permute-start | bytes 1769480 | tf_op jit(solution)/shard_map/ppermute | solution.py:457
  103.9 10.2 %collective-permute-start.17 = (bf16[4,144,384]{2,1,0:T(8,128)(2,1)S(1)}, bf16[4,144,384]{2,1,0:T(8,128)(2,1)S(1)}, u32[]{:S(2)}, u32[]{:S(2)}) collective-permute-start(bf16[4,144,384]{2,1,0:T(8,128)(2,1)S(1)} %get-tuple-element.68), channel_id=1, source_target_pairs={{0,8},{4,20},{8,0},{12,28},{16,24},{20,4},{24,16},{28,12},{1,9},{5... | collective-permute-start | bytes 1327112 | tf_op jit(solution)/shard_map/ppermute | solution.py:457
  107.7 19.8 %collective-permute-start.20 = (bf16[4,96,1152]{2,1,0:T(8,128)(2,1)S(1)}, bf16[4,96,1152]{2,1,0:T(8,128)(2,1)S(1)}, u32[]{:S(2)}, u32[]{:S(2)}) collective-permute-start(bf16[4,96,1152]{2,1,0:T(8,128)(2,1)S(1)} %get-tuple-element.74), channel_id=1, source_target_pairs={{0,8},{4,20},{8,0},{12,28},{16,24},{20,4},{24,16},{28,12},{1,9},{5... | collective-permute-start | bytes 2654216 | tf_op jit(solution)/shard_map/ppermute | solution.py:457
  115.0 18.0 %collective-permute-start.22 = (bf16[4,48,2176]{2,1,0:T(8,128)(2,1)S(1)}, bf16[4,48,2176]{2,1,0:T(8,128)(2,1)S(1)}, u32[]{:S(2)}, u32[]{:S(2)}) collective-permute-start(bf16[4,48,2176]{2,1,0:T(8,128)(2,1)S(1)} %get-tuple-element.77), channel_id=1, source_target_pairs={{0,16},{4,12},{8,24},{12,4},{16,0},{20,28},{24,8},{28,20},{1,17},{... | collective-permute-start | bytes 2506760 | tf_op jit(solution)/shard_map/ppermute | solution.py:457
  129.3 8.8 %collective-permute-start.21 = (bf16[4,48,1152]{2,1,0:T(8,128)(2,1)S(1)}, bf16[4,48,1152]{2,1,0:T(8,128)(2,1)S(1)}, u32[]{:S(2)}, u32[]{:S(2)}) collective-permute-start(bf16[4,48,1152]{2,1,0:T(8,128)(2,1)S(1)} %get-tuple-element.76), channel_id=1, source_target_pairs={{0,16},{4,12},{8,24},{12,4},{16,0},{20,28},{24,8},{28,20},{1,17},{... | collective-permute-start | bytes 1327112 | tf_op jit(solution)/shard_map/ppermute | solution.py:457
  133.7 5.5 %collective-permute-start.26 = (bf16[48,2176]{1,0:T(8,128)(2,1)S(1)}, bf16[48,2176]{1,0:T(8,128)(2,1)S(1)}, u32[]{:S(2)}, u32[]{:S(2)}) collective-permute-start(bf16[48,2176]{1,0:T(8,128)(2,1)S(1)} %get-tuple-element.83), channel_id=1, source_target_pairs={{0,1},{1,2},{2,3},{3,0},{4,5},{5,6},{6,7},{7,4},{8,9},{9,10},{10,1... | collective-permute-start | bytes 626696 | tf_op jit(solution)/shard_map/ppermute | solution.py:460
  133.8 17.0 %collective-permute-start.27 = (bf16[48,2176]{1,0:T(8,128)(2,1)S(1)}, bf16[48,2176]{1,0:T(8,128)(2,1)S(1)}, u32[]{:S(2)}, u32[]{:S(2)}) collective-permute-start(bf16[48,2176]{1,0:T(8,128)(2,1)S(1)} %get-tuple-element.84), channel_id=1, source_target_pairs={{0,2},{1,3},{2,0},{3,1},{4,6},{5,7},{6,4},{7,5},{8,10},{9,11},{10,... | collective-permute-start | bytes 626696 | tf_op jit(solution)/shard_map/ppermute | solution.py:460
  135.4 19.0 %collective-permute-start.28 = (bf16[48,2176]{1,0:T(8,128)(2,1)S(1)}, bf16[48,2176]{1,0:T(8,128)(2,1)S(1)}, u32[]{:S(2)}, u32[]{:S(2)}) collective-permute-start(bf16[48,2176]{1,0:T(8,128)(2,1)S(1)} %get-tuple-element.85), channel_id=1, source_target_pairs={{0,3},{1,0},{2,1},{3,2},{4,7},{5,4},{6,5},{7,6},{8,11},{9,8},{10,9... | collective-permute-start | bytes 626696 | tf_op jit(solution)/shard_map/ppermute | solution.py:460
  155.1 12.7 %collective-permute-start.30 = (bf16[48,2176]{1,0:T(8,128)(2,1)S(1)}, bf16[48,2176]{1,0:T(8,128)(2,1)S(1)}, u32[]{:S(2)}, u32[]{:S(2)}) collective-permute-start(bf16[48,2176]{1,0:T(8,128)(2,1)S(1)} %sum_pieces.2.refs_4_.refs_0_), channel_id=1, source_target_pairs={{0,16},{4,12},{8,24},{12,4},{16,0},{20,28},{24,8},{28,20},{1,17},{... | collective-permute-start | bytes 626696 | tf_op jit(solution)/shard_map/ppermute | solution.py:457
  156.1 4.5 %collective-permute-start.23 = (bf16[48,1152]{1,0:T(8,128)(2,1)S(1)}, bf16[48,1152]{1,0:T(8,128)(2,1)S(1)}, u32[]{:S(2)}, u32[]{:S(2)}) collective-permute-start(bf16[48,1152]{1,0:T(8,128)(2,1)S(1)} %get-tuple-element.80), channel_id=1, source_target_pairs={{0,1},{1,2},{2,3},{3,0},{4,5},{5,6},{6,7},{7,4},{8,9},{9,10},{10,1... | collective-permute-start | bytes 331784 | tf_op jit(solution)/shard_map/ppermute | solution.py:460
  156.1 9.5 %collective-permute-start.24 = (bf16[48,1152]{1,0:T(8,128)(2,1)S(1)}, bf16[48,1152]{1,0:T(8,128)(2,1)S(1)}, u32[]{:S(2)}, u32[]{:S(2)}) collective-permute-start(bf16[48,1152]{1,0:T(8,128)(2,1)S(1)} %get-tuple-element.81), channel_id=1, source_target_pairs={{0,2},{1,3},{2,0},{3,1},{4,6},{5,7},{6,4},{7,5},{8,10},{9,11},{10,... | collective-permute-start | bytes 331784 | tf_op jit(solution)/shard_map/ppermute | solution.py:460
  156.1 11.1 %collective-permute-start.25 = (bf16[48,1152]{1,0:T(8,128)(2,1)S(1)}, bf16[48,1152]{1,0:T(8,128)(2,1)S(1)}, u32[]{:S(2)}, u32[]{:S(2)}) collective-permute-start(bf16[48,1152]{1,0:T(8,128)(2,1)S(1)} %get-tuple-element.82), channel_id=1, source_target_pairs={{0,3},{1,0},{2,1},{3,2},{4,7},{5,4},{6,5},{7,6},{8,11},{9,8},{10,9... | collective-permute-start | bytes 331784 | tf_op jit(solution)/shard_map/ppermute | solution.py:460
  168.4 11.0 %copy-start.27 = (bf16[192]{0:T(256)(128)(2,1)S(1)}, bf16[192]{0:T(256)(128)(2,1)}, u32[]{:S(2)}) copy-start(bf16[192]{0:T(256)(128)(2,1)} %param.14) | copy-start | bytes 1156
  168.4 8.4 %collective-permute-start.32 = (bf16[2,48,2176]{2,1,0:T(8,128)(2,1)S(1)}, bf16[2,48,2176]{2,1,0:T(8,128)(2,1)S(1)}, u32[]{:S(2)}, u32[]{:S(2)}) collective-permute-start(bf16[2,48,2176]{2,1,0:T(8,128)(2,1)S(1)} %join.8.refs_2_.refs_0_), channel_id=1, source_target_pairs={{0,8},{4,20},{8,0},{12,28},{16,24},{20,4},{24,16},{28,12},{1,9},{5... | collective-permute-start | bytes 1253384 | tf_op jit(solution)/shard_map/ppermute | solution.py:457
  169.2 4.9 %collective-permute-start.29 = (bf16[48,1152]{1,0:T(8,128)(2,1)S(1)}, bf16[48,1152]{1,0:T(8,128)(2,1)S(1)}, u32[]{:S(2)}, u32[]{:S(2)}) collective-permute-start(bf16[48,1152]{1,0:T(8,128)(2,1)S(1)} %sum_pieces.3.refs_2_.refs_0_), channel_id=1, source_target_pairs={{0,16},{4,12},{8,24},{12,4},{16,0},{20,28},{24,8},{28,20},{1,17},{... | collective-permute-start | bytes 331784 | tf_op jit(solution)/shard_map/ppermute | solution.py:457
  177.4 3.2 %collective-permute-start.33 = (bf16[2,2,48,2176]{3,2,1,0:T(8,128)(2,1)S(1)}, bf16[2,2,48,2176]{3,2,1,0:T(8,128)(2,1)S(1)}, u32[]{:S(2)}, u32[]{:S(2)}) collective-permute-start(bf16[2,2,48,2176]{3,2,1,0:T(8,128)(2,1)S(1)} %join.10.refs_1_), channel_id=1, source_target_pairs={{0,4},{4,0},{8,12},{12,8},{16,20},{20,16},{24,28},{28,24},{1,5},{5... | collective-permute-start | bytes 2506760 | tf_op jit(solution)/shard_map/ppermute | solution.py:457
  178.7 5.1 %collective-permute-start.31 = (bf16[2,48,1152]{2,1,0:T(8,128)(2,1)S(1)}, bf16[2,48,1152]{2,1,0:T(8,128)(2,1)S(1)}, u32[]{:S(2)}, u32[]{:S(2)}) collective-permute-start(bf16[2,48,1152]{2,1,0:T(8,128)(2,1)S(1)} %join.9.refs_2_.refs_5_.refs_0_), channel_id=1, source_target_pairs={{0,8},{4,20},{8,0},{12,28},{16,24},{20,4},{24,16},{28,12},{1,9},{5... | collective-permute-start | bytes 663560 | tf_op jit(solution)/shard_map/ppermute | solution.py:457
  185.8 2.4 %collective-permute-start.34 = (bf16[2,2,48,1152]{3,2,1,0:T(8,128)(2,1)S(1)}, bf16[2,2,48,1152]{3,2,1,0:T(8,128)(2,1)S(1)}, u32[]{:S(2)}, u32[]{:S(2)}) collective-permute-start(bf16[2,2,48,1152]{3,2,1,0:T(8,128)(2,1)S(1)} %join.11.refs_1_), channel_id=1, source_target_pairs={{0,4},{4,0},{8,12},{12,8},{16,20},{20,16},{24,28},{28,24},{1,5},{5... | collective-permute-start | bytes 1327112 | tf_op jit(solution)/shard_map/ppermute | solution.py:457
  (18 other events, 24.0 us)
